TPU v7x, 256 devices: a whole 4x4x8 slice. The times are simulated.
256 devices in a mesh: tm: 4 (over z_hi, core), clip: 64 (over y, z_lo, x).
Axes of the slice: x: 4, y: 4, z: 8 (z_hi: 2, z_lo: 4; z = z_hi * 4 + z_lo), core: 2. Of those that a mesh axis runs over, the one named last changes fastest.
Arguments:
- latents: bfloat16 [64, 16, 128, 4, 128], P('clip', 'tm'), may hold values from -16 to 16
- norm_gain: float32 [128], replicated, may hold values from 0.1 to 1.9
- norm_shift: float32 [128], replicated, may hold values from -3 to 3
- kernel: bfloat16 [27, 128, 128], replicated, may hold values from -0.109375 to 0.109375
- cotangent: bfloat16 [64, 16, 128, 4, 128], P('clip', 'tm'), may hold values from -8 to 8
Outputs:
- output: bfloat16 [64, 16, 128, 4, 128], P('clip', 'tm')
- input_adjoint: bfloat16 [64, 16, 128, 4, 128], P('clip', 'tm')
- kernel_grad: float32 [27, 128, 128], replicated
All inputs are finite; a program needn't handle non-finite values.
Results may differ from a plain program's by a relative error of at most 0.0027.
Values may be sent and summed in bfloat16 or wider, within the bound.
No kernel may reach another device: no remote copies, remote signals or barrier semaphores. Data moves between devices by JAX's collectives and lax.ppermute only.
A program may use at most 128 MiB of HBM per device.

v0:
```python
import jax
import jax.numpy as jnp
from jax import lax
from jax.sharding import PartitionSpec as P

GROUPS = 32


def from_behind(shard, axis, by):
    size = lax.axis_size(axis)
    pairs = [(i, i + by) for i in range(size) if 0 <= i + by < size]
    return lax.ppermute(shard, axis, pairs)


def group_totals(values, groups):
    return jnp.sum(values, axis=(0, 2, 3)).reshape(groups, -1).sum(axis=1)


def per_channel(values, per_group):
    return jnp.repeat(values, per_group)[None, :, None, None]


def per_device(latents, norm_gain, norm_shift, kernel, cotangent):
    frames = latents[0].astype(jnp.float32)
    steps_t, chans, height, width = frames.shape
    groups = GROUPS
    per_group = chans // groups
    members = lax.axis_size("tm") * steps_t * per_group * height * width
    first_sum, second_sum = lax.psum(
        (group_totals(frames, groups), group_totals(frames * frames, groups)), "tm"
    )
    center = first_sum / members
    inverse = lax.rsqrt(second_sum / members - center * center + 1e-06)
    unit = (frames - per_channel(center, per_group)) * per_channel(inverse, per_group)
    gain_c = norm_gain[None, :, None, None]
    normed = unit * gain_c + norm_shift[None, :, None, None]
    active = jax.nn.silu(normed).astype(jnp.bfloat16)
    previous = from_behind(active[steps_t - 2 :], "tm", 1)
    padded = jnp.pad(jnp.concatenate([previous, active], 0), ((0, 0), (0, 0), (1, 1), (1, 1)))
    adjoint = cotangent[0]
    following = from_behind(adjoint[:2], "tm", -1)
    adj_padded = jnp.pad(jnp.concatenate([adjoint, following], 0), ((0, 0), (0, 0), (1, 1), (1, 1)))
    conv = jnp.zeros((steps_t, chans, height, width), jnp.float32)
    back = jnp.zeros((steps_t, chans, height, width), jnp.float32)
    grads = []
    for kt in range(3):
        for ki in range(3):
            for kj in range(3):
                tap_index = 9 * kt + 3 * ki + kj
                window = padded[kt : kt + steps_t, :, ki : ki + height, kj : kj + width]
                conv = conv + jnp.einsum(
                    "oc,tchw->tohw", kernel[tap_index], window, preferred_element_type=jnp.float32
                )
                grads.append(
                    jnp.einsum("tohw,tchw->oc", adjoint, window, preferred_element_type=jnp.float32)
                )
                adj_window = adj_padded[
                    2 - kt : 2 - kt + steps_t, :, 2 - ki : 2 - ki + height, 2 - kj : 2 - kj + width
                ]
                back = back + jnp.einsum(
                    "oc,tohw->tchw",
                    kernel[tap_index],
                    adj_window,
                    preferred_element_type=jnp.float32,
                )
    output = (frames + conv).astype(jnp.bfloat16)
    local_grad = jnp.stack(grads, 0)
    kernel_grad = lax.psum(local_grad, ("tm", "clip"))
    logistic = jax.nn.sigmoid(normed)
    scaled = back * logistic * (1.0 + normed * (1.0 - logistic)) * gain_c
    first_total, second_total = lax.psum(
        (group_totals(scaled, groups), group_totals(scaled * unit, groups)), "tm"
    )
    first = first_total / members
    second = second_total / members
    result = adjoint.astype(jnp.float32) + per_channel(inverse, per_group) * (
        scaled - per_channel(first, per_group) - unit * per_channel(second, per_group)
    )
    return (output[None], result.astype(jnp.bfloat16)[None], kernel_grad)


def solution(mesh):
    placed = (P("clip", "tm", None, None, None), P(), P(), P(), P("clip", "tm", None, None, None))
    return jax.shard_map(
        per_device,
        mesh=mesh,
        in_specs=placed,
        out_specs=(P("clip", "tm", None, None, None), P("clip", "tm", None, None, None), P()),
        check_vma=False,
    )
```

profile of v0, /device:TPU:1, one launch (start us, length us, event | category | flops | bytes accessed | tf_op | source)
XLA Modules:
  0.0 390.0 jit_solution(16264413855009773135)
XLA Ops:
  7.2 1.4 copy.69
  8.6 5.3 %collective-permute-start.1 = (bf16[2,128,4,128]{1,3,2,0:T(8,128)(2,1)S(1)}, bf16[2,128,4,128]{1,3,2,0:T(8,128)(2,1)S(1)}, u32[]{:S(2)}, u32[]{:S(2)}) collective-permute-start(bf16[2,128,4,128]{1,3,2,0:T(8,128)(2,1)S(1)} %slice_bitcast_fusion), channel_id=1, source_target_pairs={{64,0},{128,64},{192,128},{65,1},{129,65},{193,129},{66,2},{130,66... | collective-permute-start | bytes 786440 | tf_op jit(solution)/shard_map/ppermute | solution.py:12
  14.8 1.1 copy.238
  16.4 9.1 %all-reduce.3 = (f32[32]{0:T(128)S(1)}, f32[32]{0:T(128)S(1)}) all-reduce(f32[32]{0:T(128)S(1)} %reduce_sum.75, f32[32]{0:T(128)S(1)} %reduce_sum.73), channel_id=1, replica_groups=mesh['tm'=4,'clip'=64] {'tm'}, use_global_device_ids=true, to_apply=%region_5.0 | all-reduce | flops 64 | bytes 512 | tf_op jit(solution)/shard_map/psum | solution.py:29
  34.2 1.9 fusion.345
  36.5 15.3 %all-reduce.2 = (f32[32]{0:T(128)S(1)}, f32[32]{0:T(128)S(1)}) all-reduce(f32[32]{0:T(128)S(1)} %reduce_sum.79, f32[32]{0:T(128)S(1)} %reduce_sum.77), channel_id=1, replica_groups=mesh['tm'=4,'clip'=64] {'tm'}, use_global_device_ids=true, to_apply=%region_11.12 | all-reduce | flops 64 | bytes 512 | tf_op jit(solution)/shard_map/psum | solution.py:71
  52.2 1.4 fusion.119
  53.6 2.5 collective-permute-start
  56.2 2.2 convolution_bitcast_fusion.14
  58.4 1.1 copy.126
  59.6 3.4 pad_slice_fusion.24
  64.1 1.3 fusion.214
  65.4 1.3 fusion.217
  66.7 1.4 fusion.220
  68.1 1.3 fusion.227
  69.4 1.3 fusion.230
  70.7 1.3 fusion.233
  71.9 1.3 fusion.236
  73.3 1.3 fusion.239
  74.5 1.3 fusion.242
  75.8 1.3 fusion.245
  77.1 1.3 fusion.248
  78.4 1.3 fusion.255
  79.7 1.3 fusion.258
  81.0 1.3 fusion.261
  82.6 1.3 convolution_bitcast_fusion.11
  83.9 1.3 convolution_bitcast_fusion.12
  85.2 1.3 convolution_bitcast_fusion.13
  86.5 1.3 convolution_bitcast_fusion.15
  87.8 1.3 convolution_bitcast_fusion.16
  89.1 1.0 fusion.86
  91.1 1.0 fusion.84
  94.1 1.0 fusion.81
  96.1 1.0 fusion.79
  98.0 1.0 fusion.77
  100.0 1.0 fusion.75
  107.8 1.0 fusion.67
  110.8 1.2 fusion.64
  114.9 1.0 fusion.60
  116.0 1.2 fusion.252
  117.2 1.1 fusion.224
  118.3 5.4 %fusion.53 = f32[4,128,4,128]{1,3,2,0:T(8,128)S(1)} fusion(f32[4,4,128,128]{3,2,1,0:T(8,128)S(1)} %copy-done.5, f32[4,4,128,128]{3,2,1,0:T(8,128)S(1)} %copy-done.6, f32[4,4,128,128]{3,2,1,0:T(8,128)S(1)} %copy-done.7, f32[4,4,128,128]{3,2,1,0:T(8,128)S(1)} %fusion.224, f32[4,4,128,128]{3,2,1,0:T(8,128)} %fusion.227, f32[4,4,128,128]{3,2,1,0:T(8,128)} %fusion.230, ...), kind=kOutput, calls=%fused_computation.126 | convolution fusion | flops 71303168 | bytes 18644992 | tf_op jit(solution)/shard_map/oc,tchw->tohw/dot_general | solution.py:51
  123.7 1.2 convolution_bitcast_fusion.17
  124.9 1.1 convolution_bitcast_fusion.18
  126.0 1.7 fusion.59
  127.7 1.1 copy.125
  128.8 251.6 %all-reduce.6.cloned.1.call-done = f32[27,128,128]{1,2,0:T(8,128)} async-done(((f32[27,128,128]{1,2,0:T(8,128)}), f32[27,128,128]{1,2,0:T(8,128)}) %all-reduce.6.cloned.1.call-update) | async-done | bytes 1769488 | tf_op jit(solution)/shard_map/psum | solution.py:68
  380.4 2.7 copy.127
  (110 shorter events, 30.0 us)
Async XLA Ops:
  7.2 6.8 %copy-start.13 = (bf16[1,4,128,4,128]{4,3,2,1,0:T(4,128)(2,1)S(1)}, bf16[1,4,128,4,128]{4,3,2,1,0:T(4,128)(2,1)}, u32[]{:S(2)}) copy-start(bf16[1,4,128,4,128]{4,3,2,1,0:T(4,128)(2,1)} %param.5) | copy-start | bytes 1572868
  7.2 373.2 %all-reduce.6.cloned.1.call-start = ((), (), s32[]{:S(2)}) async-start(), calls=%async_computation | async-start | bytes 3538944 | tf_op jit(solution)/shard_map/psum | solution.py:68
  8.6 6.2 %copy-start.11 = (bf16[1,4,128,4,128]{4,3,2,1,0:T(4,128)(2,1)S(1)}, bf16[1,4,128,4,128]{4,3,2,1,0:T(4,128)(2,1)}, u32[]{:S(2)}) copy-start(bf16[1,4,128,4,128]{4,3,2,1,0:T(4,128)(2,1)} %param.9) | copy-start | bytes 1572868
  8.6 17.3 %copy-start.8 = (bf16[27,128,128]{2,1,0:T(8,128)(2,1)S(1)}, bf16[27,128,128]{2,1,0:T(8,128)(2,1)}, u32[]{:S(2)}) copy-start(bf16[27,128,128]{2,1,0:T(8,128)(2,1)} %param.8) | copy-start | bytes 2654212
  8.6 17.5 %collective-permute-start.1 = (bf16[2,128,4,128]{1,3,2,0:T(8,128)(2,1)S(1)}, bf16[2,128,4,128]{1,3,2,0:T(8,128)(2,1)S(1)}, u32[]{:S(2)}, u32[]{:S(2)}) collective-permute-start(bf16[2,128,4,128]{1,3,2,0:T(8,128)(2,1)S(1)} %slice_bitcast_fusion), channel_id=1, source_target_pairs={{64,0},{128,64},{192,128},{65,1},{129,65},{193,129},{66,2},{130,66... | collective-permute-start | bytes 786440 | tf_op jit(solution)/shard_map/ppermute | solution.py:12
  33.3 0.9 copy-start.15
  33.3 0.9 copy-start.16
  53.6 4.8 %copy-start.10 = (bf16[1,4,128,4,128]{2,4,3,1,0:T(8,128)(2,1)S(1)}, bf16[1,4,128,4,128]{2,4,3,1,0:T(8,128)(2,1)}, u32[]{:S(2)}) copy-start(bf16[1,4,128,4,128]{2,4,3,1,0:T(8,128)(2,1)} %get-tuple-element.41) | copy-start | bytes 1572868
  53.6 5.9 %collective-permute-start = (bf16[2,128,4,128]{1,3,2,0:T(8,128)(2,1)S(1)}, bf16[2,128,4,128]{1,3,2,0:T(8,128)(2,1)S(1)}, u32[]{:S(2)}, u32[]{:S(2)}) collective-permute-start(bf16[2,128,4,128]{1,3,2,0:T(8,128)(2,1)S(1)} %slice.363), channel_id=1, source_target_pairs={{0,64},{64,128},{128,192},{1,65},{65,129},{129,193},{2,66},{66,130... | collective-permute-start | bytes 786440 | tf_op jit(solution)/shard_map/ppermute | solution.py:12
  63.0 1.2 copy-start.9
  86.5 2.6 copy-start.14
  115.9 2.3 copy-start.5
  115.9 2.3 copy-start.6
  115.9 2.3 copy-start.7
  118.2 7.7 %copy-start.3 = (f32[4,128,4,128]{1,3,2,0:T(8,128)S(1)}, f32[4,128,4,128]{1,3,2,0:T(8,128)}, u32[]{:S(2)}) copy-start(f32[4,128,4,128]{1,3,2,0:T(8,128)} %convolution_bitcast_fusion.15) | copy-start | bytes 3145732
  118.3 7.7 %copy-start.4 = (f32[4,128,4,128]{1,3,2,0:T(8,128)S(1)}, f32[4,128,4,128]{1,3,2,0:T(8,128)}, u32[]{:S(2)}) copy-start(f32[4,128,4,128]{1,3,2,0:T(8,128)} %convolution_bitcast_fusion.16) | copy-start | bytes 3145732
  118.3 7.7 %copy-start.12 = (f32[4,128,4,128]{1,3,2,0:T(8,128)S(1)}, f32[4,128,4,128]{1,3,2,0:T(8,128)}, u32[]{:S(2)}) copy-start(f32[4,128,4,128]{1,3,2,0:T(8,128)} %convolution_bitcast_fusion.14) | copy-start | bytes 3145732
  123.7 2.3 copy-start
  123.7 2.3 copy-start.1
  123.7 2.3 copy-start.2
Sparse Core Ops, SparseCore 0:
  116.0 264.3 all-reduce.5
where the time goes:
time: 391 us; the launch traced here: 390 us
  waiting for transfers between devices  252 us (64%)
  matrix products  75.5 us (19%)
  blocking collectives  24.4 us (6%)
  between operations  14.5 us (4%)
  local copies, waits for them, and re-layouts  13.4 us (3%)
  starting transfers between devices  7.85 us (2%)
    psum x1, waiting for transfers between devices, per_device(): kernel_grad = lax.psum(local_grad, ('tm', 'clip'))  252 us
    dot_general x27, matrix products, per_device(): jnp.einsum('oc,tchw->tohw', kernel[tap_index], window, preferred_element_...  38.8 us
    dot_general x27, matrix products, per_device(): jnp.einsum('tohw,tchw->oc', adjoint, window, preferred_element_type=jnp.f...  26.7 us
    psum x1, blocking collectives, per_device(): lax.psum((group_totals(scaled, groups), group_totals(scaled * unit, group...  15.3 us
    dot_general x27, matrix products, per_device(): jnp.einsum('oc,tohw->tchw', kernel[tap_index], adj_window, preferred_elem...  9.97 us
    psum x1, blocking collectives, per_device(): lax.psum((group_totals(frames, groups), group_totals(frames * frames, gro...  9.13 us
  transfers between devices with their start and end apart: 3, of which 1 were waited for; matrix products, arithmetic and copies ran while one was open for 5% of the time, Pallas kernels for 0%

commit v1 on v0

v1 whole, which is shorter than its diff:
```python
import functools

import jax
import jax.numpy as jnp
from jax import lax
from jax.experimental import pallas as pl
from jax.experimental.pallas import tpu as pltpu
from jax.sharding import Mesh
from jax.sharding import PartitionSpec as P

C = 128
H = 4
W = 128
T = 4
HALO = 2
GROUPS = 32
PER = C // GROUPS
SLABS = 4
MEMBERS = SLABS * T * PER * H * W
ROWS = H * C
HALF = 27 * (C // 2)
COMM = HALF + 64
SIDE = 16
PART = COMM // SIDE
F32 = jnp.float32
BF16 = jnp.bfloat16
LIMIT = pltpu.CompilerParams(vmem_limit_bytes=48 * 1024 * 1024)


def lanes():
    return lax.broadcasted_iota(jnp.int32, (C, W), 1)


def rows():
    return lax.broadcasted_iota(jnp.int32, (C, W), 0)


def shifted(block):
    left = jnp.where(lanes() == 0, 0.0, pltpu.roll(block, 1, 1))
    right = jnp.where(lanes() == W - 1, 0.0, pltpu.roll(block, W - 1, 1))
    return left, block, right


def row_of(column, offset):
    lane = lax.broadcasted_iota(jnp.int32, (GROUPS, W), 1)
    sub = lax.broadcasted_iota(jnp.int32, (GROUPS, W), 0)
    return jnp.sum(jnp.where(lane == sub + offset, column, 0.0), axis=0, keepdims=True)


def channel_column(row):
    return jnp.sum(jnp.where(lanes() == rows(), row, 0.0), axis=1, keepdims=True)


def group_column(row, offset, per_channel):
    lane = lax.broadcasted_iota(jnp.int32, (GROUPS * per_channel, W), 1)
    sub = lax.broadcasted_iota(jnp.int32, (GROUPS * per_channel, W), 0)
    return jnp.sum(jnp.where(lane == sub // per_channel + offset, row, 0.0), axis=1, keepdims=True)


def center_inverse(totals, per_channel):
    row = jnp.sum(totals[...].reshape(-1, 8, W), axis=0)[0:1] / MEMBERS
    center = group_column(row, 0, per_channel)
    square = group_column(row, GROUPS, per_channel)
    return center, lax.rsqrt(square - center * center + 1e-06)


def sums_kernel(lat, out):
    total = jnp.zeros((ROWS, W), F32)
    square = jnp.zeros((ROWS, W), F32)
    for t in range(T):
        x = lat[t].astype(F32)
        total = total + x
        square = square + x * x
    total = jnp.sum(jnp.sum(total.reshape(GROUPS, -1, W), axis=1), axis=1, keepdims=True)
    square = jnp.sum(jnp.sum(square.reshape(GROUPS, -1, W), axis=1), axis=1, keepdims=True)
    row = row_of(total, 0) + row_of(square, GROUPS)
    out[...] = jnp.broadcast_to(row, (8, W))


def by_row(frame, tmp):
    tmp[...] = frame.astype(F32)
    return [tmp[pl.ds(h, C, stride=H), :] for h in range(H)]


def back_kernel(cot, following, kernel, back, tmp, window, taps):
    for f in range(T + HALO):
        blocks = by_row(cot[f] if f < T else following[f - T], tmp)
        for h in range(H):
            for s, moved in enumerate(shifted(blocks[h])):
                at = (s * H + h) * C
                window[at : at + C, f * W : (f + 1) * W] = moved.astype(BF16)
    taps[...] = jnp.zeros_like(taps)
    for kt in range(3):
        for ki in range(3):
            for kj in range(3):
                tap = kernel[9 * kt + 3 * ki + kj].astype(F32).T.astype(BF16)
                for h in range(H):
                    other = h + 1 - ki
                    if 0 <= other < H:
                        at = ((2 - kj) * H + other) * C
                        taps[2 - kt, h * C : (h + 1) * C, at : at + C] = tap
    total = jnp.dot(taps[0], window[:, 0 : T * W], preferred_element_type=F32)
    for f in range(1, 3):
        total = total + jnp.dot(taps[f], window[:, f * W : (f + T) * W], preferred_element_type=F32)
    back[...] = total


def grad_kernel(flags, lat, previous, cot, totals, gain, shift, back, window, scaled, keep, send, tmp, flat, adj):
    has_previous, core = flags[0], flags[1]
    center, inverse = center_inverse(totals, PER)
    gain_c = channel_column(gain[...])
    shift_c = channel_column(shift[...])
    first = jnp.zeros((C, W), F32)
    second = jnp.zeros((C, W), F32)
    for f in range(T + HALO):
        t = f - HALO
        blocks = by_row(previous[f] if t < 0 else lat[t], tmp)
        for h in range(H):
            unit = (blocks[h] - center) * inverse
            normed = unit * gain_c + shift_c
            sig = 1.0 / (1.0 + jnp.exp(-normed))
            active = normed * sig
            if t < 0:
                active = jnp.where(has_previous > 0, active, 0.0)
            else:
                adjoint = back[h * C : (h + 1) * C, t * W : (t + 1) * W]
                value = adjoint * sig * (1.0 + normed * (1.0 - sig)) * gain_c
                first = first + value
                second = second + value * unit
                scaled[t, pl.ds(h, C, stride=H), :] = value
            for s, moved in enumerate(shifted(active.astype(BF16).astype(F32))):
                moved = moved.astype(BF16)
                window[(s * H + h) * C : (s * H + h + 1) * C, f * W : (f + 1) * W] = moved
                flat[s * C : (s + 1) * C, (f * H + h) * W : (f * H + h + 1) * W] = moved
    zero = jnp.zeros((C, W), BF16)
    for t in range(T):
        blocks = by_row(cot[t], tmp)
        for h in range(H):
            for ki in range(3):
                source = h - ki + 1
                block = blocks[source].astype(BF16) if 0 <= source < H else zero
                adj[ki * C : (ki + 1) * C, (t * H + h) * W : (t * H + h + 1) * W] = block
    half = C // 2
    for kt in range(3):
        grads = lax.dot_general(
            adj[...],
            flat[:, kt * H * W : (kt + T) * H * W],
            (((1,), (1,)), ((), ())),
            preferred_element_type=F32,
        )
        for ki in range(3):
            for kj in range(3):
                tap = grads[ki * C : (ki + 1) * C, kj * C : (kj + 1) * C]
                low, high = tap[:half], tap[half:]
                at = (9 * kt + 3 * ki + kj) * half
                keep[at : at + half] = jnp.where(core == 0, low, high)
                send[at : at + half] = jnp.where(core == 0, high, low)
    lane, sub = lanes(), rows()
    first = jnp.sum(jnp.where(lane == sub // PER, jnp.sum(first, axis=1, keepdims=True), 0.0), axis=0, keepdims=True)
    second = jnp.sum(
        jnp.where(lane == sub // PER + GROUPS, jnp.sum(second, axis=1, keepdims=True), 0.0), axis=0, keepdims=True
    )
    tail = jnp.broadcast_to(first + second, (COMM - HALF, W))
    keep[HALF:] = tail
    send[HALF:] = tail


def conv_kernel(lat, kernel, window, output, tmp, taps):
    taps[...] = jnp.zeros_like(taps)
    for kt in range(3):
        for ki in range(3):
            for kj in range(3):
                tap = kernel[9 * kt + 3 * ki + kj]
                for h in range(H):
                    other = h - 1 + ki
                    if 0 <= other < H:
                        at = (kj * H + other) * C
                        taps[kt, h * C : (h + 1) * C, at : at + C] = tap
    total = jnp.dot(taps[0], window[:, 0 : T * W], preferred_element_type=F32)
    for f in range(1, 3):
        total = total + jnp.dot(taps[f], window[:, f * W : (f + T) * W], preferred_element_type=F32)
    for t in range(T):
        for h in range(H):
            tmp[pl.ds(h, C, stride=H), :] = total[h * C : (h + 1) * C, t * W : (t + 1) * W]
        output[t] = (lat[t].astype(F32) + tmp[...]).astype(BF16)


def adjoint_kernel(lat, cot, totals, backward, scaled, result):
    center, inverse = center_inverse(totals, PER * H)
    row = backward[...][0:1] / MEMBERS
    first = group_column(row, 0, PER * H)
    second = group_column(row, GROUPS, PER * H)
    for t in range(T):
        unit = (lat[t].astype(F32) - center) * inverse
        value = cot[t].astype(F32) + inverse * (scaled[t] - first - unit * second)
        result[t] = value.astype(BF16)


def call(body, out, scratch, *operands, scalars=0):
    inside = pl.BlockSpec(memory_space=pltpu.VMEM)
    return pl.pallas_call(
        body,
        out_shape=out,
        in_specs=[pl.BlockSpec(memory_space=pltpu.SMEM)] * scalars + [inside] * (len(operands) - scalars),
        out_specs=jax.tree.map(lambda _: inside, out),
        scratch_shapes=scratch,
        compiler_params=LIMIT,
    )(*operands)


def shape(*dims, dtype=F32):
    return jax.ShapeDtypeStruct(dims, dtype)


def swap(value, axis):
    return lax.ppermute(value, axis, [(0, 1), (1, 0)])


def per_device(latents, norm_gain, norm_shift, kernel, cotangent):
    lat = latents.reshape(T, ROWS, W)
    cot = cotangent.reshape(T, ROWS, W)
    slab = ("zh", "core")
    previous = lax.ppermute(lat[T - HALO :], slab, [(i, i + 1) for i in range(SLABS - 1)])
    following = lax.ppermute(cot[:HALO], slab, [(i + 1, i) for i in range(SLABS - 1)])
    own = call(sums_kernel, shape(8, W), [], lat)
    pair = own + swap(own, "core")
    totals = jnp.concatenate([pair, swap(pair, "zh")], axis=0)
    tmp = pltpu.VMEM((ROWS, W), F32)
    window_scratch = pltpu.VMEM((3 * ROWS, (T + HALO) * W), BF16)
    taps = pltpu.VMEM((3, ROWS, 3 * ROWS), BF16)
    back = call(back_kernel, shape(ROWS, T * W), [tmp, window_scratch, taps], cot, following, kernel)
    zh, core = lax.axis_index("zh"), lax.axis_index("core")
    flags = jnp.stack([zh * 2 + core, core]).astype(jnp.int32)
    window, scaled, keep, send = call(
        grad_kernel,
        (
            shape(3 * ROWS, (T + HALO) * W, dtype=BF16),
            shape(T, ROWS, W),
            shape(COMM, C),
            shape(COMM, C),
        ),
        [
            tmp,
            pltpu.VMEM((3 * C, (T + HALO) * H * W), BF16),
            pltpu.VMEM((3 * C, T * H * W), BF16),
        ],
        flags,
        lat,
        previous,
        cot,
        totals,
        norm_gain.reshape(1, C),
        norm_shift.reshape(1, C),
        back,
        scalars=1,
    )
    chip = keep + swap(send, "core")
    output = call(conv_kernel, shape(T, ROWS, W, dtype=BF16), [tmp, taps], lat, kernel, window)
    parts = lax.all_to_all(chip.astype(WIRE).reshape(SIDE, PART, C), ("y", "x"), 0, 0)
    part = jnp.sum(parts.astype(F32), axis=0)
    packed = jnp.concatenate([part, chip[HALF : HALF + 8]], axis=0)
    size = 8
    over_z = lax.all_to_all(jnp.broadcast_to(packed, (size,) + packed.shape), ("zh", "zl"), 0, 0)
    part = jnp.sum(over_z[:, :PART], axis=0).astype(BF16)
    zl = lax.axis_index("zl")
    backward = lax.dynamic_slice_in_dim(over_z[:4, PART:], zl, 1, 0)[0] + lax.dynamic_slice_in_dim(over_z[4:, PART:], zl, 1, 0)[0]
    result = call(adjoint_kernel, shape(T, ROWS, W, dtype=BF16), [], lat, cot, totals, backward, scaled)
    mine = lax.all_to_all(jnp.broadcast_to(part, (SIDE,) + part.shape), ("y", "x"), 0, 0).reshape(COMM, C)[:HALF]
    other = swap(mine, "core")
    mine, other = mine.reshape(27, C // 2, C), other.reshape(27, C // 2, C)
    low = jnp.where(core == 0, mine, other)
    high = jnp.where(core == 0, other, mine)
    kernel_grad = jnp.concatenate([low, high], axis=1).astype(F32)
    return output.reshape(latents.shape), result.reshape(latents.shape), kernel_grad


WIRE = F32


def solution(mesh):
    fine = Mesh(mesh.devices.reshape(2, 2, 4, 4, 4), ("zh", "core", "y", "zl", "x"))
    frames = P(("y", "zl", "x"), ("zh", "core"), None, None, None)
    return jax.shard_map(
        per_device,
        mesh=fine,
        in_specs=(frames, P(), P(), P(), frames),
        out_specs=(frames, frames, P()),
        check_vma=False,
    )
```

time: 391 us -> 107 us (0.27)
  waiting for transfers between devices: 252 us -> 23.5 us
  matrix products: 75.5 us -> 0 us
  starting transfers between devices: 7.85 us -> 24.8 us
  between operations: 14.5 us -> 0.83 us
  Pallas kernels: 0 us -> 13.5 us
  blocking collectives: 24.4 us -> 31 us
  local copies, waits for them, and re-layouts: 13.4 us -> 9.21 us
    psum x1 -> x0, waiting for transfers between devices: 252 us -> none  [per_device(): kernel_grad = lax.psum(local_grad, ('tm', 'clip'))]
    dot_general x81 -> x0, matrix products: 75.5 us -> none  [the longest x27 38.8 us: per_device(): jnp.einsum('oc,tchw->tohw', kernel[tap_index], window, preferred_element_...]
    all_to_all x0 -> x2, blocking collectives: none -> 31 us  [the longest x1 17.2 us: per_device(): lax.all_to_all(jnp.broadcast_to(packed, (size,) + packed.shape), ('zh', '...]
    psum x2 -> x0, blocking collectives: 24.4 us -> none  [the longest x1 15.3 us: per_device(): lax.psum((group_totals(scaled, groups), group_totals(scaled * unit, group...]
    all_to_all x0 -> x1, waiting for transfers between devices: none -> 14.2 us  [per_device(): lax.all_to_all(chip.astype(WIRE).reshape(SIDE, PART, C), ('y', 'x'), 0, 0)]
    pallas_call x0 -> x5, Pallas kernels: none -> 13.5 us  [call(): pl.pallas_call(body, out_shape=out, in_specs=[pl.BlockSpec(memory_space=p...]
    ppermute x2 -> x6, starting transfers between devices: 7.81 us -> 18.1 us  [the longest x1 6.98 us: per_device(): lax.ppermute(lat[T - HALO:], slab, [(i, i + 1) for i in range(SLABS - 1)])]
    ppermute x2 -> x6, waiting for transfers between devices: 0.01 us -> 9.26 us  [the longest x4 9.25 us: swap(): return lax.ppermute(value, axis, [(0, 1), (1, 0)])]
  transfers between devices with their start and end apart: 3 -> 7, of which waited for: 1 -> 4; matrix products, arithmetic and copies ran while one was open for 5% -> 2% of each run, Pallas kernels for 0% -> 8%
where the time goes in v1:
time: 107 us
  blocking collectives  31 us (29%)
  starting transfers between devices  24.8 us (23%)
  waiting for transfers between devices  23.5 us (22%)
  Pallas kernels  13.5 us (13%)
  local copies, waits for them, and re-layouts  9.21 us (9%)
  other arithmetic  3.67 us (3%)
    all_to_all x1, blocking collectives, per_device(): lax.all_to_all(jnp.broadcast_to(packed, (size,) + packed.shape), ('zh', '...  17.2 us
    all_to_all x1, waiting for transfers between devices, per_device(): lax.all_to_all(chip.astype(WIRE).reshape(SIDE, PART, C), ('y', 'x'), 0, 0)  14.2 us
    all_to_all x1, blocking collectives, per_device(): lax.all_to_all(jnp.broadcast_to(part, (SIDE,) + part.shape), ('y', 'x'),...  13.8 us
    pallas_call x5, Pallas kernels, call(): pl.pallas_call(body, out_shape=out, in_specs=[pl.BlockSpec(memory_space=p...  13.5 us
    ppermute x4, waiting for transfers between devices, swap(): return lax.ppermute(value, axis, [(0, 1), (1, 0)])  9.25 us
    ppermute x1, starting transfers between devices, per_device(): lax.ppermute(lat[T - HALO:], slab, [(i, i + 1) for i in range(SLABS - 1)])  6.98 us
    all_to_all x1, starting transfers between devices, per_device(): lax.all_to_all(chip.astype(WIRE).reshape(SIDE, PART, C), ('y', 'x'), 0, 0)  6.76 us
    ppermute x4, starting transfers between devices, swap(): return lax.ppermute(value, axis, [(0, 1), (1, 0)])  5.96 us
  transfers between devices with their start and end apart: 7, of which 4 were waited for; matrix products, arithmetic and copies ran while one was open for 2% of the time, Pallas kernels for 8%

profile of v1, /device:TPU:1, one launch (start us, length us, event | category | flops | bytes accessed | tf_op | source)
XLA Modules:
  0.0 106.6 jit_solution(415380037696879562)
XLA Ops:
  0.6 0.0 copy-start.2
  0.6 1.1 %slice.29 = bf16[1,2,128,4,128]{4,3,2,1,0:T(4,128)(2,1)S(1)} slice(bf16[1,4,128,4,128]{4,3,2,1,0:T(4,128)(2,1)} %param.9), slice={[0:1], [0:2], [0:128], [0:4], [0:128]} | slice | bytes 524288 | tf_op jit(solution)/shard_map/slice | solution.py:224
  1.7 5.1 %collective-permute-start.3 = (bf16[2,512,128]{2,1,0:T(8,128)(2,1)S(1)}, bf16[2,512,128]{2,1,0:T(8,128)(2,1)S(1)}, u32[]{:S(2)}, u32[]{:S(2)}) collective-permute-start(bf16[2,512,128]{2,1,0:T(8,128)(2,1)S(1)} %bitcast.32), channel_id=1, source_target_pairs={{64,0},{128,64},{192,128},{65,1},{129,65},{193,129},{66,2},{130,66... | collective-permute-start | bytes 786440 | tf_op jit(solution)/shard_map/ppermute | solution.py:224
  6.9 0.0 copy-start.1
  6.9 1.1 %slice.27 = bf16[1,2,128,4,128]{4,3,2,1,0:T(4,128)(2,1)S(1)} slice(bf16[1,4,128,4,128]{4,3,2,1,0:T(4,128)(2,1)} %param.5), slice={[0:1], [2:4], [0:128], [0:4], [0:128]} | slice | bytes 524288 | tf_op jit(solution)/shard_map/slice | solution.py:223
  8.0 0.0 copy-start.6
  8.0 0.0 copy-start.7
  8.1 7.0 %collective-permute-start = (bf16[2,512,128]{2,1,0:T(8,128)(2,1)S(1)}, bf16[2,512,128]{2,1,0:T(8,128)(2,1)S(1)}, u32[]{:S(2)}, u32[]{:S(2)}) collective-permute-start(bf16[2,512,128]{2,1,0:T(8,128)(2,1)S(1)} %bitcast.31), channel_id=1, source_target_pairs={{0,64},{64,128},{128,192},{1,65},{65,129},{129,193},{2,66},{66,130... | collective-permute-start | bytes 786440 | tf_op jit(solution)/shard_map/ppermute | solution.py:223
  15.0 0.0 copy-start
  15.1 1.0 copy-done
  16.1 0.3 shard_map.76
  16.4 0.1 collective-permute-start.1
  16.5 1.1 %collective-permute-done.1 = f32[8,128]{1,0:T(8,128)S(1)} collective-permute-done((f32[8,128]{1,0:T(8,128)S(1)}, f32[8,128]{1,0:T(8,128)S(1)}, u32[]{:S(2)}, u32[]{:S(2)}) %collective-permute-start.1) | collective-permute-done | bytes 4128 | tf_op jit(solution)/shard_map/ppermute | solution.py:216
  17.6 0.3 collective-permute-start.2
  17.9 0.1 pad_add_fusion.flags
  18.0 6.0 %collective-permute-done.2 = f32[8,128]{1,0:T(8,128)S(1)} collective-permute-done((f32[8,128]{1,0:T(8,128)S(1)}, f32[8,128]{1,0:T(8,128)S(1)}, u32[]{:S(2)}, u32[]{:S(2)}) %collective-permute-start.2) | collective-permute-done | bytes 4128 | tf_op jit(solution)/shard_map/ppermute | solution.py:216
  24.0 0.0 collective-permute-done.3.following
  24.0 0.0 copy-done.2
  24.0 0.0 copy-start.3
  24.0 1.2 %copy-done.3 = bf16[27,128,128]{2,1,0:T(8,128)(2,1)S(1)} copy-done((bf16[27,128,128]{2,1,0:T(8,128)(2,1)S(1)}, bf16[27,128,128]{2,1,0:T(8,128)(2,1)}, u32[]{:S(2)}) %copy-start.3) | copy-done | bytes 884760
  25.2 3.3 %shard_map.77.back = f32[512,512]{1,0:T(8,128)S(1)} custom-call(bf16[4,512,128]{2,1,0:T(8,128)(2,1)S(1)} %bitcast.20, bf16[2,512,128]{2,1,0:T(8,128)(2,1)S(1)} %collective-permute-done.3.following, bf16[27,128,128]{2,1,0:T(8,128)(2,1)S(1)} %copy-done.3), custom_call_target="tpu_custom_call" | custom-call | tf_op jit(solution)/shard_map/pallas_call | solution.py:201
  28.5 0.0 collective-permute-done.previous
  28.5 0.0 copy-done.1
  28.5 0.0 copy-done.6
  28.5 0.0 copy-done.7
  28.5 4.7 %shard_map.78 = (bf16[1536,768]{1,0:T(8,128)(2,1)}, f32[4,512,128]{2,1,0:T(8,128)S(1)}, f32[1792,128]{1,0:T(8,128)S(1)}, f32[1792,128]{1,0:T(8,128)S(1)}) custom-call(s32[2]{0:T(128)S(1)} %pad_add_fusion.flags, bf16[4,512,128]{2,1,0:T(8,128)(2,1)S(1)} %bitcast.17, bf16[2,512,128]{2,1,0:T(8,128)(2,1)S(1)} %collective-permute-done.previous, ...), custom_call_target="tpu_custom_call" | custom-call | tf_op jit(solution)/shard_map/pallas_call | solution.py:201
  33.3 1.4 %collective-permute-start.4 = (f32[1792,128]{1,0:T(8,128)S(1)}, f32[1792,128]{1,0:T(8,128)S(1)}, u32[]{:S(2)}, u32[]{:S(2)}) collective-permute-start(f32[1792,128]{1,0:T(8,128)S(1)} %get-tuple-element.9), channel_id=1, source_target_pairs={{0,64},{64,0},{1,65},{65,1},{2,66},{66,2},{3,67},{67,3},{4,68},{68... | collective-permute-start | bytes 2752520 | tf_op jit(solution)/shard_map/ppermute | solution.py:216
  34.7 2.1 %collective-permute-done.4 = f32[1792,128]{1,0:T(8,128)S(1)} collective-permute-done((f32[1792,128]{1,0:T(8,128)S(1)}, f32[1792,128]{1,0:T(8,128)S(1)}, u32[]{:S(2)}, u32[]{:S(2)}) %collective-permute-start.4) | collective-permute-done | bytes 917536 | tf_op jit(solution)/shard_map/ppermute | solution.py:216
  36.8 1.0 add.20
  37.8 6.8 %all-to-all-start = ((f32[16,112,128]{2,1,0:T(8,128)}), f32[16,112,128]{2,1,0:T(8,128)S(1)}, u32[]{:S(2)}, u32[]{:S(2)}) async-start(f32[16,112,128]{2,1,0:T(8,128)} %bitcast.9), calls=%async_computation | async-start | bytes 1835008 | tf_op jit(solution)/shard_map/all_to_all | solution.py:259
  44.6 0.7 slice.36
  45.3 14.2 %all-to-all-done = f32[16,112,128]{2,1,0:T(8,128)S(1)} async-done(((f32[16,112,128]{2,1,0:T(8,128)}), f32[16,112,128]{2,1,0:T(8,128)S(1)}, u32[]{:S(2)}, u32[]{:S(2)}) %all-to-all-start) | async-done | bytes 917536 | tf_op jit(solution)/shard_map/all_to_all | solution.py:259
  59.5 0.1 reduce_sum.18
  59.6 0.0 copy-start.4
  59.6 17.2 %all_to_all.15 = f32[8,120,128]{2,1,0:T(8,128)S(1)} all-to-all(f32[8,120,128]{2,1,0:T(8,128)S(1)} %broadcast_in_dim.6), channel_id=1, replica_groups=mesh['zh'=2,'core'=2,'y'=4,'zl'=4,'x'=4] {'zh','zl'}, dimensions={0} | all-to-all | bytes 983040 | tf_op jit(solution)/shard_map/all_to_all | solution.py:263
  76.8 0.8 copy-done.8
  77.6 0.1 broadcast_in_dim.7
  77.7 13.8 %all_to_all.16 = bf16[16,112,128]{2,1,0:T(8,128)(2,1)S(1)} all-to-all(bf16[16,112,128]{2,1,0:T(8,128)(2,1)S(1)} %broadcast_in_dim.7), channel_id=1, replica_groups=mesh['zh'=2,'core'=2,'y'=4,'zl'=4,'x'=4] {'y','x'}, dimensions={0} | all-to-all | bytes 917504 | tf_op jit(solution)/shard_map/all_to_all | solution.py:268
  91.5 0.8 slice.40
  92.3 4.2 %collective-permute-start.5 = (bf16[1728,128]{1,0:T(8,128)(2,1)}, bf16[1728,128]{1,0:T(8,128)(2,1)}, u32[]{:S(2)}, u32[]{:S(2)}) collective-permute-start(bf16[1728,128]{1,0:T(8,128)(2,1)} %slice.40), channel_id=1, source_target_pairs={{0,64},{64,0},{1,65},{65,1},{2,66},{66,2},{3,67},{67,3},{4,68},{68... | collective-permute-start | bytes 1327112 | tf_op jit(solution)/shard_map/ppermute | solution.py:216
  96.5 0.0 copy-done.4
  96.5 1.7 %copy-done.5 = bf16[1536,768]{1,0:T(8,128)(2,1)S(1)} copy-done((bf16[1536,768]{1,0:T(8,128)(2,1)S(1)}, bf16[1536,768]{1,0:T(8,128)(2,1)}, u32[]{:S(2)}) %copy-start.5) | copy-done | bytes 2359320
  98.2 3.7 %shard_map.79 = bf16[4,512,128]{2,1,0:T(8,128)(2,1)} custom-call(bf16[4,512,128]{2,1,0:T(8,128)(2,1)S(1)} %bitcast.18, bf16[27,128,128]{2,1,0:T(8,128)(2,1)S(1)} %copy-done.4, bf16[1536,768]{1,0:T(8,128)(2,1)S(1)} %copy-done.5), custom_call_target="tpu_custom_call" | custom-call | tf_op jit(solution)/shard_map/pallas_call | solution.py:201
  101.9 0.7 fusion
  102.6 1.4 %shard_map.80 = bf16[4,512,128]{2,1,0:T(8,128)(2,1)} custom-call(bf16[4,512,128]{2,1,0:T(8,128)(2,1)S(1)} %bitcast.19, bf16[4,512,128]{2,1,0:T(8,128)(2,1)S(1)} %bitcast.22, f32[16,128]{1,0:T(8,128)S(1)} %pad_maximum_fusion.1.totals, f32[8,128]{1,0:T(8,128)S(1)} %add_bitcast_fusion.backward, f32[4,512,128]{2,1,0:T(8,128)S(1)} %get-tuple-element.10.scaled), custom_call_target="tpu_custom_call" | custom-call | tf_op jit(solution)/shard_map/pallas_call | solution.py:201
  104.1 0.0 collective-permute-done.5
  104.1 1.1 %broadcast_select_fusion.1 = (bf16[1728,128]{1,0:T(8,128)(2,1)S(1)}, bf16[1728,128]{1,0:T(8,128)(2,1)S(1)}) fusion(bf16[1728,128]{1,0:T(8,128)(2,1)} %collective-permute-done.5, pred[]{:T(512)S(6)} %eq.4, bf16[1792,128]{1,0:T(8,128)(2,1)S(1)} %bitcast.26), kind=kLoop, calls=%fused_computation.3 | loop fusion | flops 442368 | bytes 1769473 | tf_op jit(solution)/shard_map/jit(_where)/select_n | solution.py:271
  105.1 1.4 %maximum_convert_fusion = f32[27,128,128]{2,1,0:T(8,128)} fusion(bf16[27,64,128]{2,1,0:T(8,128)(2,1)S(1)} %bitcast.28, bf16[27,64,128]{2,1,0:T(8,128)(2,1)S(1)} %bitcast.27), kind=kLoop, calls=%fused_computation | loop fusion | flops 1769472 | bytes 2654208 | tf_op jit(solution)/shard_map/convert_element_type | solution.py:273
  (8 shorter events, 0.1 us)
Async XLA Ops:
  0.6 23.3 %copy-start.2 = (bf16[1,4,128,4,128]{4,3,2,1,0:T(4,128)(2,1)S(1)}, bf16[1,4,128,4,128]{4,3,2,1,0:T(4,128)(2,1)}, u32[]{:S(2)}) copy-start(bf16[1,4,128,4,128]{4,3,2,1,0:T(4,128)(2,1)} %param.9) | copy-start | bytes 1572868
  1.7 22.2 %collective-permute-start.3 = (bf16[2,512,128]{2,1,0:T(8,128)(2,1)S(1)}, bf16[2,512,128]{2,1,0:T(8,128)(2,1)S(1)}, u32[]{:S(2)}, u32[]{:S(2)}) collective-permute-start(bf16[2,512,128]{2,1,0:T(8,128)(2,1)S(1)} %bitcast.32), channel_id=1, source_target_pairs={{64,0},{128,64},{192,128},{65,1},{129,65},{193,129},{66,2},{130,66... | collective-permute-start | bytes 786440 | tf_op jit(solution)/shard_map/ppermute | solution.py:224
  6.9 21.6 %copy-start.1 = (bf16[1,4,128,4,128]{4,3,2,1,0:T(4,128)(2,1)S(1)}, bf16[1,4,128,4,128]{4,3,2,1,0:T(4,128)(2,1)}, u32[]{:S(2)}) copy-start(bf16[1,4,128,4,128]{4,3,2,1,0:T(4,128)(2,1)} %param.5) | copy-start | bytes 1572868
  8.0 20.5 %copy-start.6 = (f32[128]{0:T(128)S(1)}, f32[128]{0:T(128)}, u32[]{:S(2)}) copy-start(f32[128]{0:T(128)} %param.6) | copy-start | bytes 1540
  8.0 20.5 %copy-start.7 = (f32[128]{0:T(128)S(1)}, f32[128]{0:T(128)}, u32[]{:S(2)}) copy-start(f32[128]{0:T(128)} %param.7) | copy-start | bytes 1540
  8.1 20.4 %collective-permute-start = (bf16[2,512,128]{2,1,0:T(8,128)(2,1)S(1)}, bf16[2,512,128]{2,1,0:T(8,128)(2,1)S(1)}, u32[]{:S(2)}, u32[]{:S(2)}) collective-permute-start(bf16[2,512,128]{2,1,0:T(8,128)(2,1)S(1)} %bitcast.31), channel_id=1, source_target_pairs={{0,64},{64,128},{128,192},{1,65},{65,129},{129,193},{2,66},{66,130... | collective-permute-start | bytes 786440 | tf_op jit(solution)/shard_map/ppermute | solution.py:223
  15.0 1.0 copy-start
  16.4 1.2 %collective-permute-start.1 = (f32[8,128]{1,0:T(8,128)S(1)}, f32[8,128]{1,0:T(8,128)S(1)}, u32[]{:S(2)}, u32[]{:S(2)}) collective-permute-start(f32[8,128]{1,0:T(8,128)S(1)} %shard_map.76), channel_id=1, source_target_pairs={{0,64},{64,0},{1,65},{65,1},{2,66},{66,2},{3,67},{67,3},{4,68},{68... | collective-permute-start | bytes 12296 | tf_op jit(solution)/shard_map/ppermute | solution.py:216
  17.6 6.4 %collective-permute-start.2 = (f32[8,128]{1,0:T(8,128)S(1)}, f32[8,128]{1,0:T(8,128)S(1)}, u32[]{:S(2)}, u32[]{:S(2)}) collective-permute-start(f32[8,128]{1,0:T(8,128)S(1)} %add.19), channel_id=1, source_target_pairs={{0,128},{128,0},{1,129},{129,1},{2,130},{130,2},{3,131},{131,3},{4... | collective-permute-start | bytes 12296 | tf_op jit(solution)/shard_map/ppermute | solution.py:216
  24.0 1.2 %copy-start.3 = (bf16[27,128,128]{2,1,0:T(8,128)(2,1)S(1)}, bf16[27,128,128]{2,1,0:T(8,128)(2,1)}, u32[]{:S(2)}) copy-start(bf16[27,128,128]{2,1,0:T(8,128)(2,1)} %kernel.3) | copy-start | bytes 2654212
  33.3 3.5 %collective-permute-start.4 = (f32[1792,128]{1,0:T(8,128)S(1)}, f32[1792,128]{1,0:T(8,128)S(1)}, u32[]{:S(2)}, u32[]{:S(2)}) collective-permute-start(f32[1792,128]{1,0:T(8,128)S(1)} %get-tuple-element.9), channel_id=1, source_target_pairs={{0,64},{64,0},{1,65},{65,1},{2,66},{66,2},{3,67},{67,3},{4,68},{68... | collective-permute-start | bytes 2752520 | tf_op jit(solution)/shard_map/ppermute | solution.py:216
  37.8 21.7 %all-to-all-start = ((f32[16,112,128]{2,1,0:T(8,128)}), f32[16,112,128]{2,1,0:T(8,128)S(1)}, u32[]{:S(2)}, u32[]{:S(2)}) async-start(f32[16,112,128]{2,1,0:T(8,128)} %bitcast.9), calls=%async_computation | async-start | bytes 1835008 | tf_op jit(solution)/shard_map/all_to_all | solution.py:259
  59.6 36.9 %copy-start.4 = (bf16[27,128,128]{2,1,0:T(8,128)(2,1)S(1)}, bf16[27,128,128]{2,1,0:T(8,128)(2,1)}, u32[]{:S(2)}) copy-start(bf16[27,128,128]{2,1,0:T(8,128)(2,1)} %kernel.3) | copy-start | bytes 2654212
  76.8 0.8 copy-start.8
  92.3 11.7 %collective-permute-start.5 = (bf16[1728,128]{1,0:T(8,128)(2,1)}, bf16[1728,128]{1,0:T(8,128)(2,1)}, u32[]{:S(2)}, u32[]{:S(2)}) collective-permute-start(bf16[1728,128]{1,0:T(8,128)(2,1)} %slice.40), channel_id=1, source_target_pairs={{0,64},{64,0},{1,65},{65,1},{2,66},{66,2},{3,67},{67,3},{4,68},{68... | collective-permute-start | bytes 1327112 | tf_op jit(solution)/shard_map/ppermute | solution.py:216
  96.5 1.7 %copy-start.5 = (bf16[1536,768]{1,0:T(8,128)(2,1)S(1)}, bf16[1536,768]{1,0:T(8,128)(2,1)}, u32[]{:S(2)}) copy-start(bf16[1536,768]{1,0:T(8,128)(2,1)} %get-tuple-element.7.window) | copy-start | bytes 7077892

commit v2 on v1

v2 whole, which is shorter than its diff:
```python
import functools

import jax
import jax.numpy as jnp
from jax import lax
from jax.experimental import pallas as pl
from jax.experimental.pallas import tpu as pltpu
from jax.sharding import Mesh
from jax.sharding import PartitionSpec as P

C = 128
H = 4
W = 128
T = 4
HALO = 2
GROUPS = 32
PER = C // GROUPS
SLABS = 4
MEMBERS = SLABS * T * PER * H * W
ROWS = H * C
HALF = 27 * (C // 2)
COMM = HALF + 64
SIDE = 32
PART = COMM // SIDE
F32 = jnp.float32
BF16 = jnp.bfloat16
LIMIT = pltpu.CompilerParams(vmem_limit_bytes=24 * 1024 * 1024)


def lanes():
    return lax.broadcasted_iota(jnp.int32, (C, W), 1)


def rows():
    return lax.broadcasted_iota(jnp.int32, (C, W), 0)


def shifted(block):
    left = jnp.where(lanes() == 0, 0.0, pltpu.roll(block, 1, 1))
    right = jnp.where(lanes() == W - 1, 0.0, pltpu.roll(block, W - 1, 1))
    return left, block, right


def row_of(column, offset):
    lane = lax.broadcasted_iota(jnp.int32, (GROUPS, W), 1)
    sub = lax.broadcasted_iota(jnp.int32, (GROUPS, W), 0)
    return jnp.sum(jnp.where(lane == sub + offset, column, 0.0), axis=0, keepdims=True)


def channel_column(row):
    return jnp.sum(jnp.where(lanes() == rows(), row, 0.0), axis=1, keepdims=True)


def group_column(row, offset, per_channel):
    lane = lax.broadcasted_iota(jnp.int32, (GROUPS * per_channel, W), 1)
    sub = lax.broadcasted_iota(jnp.int32, (GROUPS * per_channel, W), 0)
    return jnp.sum(jnp.where(lane == sub // per_channel + offset, row, 0.0), axis=1, keepdims=True)


def center_inverse(totals, per_channel):
    row = jnp.sum(totals[...].reshape(-1, 8, W), axis=0)[0:1] / MEMBERS
    center = group_column(row, 0, per_channel)
    square = group_column(row, GROUPS, per_channel)
    return center, lax.rsqrt(square - center * center + 1e-06)


def copies(sem, *pairs):
    started = [pltpu.make_async_copy(source, target, sem.at[i]) for i, (source, target) in enumerate(pairs)]
    for copy in started:
        copy.start()
    return started


def start_kernel(lat, cot, sums, tail, head, first, sem):
    early, late, moved = copies(sem, (lat.at[: T - HALO], first), (lat.at[T - HALO :], tail), (cot.at[:HALO], head))
    total = jnp.zeros((ROWS, W), F32)
    square = jnp.zeros((ROWS, W), F32)
    for copy, frames in ((early, first), (late, tail)):
        copy.wait()
        for t in range(T // 2):
            x = frames[t].astype(F32)
            total = total + x
            square = square + x * x
    total = jnp.sum(jnp.sum(total.reshape(GROUPS, -1, W), axis=1), axis=1, keepdims=True)
    square = jnp.sum(jnp.sum(square.reshape(GROUPS, -1, W), axis=1), axis=1, keepdims=True)
    row = row_of(total, 0) + row_of(square, GROUPS)
    sums[...] = jnp.broadcast_to(row, (8, W))
    moved.wait()


def prepare_kernel(lat, cot, gain, shift, blocks, adj, scales, lat_v, cot_v, tmp, sem):
    from_lat, from_cot = copies(sem, (lat, lat_v), (cot, cot_v))
    scales[0] = jnp.broadcast_to(channel_column(gain[...]), (C, W))
    scales[1] = jnp.broadcast_to(channel_column(shift[...]), (C, W))
    from_lat.wait()
    for t in range(T):
        for h, block in enumerate(by_row(lat_v[t], tmp)):
            blocks[t * H + h] = block
    from_cot.wait()
    zero = jnp.zeros((C, W), BF16)
    for t in range(T):
        mine = by_row(cot_v[t], tmp)
        for h in range(H):
            for ki in range(3):
                source = h - ki + 1
                block = mine[source].astype(BF16) if 0 <= source < H else zero
                adj[ki * C : (ki + 1) * C, (t * H + h) * W : (t * H + h + 1) * W] = block


def by_row(frame, tmp):
    tmp[...] = frame.astype(F32)
    return [tmp[pl.ds(h, C, stride=H), :] for h in range(H)]


def back_kernel(
    lat, cot, following, kernel, totals, scales, scaled, sums, tmp, window, taps, lat_v, cot_v, kernel_v, scaled_v, sem
):
    from_cot, from_kernel, from_lat = copies(sem, (cot, cot_v), (kernel, kernel_v), (lat, lat_v))
    from_cot.wait()
    for f in range(T + HALO):
        blocks = by_row(cot_v[f] if f < T else following[f - T], tmp)
        for h in range(H):
            for s, moved in enumerate(shifted(blocks[h])):
                at = (s * H + h) * C
                window[at : at + C, f * W : (f + 1) * W] = moved.astype(BF16)
    taps[...] = jnp.zeros_like(taps)
    from_kernel.wait()
    for kt in range(3):
        for ki in range(3):
            for kj in range(3):
                tap = kernel_v[9 * kt + 3 * ki + kj].astype(F32).T.astype(BF16)
                for h in range(H):
                    other = h + 1 - ki
                    if 0 <= other < H:
                        at = ((2 - kj) * H + other) * C
                        taps[2 - kt, h * C : (h + 1) * C, at : at + C] = tap
    back = jnp.dot(taps[0], window[:, 0 : T * W], preferred_element_type=F32)
    for f in range(1, 3):
        back = back + jnp.dot(taps[f], window[:, f * W : (f + T) * W], preferred_element_type=F32)
    center, inverse = center_inverse(totals, PER)
    from_lat.wait()
    first = jnp.zeros((C, W), F32)
    second = jnp.zeros((C, W), F32)
    for t in range(T):
        blocks = by_row(lat_v[t], tmp)
        for h in range(H):
            unit = (blocks[h] - center) * inverse
            normed = unit * scales[0] + scales[1]
            sig = 1.0 / (1.0 + jnp.exp(-normed))
            adjoint = back[h * C : (h + 1) * C, t * W : (t + 1) * W]
            value = adjoint * sig * (1.0 + normed * (1.0 - sig)) * scales[0]
            first = first + value
            second = second + value * unit
            scaled_v[t, pl.ds(h, C, stride=H), :] = value
    (to_scaled,) = copies(sem, (scaled_v, scaled))
    lane, sub = lanes(), rows()
    first = jnp.where(lane == sub // PER, jnp.sum(first, axis=1, keepdims=True), 0.0)
    second = jnp.where(lane == sub // PER + GROUPS, jnp.sum(second, axis=1, keepdims=True), 0.0)
    sums[...] = jnp.broadcast_to(jnp.sum(first + second, axis=0, keepdims=True), (8, W))
    to_scaled.wait()


def grad_kernel(flags, blocks, previous, adj, totals, scales, window, keep, send, tmp, flat, window_v, sem):
    has_previous, core = flags[0], flags[1]
    center, inverse = center_inverse(totals, PER)
    for f in range(T + HALO):
        t = f - HALO
        halo = by_row(previous[f], tmp) if t < 0 else None
        for h in range(H):
            block = halo[h] if t < 0 else blocks[t * H + h]
            normed = (block - center) * inverse * scales[0] + scales[1]
            active = normed * (1.0 / (1.0 + jnp.exp(-normed)))
            if t < 0:
                active = jnp.where(has_previous > 0, active, 0.0)
            for s, moved in enumerate(shifted(active.astype(BF16).astype(F32))):
                moved = moved.astype(BF16)
                window_v[(s * H + h) * C : (s * H + h + 1) * C, f * W : (f + 1) * W] = moved
                flat[s * C : (s + 1) * C, (f * H + h) * W : (f * H + h + 1) * W] = moved
    (to_window,) = copies(sem, (window_v, window))
    half = C // 2
    for kt in range(3):
        grads = lax.dot_general(
            adj[...],
            flat[:, kt * H * W : (kt + T) * H * W],
            (((1,), (1,)), ((), ())),
            preferred_element_type=F32,
        )
        for ki in range(3):
            for kj in range(3):
                tap = grads[ki * C : (ki + 1) * C, kj * C : (kj + 1) * C]
                low, high = tap[:half], tap[half:]
                at = (9 * kt + 3 * ki + kj) * half
                keep[at : at + half] = jnp.where(core == 0, low, high)
                send[at : at + half] = jnp.where(core == 0, high, low)
    keep[HALF:] = jnp.zeros((COMM - HALF, C), F32)
    send[HALF:] = jnp.zeros((COMM - HALF, C), F32)
    to_window.wait()


def add_kernel(keep, received, chip):
    chip[...] = (keep[...] + received[...]).astype(chip.dtype)


def part_kernel(parts, sums, packed):
    packed[:PART] = jnp.sum(parts[...].astype(F32), axis=0)
    packed[PART:] = sums[...]


def place_kernel(flags, mine, other, grad):
    half = C // 2
    core = flags[1]
    for tap in range(27):
        a = mine[tap * half : (tap + 1) * half].astype(F32)
        b = other[tap * half : (tap + 1) * half].astype(F32)
        grad[tap, :half] = jnp.where(core == 0, a, b)
        grad[tap, half:] = jnp.where(core == 0, b, a)


def conv_kernel(lat, kernel, window, output, tmp, taps, lat_v, kernel_v, window_v, sem):
    from_kernel, from_window, from_lat = copies(sem, (kernel, kernel_v), (window, window_v), (lat, lat_v))
    taps[...] = jnp.zeros_like(taps)
    from_kernel.wait()
    for kt in range(3):
        for ki in range(3):
            for kj in range(3):
                tap = kernel_v[9 * kt + 3 * ki + kj]
                for h in range(H):
                    other = h - 1 + ki
                    if 0 <= other < H:
                        at = (kj * H + other) * C
                        taps[kt, h * C : (h + 1) * C, at : at + C] = tap
    from_window.wait()
    total = jnp.dot(taps[0], window_v[:, 0 : T * W], preferred_element_type=F32)
    for f in range(1, 3):
        total = total + jnp.dot(taps[f], window_v[:, f * W : (f + T) * W], preferred_element_type=F32)
    from_lat.wait()
    for t in range(T):
        for h in range(H):
            tmp[pl.ds(h, C, stride=H), :] = total[h * C : (h + 1) * C, t * W : (t + 1) * W]
        output[t] = (lat_v[t].astype(F32) + tmp[...]).astype(BF16)


def adjoint_kernel(lat, cot, totals, backward, scaled, result, lat_v, cot_v, scaled_v, sem):
    started = copies(sem, (lat, lat_v), (cot, cot_v), (scaled, scaled_v))
    center, inverse = center_inverse(totals, PER * H)
    row = backward[...][0:1] / MEMBERS
    first = group_column(row, 0, PER * H)
    second = group_column(row, GROUPS, PER * H)
    for copy in started:
        copy.wait()
    for t in range(T):
        unit = (lat_v[t].astype(F32) - center) * inverse
        value = cot_v[t].astype(F32) + inverse * (scaled_v[t] - first - unit * second)
        result[t] = value.astype(BF16)


VMEM, HBM, SMEM = (
    pl.BlockSpec(memory_space=pltpu.VMEM),
    pl.BlockSpec(memory_space=pltpu.HBM),
    pl.BlockSpec(memory_space=pltpu.SMEM),
)


def call(body, out, scratch, *operands, far=(), out_far=(), scalars=0, flops=0, moved=1 << 20):
    single = not isinstance(out, tuple)
    count = 1 if single else len(out)
    outs = tuple(HBM if i in out_far else VMEM for i in range(count))
    shapes = tuple(pltpu.HBM(o.shape, o.dtype) if i in out_far else o for i, o in enumerate((out,) if single else out))
    operands = [pltpu.with_memory_space_constraint(x, pltpu.HBM) if i in far else x for i, x in enumerate(operands)]
    return pl.pallas_call(
        body,
        out_shape=shapes[0] if single else shapes,
        in_specs=[SMEM if i < scalars else HBM if i in far else VMEM for i in range(len(operands))],
        out_specs=outs[0] if single else outs,
        scratch_shapes=scratch,
        compiler_params=LIMIT,
        cost_estimate=pl.CostEstimate(flops=flops, bytes_accessed=moved, transcendentals=0),
    )(*operands)


def shape(*dims, dtype=F32):
    return jax.ShapeDtypeStruct(dims, dtype)


def sems(count):
    return pltpu.SemaphoreType.DMA((count,))


def swap(value, axis):
    return lax.ppermute(value, axis, [(0, 1), (1, 0)])


def exchange(parts, axes):
    return lax.all_to_all(parts, axes, 0, 0)


def same_to_all(part, size, axes):
    return exchange(jnp.broadcast_to(part, (size,) + part.shape), axes)


def per_device(latents, norm_gain, norm_shift, kernel, cotangent):
    lat = latents.reshape(T, ROWS, W)
    cot = cotangent.reshape(T, ROWS, W)
    gain, shift = norm_gain.reshape(1, C), norm_shift.reshape(1, C)
    slab = ("zh", "core")
    halo = shape(HALO, ROWS, W, dtype=BF16)
    frames = pltpu.VMEM((T, ROWS, W), BF16)
    tmp = pltpu.VMEM((ROWS, W), F32)
    window_scratch = pltpu.VMEM((3 * ROWS, (T + HALO) * W), BF16)
    taps = pltpu.VMEM((3, ROWS, 3 * ROWS), BF16)
    kernel_scratch = pltpu.VMEM((27, C, C), BF16)
    scaled_scratch = pltpu.VMEM((T, ROWS, W), F32)
    own, tail, head = call(
        start_kernel,
        (shape(8, W), halo, halo),
        [pltpu.VMEM((T - HALO, ROWS, W), BF16), sems(3)],
        lat,
        cot,
        far=(0, 1),
    )
    blocks, adj, scales = call(
        prepare_kernel,
        (shape(T * H, C, W), shape(3 * C, T * H * W, dtype=BF16), shape(2, C, W)),
        [frames, frames, tmp, sems(2)],
        lat,
        cot,
        gain,
        shift,
        far=(0, 1),
    )
    pair = own + swap(own, "core")
    totals = jnp.concatenate([pair, swap(pair, "zh")], axis=0)
    previous = lax.ppermute(tail, slab, [(i, i + 1) for i in range(SLABS - 1)])
    following = lax.ppermute(head, slab, [(i + 1, i) for i in range(SLABS - 1)])
    zh, core = lax.axis_index("zh"), lax.axis_index("core")
    flags = jnp.stack([zh * 2 + core, core]).astype(jnp.int32)
    window, keep, send = call(
        grad_kernel,
        (shape(3 * ROWS, (T + HALO) * W, dtype=BF16), shape(COMM, C), shape(COMM, C)),
        [tmp, pltpu.VMEM((3 * C, (T + HALO) * H * W), BF16), window_scratch, sems(1)],
        flags,
        blocks,
        previous,
        adj,
        totals,
        scales,
        out_far=(0,),
        scalars=1,
        flops=4 * 10**9,
    )
    chip = call(add_kernel, shape(COMM, C, dtype=WIRE), [], keep, swap(send, "core"))
    parts = exchange(chip.reshape(SIDE, PART, C), ("y", "zn", "x"))
    scaled, sums = call(
        back_kernel,
        (shape(T, ROWS, W), shape(8, W)),
        [tmp, window_scratch, taps, frames, frames, kernel_scratch, scaled_scratch, sems(3)],
        lat,
        cot,
        following,
        kernel,
        totals,
        scales,
        far=(0, 1, 3),
        out_far=(0,),
        flops=4 * 10**9,
    )
    sums = sums + swap(sums, "core")
    packed = call(part_kernel, shape(PART + 8, C), [], parts, sums)
    over_z = same_to_all(packed, 4, ("zh", "zm"))
    part = jnp.sum(over_z[:, :PART], axis=0).astype(BF16)
    zm = lax.axis_index("zm")
    backward = jnp.sum(
        jnp.where(lax.broadcasted_iota(jnp.int32, (2, 2, 8, C), 1) == zm, over_z[:, PART:].reshape(2, 2, 8, C), 0.0),
        axis=(0, 1),
    )
    part, window = lax.optimization_barrier((part, window))
    mine = same_to_all(part, SIDE, ("y", "zn", "x")).reshape(COMM, C)
    output = call(
        conv_kernel,
        shape(T, ROWS, W, dtype=BF16),
        [tmp, taps, frames, kernel_scratch, window_scratch, sems(3)],
        lat,
        kernel,
        window,
        far=(0, 1, 2),
        flops=4 * 10**9,
    )
    mine, output = lax.optimization_barrier((mine, output))
    other = swap(mine, "core")
    result = call(
        adjoint_kernel,
        shape(T, ROWS, W, dtype=BF16),
        [frames, frames, scaled_scratch, sems(3)],
        lat,
        cot,
        totals,
        backward,
        scaled,
        far=(0, 1, 4),
        flops=10**9,
    )
    kernel_grad = call(place_kernel, shape(27, C, C), [], flags, mine, other, scalars=1)
    return output.reshape(latents.shape), result.reshape(latents.shape), kernel_grad


WIRE = F32


def solution(mesh):
    fine = Mesh(mesh.devices.reshape(2, 2, 4, 2, 2, 4), ("zh", "core", "y", "zm", "zn", "x"))
    frames = P(("y", "zm", "zn", "x"), ("zh", "core"), None, None, None)
    return jax.shard_map(
        per_device,
        mesh=fine,
        in_specs=(frames, P(), P(), P(), frames),
        out_specs=(frames, frames, P()),
        check_vma=False,
    )
```

time: 107 us -> 99.6 us (0.931)
  blocking collectives: 31 us -> 11.7 us
  Pallas kernels: 13.5 us -> 24.5 us
  starting transfers between devices: 24.8 us -> 33.8 us
  local copies, waits for them, and re-layouts: 9.21 us -> 2.24 us
  other arithmetic: 3.67 us -> 0.18 us
  waiting for transfers between devices: 23.5 us -> 25.9 us
    all_to_all x2 -> x1, blocking collectives: 31 us -> 11.7 us  [exchange(): return lax.all_to_all(parts, axes, 0, 0)]
    ppermute x2, waiting for transfers between devices: 0.01 us -> 14.9 us  [the longest x1 14.9 us: per_device(): following = lax.ppermute(head, slab, [(i + 1, i) for i in range(SLABS - 1)])]
    pallas_call x5 -> x9, Pallas kernels: 13.5 us -> 24.5 us  [call(): pl.pallas_call(body, out_shape=shapes[0] if single else shapes, in_specs=...]
    all_to_all x1 -> x2, waiting for transfers between devices: 14.2 us -> 3.26 us  [exchange(): return lax.all_to_all(parts, axes, 0, 0)]
    all_to_all x1 -> x2, starting transfers between devices: 6.76 us -> 16.6 us  [exchange(): return lax.all_to_all(parts, axes, 0, 0)]
    slice x5 -> x0, local copies, waits for them, and re-layouts: 4.45 us -> none  [the longest x1 1.11 us: per_device(): cot[:HALO]]
    unnamed x18 -> x4, local copies, waits for them, and re-layouts: 4.67 us -> 1.31 us
    ppermute x4 -> x5, starting transfers between devices: 5.96 us -> 4.35 us  [swap(): return lax.ppermute(value, axis, [(0, 1), (1, 0)])]
  transfers between devices with their start and end apart: 7 -> 9, of which waited for: 4 -> 6; matrix products, arithmetic and copies ran while one was open for 2% -> 0% of each run, Pallas kernels for 8% -> 16%
where the time goes in v2:
time: 99.6 us; the launch traced here: 99.2 us
  starting transfers between devices  33.8 us (34%)
  waiting for transfers between devices  25.9 us (26%)
  Pallas kernels  24.5 us (25%)
  blocking collectives  11.7 us (12%)
  local copies, waits for them, and re-layouts  2.24 us (2%)
    pallas_call x9, Pallas kernels, call(): pl.pallas_call(body, out_shape=shapes[0] if single else shapes, in_specs=...  24.5 us
    all_to_all x2, starting transfers between devices, exchange(): return lax.all_to_all(parts, axes, 0, 0)  16.6 us
    ppermute x1, waiting for transfers between devices, per_device(): following = lax.ppermute(head, slab, [(i + 1, i) for i in range(SLABS - 1)])  14.9 us
    all_to_all x1, blocking collectives, exchange(): return lax.all_to_all(parts, axes, 0, 0)  11.7 us
    ppermute x1, starting transfers between devices, per_device(): previous = lax.ppermute(tail, slab, [(i, i + 1) for i in range(SLABS - 1)])  10.2 us
    ppermute x5, waiting for transfers between devices, swap(): return lax.ppermute(value, axis, [(0, 1), (1, 0)])  7.79 us
    ppermute x5, starting transfers between devices, swap(): return lax.ppermute(value, axis, [(0, 1), (1, 0)])  4.35 us
    all_to_all x2, waiting for transfers between devices, exchange(): return lax.all_to_all(parts, axes, 0, 0)  3.26 us
  transfers between devices with their start and end apart: 9, of which 6 were waited for; matrix products, arithmetic and copies ran while one was open for 0% of the time, Pallas kernels for 16%

profile of v2, /device:TPU:1, one launch (start us, length us, event | category | flops | bytes accessed | tf_op | source)
XLA Modules:
  0.0 99.2 jit_solution(15494026548298314326)
XLA Ops:
  0.6 1.3 %shard_map.77 = (f32[8,128]{1,0:T(8,128)S(1)}, bf16[2,512,128]{2,1,0:T(8,128)(2,1)S(1)}, bf16[2,512,128]{2,1,0:T(8,128)(2,1)S(1)}) custom-call(bf16[4,512,128]{2,1,0:T(8,128)(2,1)} %bitcast.14, bf16[4,512,128]{2,1,0:T(8,128)(2,1)} %bitcast.19), custom_call_target="tpu_custom_call" | custom-call | bytes 1048576 | tf_op jit(solution)/shard_map/pallas_call | solution.py:270
  1.9 10.2 %collective-permute-start = (bf16[2,512,128]{2,1,0:T(8,128)(2,1)S(1)}, bf16[2,512,128]{2,1,0:T(8,128)(2,1)S(1)}, u32[]{:S(2)}, u32[]{:S(2)}) collective-permute-start(bf16[2,512,128]{2,1,0:T(8,128)(2,1)S(1)} %get-tuple-element.19), channel_id=1, source_target_pairs={{0,64},{64,128},{128,192},{1,65},{65,129},{129,193},{2,66},{66,130... | collective-permute-start | bytes 786440 | tf_op jit(solution)/shard_map/ppermute | solution.py:333
  12.1 0.1 collective-permute-start.1
  12.3 1.1 %collective-permute-done.1 = f32[8,128]{1,0:T(8,128)S(1)} collective-permute-done((f32[8,128]{1,0:T(8,128)S(1)}, f32[8,128]{1,0:T(8,128)S(1)}, u32[]{:S(2)}, u32[]{:S(2)}) %collective-permute-start.1) | collective-permute-done | bytes 4128 | tf_op jit(solution)/shard_map/ppermute | solution.py:290
  13.4 0.0 collective-permute-start.2
  13.4 0.1 pad_add_fusion.flags
  13.5 0.0 copy-start
  13.5 0.7 copy-done
  14.1 0.0 copy-start.1
  14.1 0.7 copy-done.1
  14.8 1.6 %shard_map.76 = (f32[16,128,128]{2,1,0:T(8,128)S(1)}, bf16[384,2048]{1,0:T(8,128)(2,1)S(1)}, f32[2,128,128]{2,1,0:T(8,128)S(1)}) custom-call(bf16[4,512,128]{2,1,0:T(8,128)(2,1)} %bitcast.15, bf16[4,512,128]{2,1,0:T(8,128)(2,1)} %bitcast.20, f32[1,128]{1,0:T(1,128)S(1)} %bitcast.12, f32[1,128]{1,0:T(1,128)S(1)} %bitcast.13), custom_call_target="tpu_custom_call" | custom-call | bytes 1048576 | tf_op jit(solution)/shard_map/pallas_call | solution.py:270
  16.4 3.4 %collective-permute-done.2 = f32[8,128]{1,0:T(8,128)S(1)} collective-permute-done((f32[8,128]{1,0:T(8,128)S(1)}, f32[8,128]{1,0:T(8,128)S(1)}, u32[]{:S(2)}, u32[]{:S(2)}) %collective-permute-start.2) | collective-permute-done | bytes 4128 | tf_op jit(solution)/shard_map/ppermute | solution.py:290
  19.8 0.0 collective-permute-done.previous
  19.8 4.0 %shard_map.78 = (bf16[1536,768]{1,0:T(8,128)(2,1)}, f32[1792,128]{1,0:T(8,128)S(1)}, f32[1792,128]{1,0:T(8,128)S(1)}) custom-call(s32[2]{0:T(128)S(1)} %pad_add_fusion.flags, f32[16,128,128]{2,1,0:T(8,128)S(1)} %get-tuple-element.18.blocks, bf16[2,512,128]{2,1,0:T(8,128)(2,1)S(1)} %collective-permute-done.previous, ...), custom_call_target="tpu_custom_call" | custom-call | flops 4000000000 | bytes 1048576 | tf_op jit(solution)/shard_map/pallas_call | solution.py:270
  23.7 1.4 %collective-permute-start.3 = (f32[1792,128]{1,0:T(8,128)S(1)}, f32[1792,128]{1,0:T(8,128)S(1)}, u32[]{:S(2)}, u32[]{:S(2)}) collective-permute-start(f32[1792,128]{1,0:T(8,128)S(1)} %get-tuple-element.24), channel_id=1, source_target_pairs={{0,64},{64,0},{1,65},{65,1},{2,66},{66,2},{3,67},{67,3},{4,68},{68... | collective-permute-start | bytes 2752520 | tf_op jit(solution)/shard_map/ppermute | solution.py:290
  25.1 2.1 %collective-permute-done.3.received = f32[1792,128]{1,0:T(8,128)S(1)} collective-permute-done((f32[1792,128]{1,0:T(8,128)S(1)}, f32[1792,128]{1,0:T(8,128)S(1)}, u32[]{:S(2)}, u32[]{:S(2)}) %collective-permute-start.3) | collective-permute-done | bytes 917536 | tf_op jit(solution)/shard_map/ppermute | solution.py:290
  27.2 1.1 %shard_map.79 = f32[1792,128]{1,0:T(8,128)} custom-call(f32[1792,128]{1,0:T(8,128)S(1)} %get-tuple-element.23.keep, f32[1792,128]{1,0:T(8,128)S(1)} %collective-permute-done.3.received), custom_call_target="tpu_custom_call" | custom-call | bytes 1048576 | tf_op jit(solution)/shard_map/pallas_call | solution.py:270
  28.3 7.5 %all-to-all-start = ((f32[32,56,128]{2,1,0:T(8,128)}), f32[32,56,128]{2,1,0:T(8,128)S(1)}, u32[]{:S(2)}, u32[]{:S(2)}) async-start(f32[32,56,128]{2,1,0:T(8,128)} %bitcast.6), calls=%async_computation | async-start | bytes 1835008 | tf_op jit(solution)/shard_map/all_to_all | solution.py:294
  35.8 2.6 %collective-permute-start.4 = (bf16[2,512,128]{2,1,0:T(8,128)(2,1)S(1)}, bf16[2,512,128]{2,1,0:T(8,128)(2,1)S(1)}, u32[]{:S(2)}, u32[]{:S(2)}) collective-permute-start(bf16[2,512,128]{2,1,0:T(8,128)(2,1)S(1)} %get-tuple-element.25), channel_id=1, source_target_pairs={{64,0},{128,64},{192,128},{65,1},{129,65},{193,129},{66,2},{130,66... | collective-permute-start | bytes 786440 | tf_op jit(solution)/shard_map/ppermute | solution.py:334
  38.4 14.9 %collective-permute-done.4.following = bf16[2,512,128]{2,1,0:T(8,128)(2,1)S(1)} collective-permute-done((bf16[2,512,128]{2,1,0:T(8,128)(2,1)S(1)}, bf16[2,512,128]{2,1,0:T(8,128)(2,1)S(1)}, u32[]{:S(2)}, u32[]{:S(2)}) %collective-permute-start.4) | collective-permute-done | bytes 262176 | tf_op jit(solution)/shard_map/ppermute | solution.py:334
  53.3 6.3 %shard_map.80 = (f32[4,512,128]{2,1,0:T(8,128)}, f32[8,128]{1,0:T(8,128)S(1)}) custom-call(bf16[4,512,128]{2,1,0:T(8,128)(2,1)} %bitcast.16, bf16[4,512,128]{2,1,0:T(8,128)(2,1)} %bitcast.21, bf16[2,512,128]{2,1,0:T(8,128)(2,1)S(1)} %collective-permute-done.4.following, bf16[27,128,128]{2,1,0:T(8,128)(2,1)} %kernel.3, f32[16,128]{1,0:T(8,128)S(1)} %pad_maximum_fusion.totals, ...), custom_call_target="tpu_custom_call" | custom-call | flops 4000000000 | bytes 1048576 | tf_op jit(solution)/shard_map/pallas_call | solution.py:270
  59.6 0.1 collective-permute-start.5
  59.7 1.2 %collective-permute-done.5 = f32[8,128]{1,0:T(8,128)S(1)} collective-permute-done((f32[8,128]{1,0:T(8,128)S(1)}, f32[8,128]{1,0:T(8,128)S(1)}, u32[]{:S(2)}, u32[]{:S(2)}) %collective-permute-start.5) | collective-permute-done | bytes 4128 | tf_op jit(solution)/shard_map/ppermute | solution.py:290
  60.8 0.0 all-to-all-done.parts
  60.8 0.1 shard_map.81
  60.9 11.7 %all_to_all.15 = f32[4,64,128]{2,1,0:T(8,128)S(1)} all-to-all(f32[4,64,128]{2,1,0:T(8,128)S(1)} %broadcast_in_dim.10), channel_id=1, replica_groups=mesh['zh'=2,'core'=2,'y'=4,'zm'=2,'zn'=2,'x'=4] {'zh','zm'}, dimensions={0} | all-to-all | bytes 262144 | tf_op jit(solution)/shard_map/all_to_all | solution.py:294
  72.7 0.8 broadcast_in_dim.11
  73.5 9.2 %all-to-all-start.2 = ((bf16[32,56,128]{2,1,0:T(8,128)(2,1)}), bf16[32,56,128]{2,1,0:T(8,128)(2,1)S(1)}, u32[]{:S(2)}, u32[]{:S(2)}) async-start(bf16[32,56,128]{2,1,0:T(8,128)(2,1)} %broadcast_in_dim.11), calls=%async_computation.2 | async-start | bytes 917504 | tf_op jit(solution)/shard_map/all_to_all | solution.py:294
  82.7 5.6 %shard_map.82 = bf16[4,512,128]{2,1,0:T(8,128)(2,1)} custom-call(bf16[4,512,128]{2,1,0:T(8,128)(2,1)} %bitcast.17, bf16[27,128,128]{2,1,0:T(8,128)(2,1)} %kernel.3, bf16[1536,768]{1,0:T(8,128)(2,1)} %get-tuple-element.29.window), custom_call_target="tpu_custom_call" | custom-call | flops 4000000000 | bytes 1048576 | tf_op jit(solution)/shard_map/pallas_call | solution.py:270
  88.3 3.3 %all-to-all-done.2 = bf16[32,56,128]{2,1,0:T(8,128)(2,1)S(1)} async-done(((bf16[32,56,128]{2,1,0:T(8,128)(2,1)}), bf16[32,56,128]{2,1,0:T(8,128)(2,1)S(1)}, u32[]{:S(2)}, u32[]{:S(2)}) %all-to-all-start.2) | async-done | bytes 458784 | tf_op jit(solution)/shard_map/all_to_all | solution.py:294
  91.5 2.8 %collective-permute-start.6 = (bf16[1792,128]{1,0:T(8,128)(2,1)S(1)}, bf16[1792,128]{1,0:T(8,128)(2,1)S(1)}, u32[]{:S(2)}, u32[]{:S(2)}) collective-permute-start(bf16[1792,128]{1,0:T(8,128)(2,1)S(1)} %bitcast.10), channel_id=1, source_target_pairs={{0,64},{64,0},{1,65},{65,1},{2,66},{66,2},{3,67},{67,3},{4,68},{68... | collective-permute-start | bytes 1376264 | tf_op jit(solution)/shard_map/ppermute | solution.py:290
  94.3 0.1 iota.12
  94.4 0.1 fusion.backward
  94.4 2.8 %shard_map.83 = bf16[4,512,128]{2,1,0:T(8,128)(2,1)} custom-call(bf16[4,512,128]{2,1,0:T(8,128)(2,1)} %bitcast.18, bf16[4,512,128]{2,1,0:T(8,128)(2,1)} %bitcast.22, f32[16,128]{1,0:T(8,128)S(1)} %pad_maximum_fusion.totals, f32[8,128]{1,0:T(8,128)S(1)} %fusion.backward, f32[4,512,128]{2,1,0:T(8,128)} %get-tuple-element.31.scaled), custom_call_target="tpu_custom_call" | custom-call | flops 1000000000 | bytes 1048576 | tf_op jit(solution)/shard_map/pallas_call | solution.py:270
  97.3 0.0 collective-permute-done.6.other
  97.3 1.9 %shard_map.84 = f32[27,128,128]{2,1,0:T(8,128)} custom-call(s32[2]{0:T(128)S(1)} %pad_add_fusion.flags, bf16[1792,128]{1,0:T(8,128)(2,1)S(1)} %bitcast.11, bf16[1792,128]{1,0:T(8,128)(2,1)S(1)} %collective-permute-done.6.other), custom_call_target="tpu_custom_call" | custom-call | bytes 1048576 | tf_op jit(solution)/shard_map/pallas_call | solution.py:270
  (7 shorter events, 0.0 us)
Async XLA Ops:
  1.9 17.8 %collective-permute-start = (bf16[2,512,128]{2,1,0:T(8,128)(2,1)S(1)}, bf16[2,512,128]{2,1,0:T(8,128)(2,1)S(1)}, u32[]{:S(2)}, u32[]{:S(2)}) collective-permute-start(bf16[2,512,128]{2,1,0:T(8,128)(2,1)S(1)} %get-tuple-element.19), channel_id=1, source_target_pairs={{0,64},{64,128},{128,192},{1,65},{65,129},{129,193},{2,66},{66,130... | collective-permute-start | bytes 786440 | tf_op jit(solution)/shard_map/ppermute | solution.py:333
  12.1 1.3 %collective-permute-start.1 = (f32[8,128]{1,0:T(8,128)S(1)}, f32[8,128]{1,0:T(8,128)S(1)}, u32[]{:S(2)}, u32[]{:S(2)}) collective-permute-start(f32[8,128]{1,0:T(8,128)S(1)} %get-tuple-element.21), channel_id=1, source_target_pairs={{0,64},{64,0},{1,65},{65,1},{2,66},{66,2},{3,67},{67,3},{4,68},{68... | collective-permute-start | bytes 12296 | tf_op jit(solution)/shard_map/ppermute | solution.py:290
  13.4 6.4 %collective-permute-start.2 = (f32[8,128]{1,0:T(8,128)S(1)}, f32[8,128]{1,0:T(8,128)S(1)}, u32[]{:S(2)}, u32[]{:S(2)}) collective-permute-start(f32[8,128]{1,0:T(8,128)S(1)} %add.10), channel_id=1, source_target_pairs={{0,128},{128,0},{1,129},{129,1},{2,130},{130,2},{3,131},{131,3},{4... | collective-permute-start | bytes 12296 | tf_op jit(solution)/shard_map/ppermute | solution.py:290
  13.5 0.7 copy-start
  14.1 0.7 copy-start.1
  23.7 3.5 %collective-permute-start.3 = (f32[1792,128]{1,0:T(8,128)S(1)}, f32[1792,128]{1,0:T(8,128)S(1)}, u32[]{:S(2)}, u32[]{:S(2)}) collective-permute-start(f32[1792,128]{1,0:T(8,128)S(1)} %get-tuple-element.24), channel_id=1, source_target_pairs={{0,64},{64,0},{1,65},{65,1},{2,66},{66,2},{3,67},{67,3},{4,68},{68... | collective-permute-start | bytes 2752520 | tf_op jit(solution)/shard_map/ppermute | solution.py:290
  28.3 32.5 %all-to-all-start = ((f32[32,56,128]{2,1,0:T(8,128)}), f32[32,56,128]{2,1,0:T(8,128)S(1)}, u32[]{:S(2)}, u32[]{:S(2)}) async-start(f32[32,56,128]{2,1,0:T(8,128)} %bitcast.6), calls=%async_computation | async-start | bytes 1835008 | tf_op jit(solution)/shard_map/all_to_all | solution.py:294
  35.8 17.4 %collective-permute-start.4 = (bf16[2,512,128]{2,1,0:T(8,128)(2,1)S(1)}, bf16[2,512,128]{2,1,0:T(8,128)(2,1)S(1)}, u32[]{:S(2)}, u32[]{:S(2)}) collective-permute-start(bf16[2,512,128]{2,1,0:T(8,128)(2,1)S(1)} %get-tuple-element.25), channel_id=1, source_target_pairs={{64,0},{128,64},{192,128},{65,1},{129,65},{193,129},{66,2},{130,66... | collective-permute-start | bytes 786440 | tf_op jit(solution)/shard_map/ppermute | solution.py:334
  59.6 1.3 %collective-permute-start.5 = (f32[8,128]{1,0:T(8,128)S(1)}, f32[8,128]{1,0:T(8,128)S(1)}, u32[]{:S(2)}, u32[]{:S(2)}) collective-permute-start(f32[8,128]{1,0:T(8,128)S(1)} %get-tuple-element.26), channel_id=1, source_target_pairs={{0,64},{64,0},{1,65},{65,1},{2,66},{66,2},{3,67},{67,3},{4,68},{68... | collective-permute-start | bytes 12296 | tf_op jit(solution)/shard_map/ppermute | solution.py:290
  73.5 18.0 %all-to-all-start.2 = ((bf16[32,56,128]{2,1,0:T(8,128)(2,1)}), bf16[32,56,128]{2,1,0:T(8,128)(2,1)S(1)}, u32[]{:S(2)}, u32[]{:S(2)}) async-start(bf16[32,56,128]{2,1,0:T(8,128)(2,1)} %broadcast_in_dim.11), calls=%async_computation.2 | async-start | bytes 917504 | tf_op jit(solution)/shard_map/all_to_all | solution.py:294
  91.5 5.8 %collective-permute-start.6 = (bf16[1792,128]{1,0:T(8,128)(2,1)S(1)}, bf16[1792,128]{1,0:T(8,128)(2,1)S(1)}, u32[]{:S(2)}, u32[]{:S(2)}) collective-permute-start(bf16[1792,128]{1,0:T(8,128)(2,1)S(1)} %bitcast.10), channel_id=1, source_target_pairs={{0,64},{64,0},{1,65},{65,1},{2,66},{66,2},{3,67},{67,3},{4,68},{68... | collective-permute-start | bytes 1376264 | tf_op jit(solution)/shard_map/ppermute | solution.py:290

commit v3 on v2

--- a/solution.py
+++ b/solution.py
@@ -71,40 +71,56 @@
     return started
 
 
-def start_kernel(lat, cot, sums, tail, head, first, sem):
-    early, late, moved = copies(sem, (lat.at[: T - HALO], first), (lat.at[T - HALO :], tail), (cot.at[:HALO], head))
+def start_kernel(flags, lat, cot, sums, near, far, lat_v, sem, halo_sem):
+    tail, head = lat.at[T - HALO :], cot.at[:HALO]
+
+    @pl.when(flags[1] == 0)
+    def _():
+        copies(halo_sem, (tail, near), (head, far))
+
+    @pl.when(flags[1] != 0)
+    def _():
+        copies(halo_sem, (head, near), (tail, far))
+
+    parts = copies(sem, (lat.at[: T // 2], lat_v.at[: T // 2]), (lat.at[T // 2 :], lat_v.at[T // 2 :]))
     total = jnp.zeros((ROWS, W), F32)
     square = jnp.zeros((ROWS, W), F32)
-    for copy, frames in ((early, first), (late, tail)):
-        copy.wait()
-        for t in range(T // 2):
-            x = frames[t].astype(F32)
-            total = total + x
-            square = square + x * x
+    for t in range(T):
+        if t % (T // 2) == 0:
+            parts[t // (T // 2)].wait()
+        x = lat_v[t].astype(F32)
+        total = total + x
+        square = square + x * x
     total = jnp.sum(jnp.sum(total.reshape(GROUPS, -1, W), axis=1), axis=1, keepdims=True)
     square = jnp.sum(jnp.sum(square.reshape(GROUPS, -1, W), axis=1), axis=1, keepdims=True)
     row = row_of(total, 0) + row_of(square, GROUPS)
     sums[...] = jnp.broadcast_to(row, (8, W))
-    moved.wait()
-
-
-def prepare_kernel(lat, cot, gain, shift, blocks, adj, scales, lat_v, cot_v, tmp, sem):
-    from_lat, from_cot = copies(sem, (lat, lat_v), (cot, cot_v))
-    scales[0] = jnp.broadcast_to(channel_column(gain[...]), (C, W))
-    scales[1] = jnp.broadcast_to(channel_column(shift[...]), (C, W))
+    pltpu.make_async_copy(tail, near, halo_sem.at[0]).wait()
+    pltpu.make_async_copy(head, far, halo_sem.at[1]).wait()
+
+
+def put_adjoint(adj, f, mine):
+    zero = jnp.zeros((C, W), BF16)
+    for h in range(H):
+        for ki in range(3):
+            source = h - ki + 1
+            block = mine[source].astype(BF16) if 0 <= source < H else zero
+            adj[ki * C : (ki + 1) * C, (f * H + h) * W : (f * H + h + 1) * W] = block
+
+
+def prepare_kernel(lat, cot, gain, shift, blocks, adj, scales, lat_v, cot_v, gain_v, shift_v, tmp, sem):
+    from_lat, from_cot, *small = copies(sem, (lat, lat_v), (cot, cot_v), (gain, gain_v), (shift, shift_v))
     from_lat.wait()
     for t in range(T):
         for h, block in enumerate(by_row(lat_v[t], tmp)):
             blocks[t * H + h] = block
     from_cot.wait()
-    zero = jnp.zeros((C, W), BF16)
-    for t in range(T):
-        mine = by_row(cot_v[t], tmp)
-        for h in range(H):
-            for ki in range(3):
-                source = h - ki + 1
-                block = mine[source].astype(BF16) if 0 <= source < H else zero
-                adj[ki * C : (ki + 1) * C, (t * H + h) * W : (t * H + h + 1) * W] = block
+    for t in range(T):
+        put_adjoint(adj, t, by_row(cot_v[t], tmp))
+    for copy in small:
+        copy.wait()
+    scales[0] = jnp.broadcast_to(channel_column(gain_v[...]), (C, W))
+    scales[1] = jnp.broadcast_to(channel_column(shift_v[...]), (C, W))
 
 
 def by_row(frame, tmp):
@@ -112,13 +128,17 @@
     return [tmp[pl.ds(h, C, stride=H), :] for h in range(H)]
 
 
+def pick(condition, first, second):
+    return jnp.where(condition, first.astype(F32), second.astype(F32))
+
+
 def back_kernel(
-    lat, cot, following, kernel, totals, scales, scaled, sums, tmp, window, taps, lat_v, cot_v, kernel_v, scaled_v, sem
+    flags, lat, cot, near, far, kernel, totals, scales, scaled, sums, tmp, window, taps, lat_v, cot_v, kernel_v, scaled_v, sem
 ):
     from_cot, from_kernel, from_lat = copies(sem, (cot, cot_v), (kernel, kernel_v), (lat, lat_v))
     from_cot.wait()
     for f in range(T + HALO):
-        blocks = by_row(cot_v[f] if f < T else following[f - T], tmp)
+        blocks = by_row(cot_v[f] if f < T else pick(flags[1] == 0, near[f - T], far[f - T]), tmp)
         for h in range(H):
             for s, moved in enumerate(shifted(blocks[h])):
                 at = (s * H + h) * C
@@ -160,31 +180,36 @@
     to_scaled.wait()
 
 
-def grad_kernel(flags, blocks, previous, adj, totals, scales, window, keep, send, tmp, flat, window_v, sem):
-    has_previous, core = flags[0], flags[1]
+def activated(block, center, inverse, scales):
+    normed = (block - center) * inverse * scales[0] + scales[1]
+    return (normed * (1.0 / (1.0 + jnp.exp(-normed)))).astype(BF16).astype(F32)
+
+
+def grad_kernel(flags, blocks, near, far, adj, totals, scales, window, keep, send, tmp, flat, adj_v, window_v, sem):
+    core = flags[1]
     center, inverse = center_inverse(totals, PER)
-    for f in range(T + HALO):
-        t = f - HALO
-        halo = by_row(previous[f], tmp) if t < 0 else None
+    for f in range(HALO):
+        put_adjoint(adj_v, f, by_row(pick(core == 0, near[f], far[f]), tmp))
+    for t in range(T):
         for h in range(H):
-            block = halo[h] if t < 0 else blocks[t * H + h]
-            normed = (block - center) * inverse * scales[0] + scales[1]
-            active = normed * (1.0 / (1.0 + jnp.exp(-normed)))
-            if t < 0:
-                active = jnp.where(has_previous > 0, active, 0.0)
-            for s, moved in enumerate(shifted(active.astype(BF16).astype(F32))):
+            for s, moved in enumerate(shifted(activated(blocks[t * H + h], center, inverse, scales))):
                 moved = moved.astype(BF16)
-                window_v[(s * H + h) * C : (s * H + h + 1) * C, f * W : (f + 1) * W] = moved
-                flat[s * C : (s + 1) * C, (f * H + h) * W : (f * H + h + 1) * W] = moved
+                window_v[(s * H + h) * C : (s * H + h + 1) * C, t * W : (t + 1) * W] = moved
+                flat[s * C : (s + 1) * C, (t * H + h) * W : (t * H + h + 1) * W] = moved
     (to_window,) = copies(sem, (window_v, window))
+    contract = (((1,), (1,)), ((), ()))
+    plane = H * W
     half = C // 2
     for kt in range(3):
+        ahead = 2 - kt
+        own = T - ahead
         grads = lax.dot_general(
-            adj[...],
-            flat[:, kt * H * W : (kt + T) * H * W],
-            (((1,), (1,)), ((), ())),
-            preferred_element_type=F32,
+            adj[:, ahead * plane :], flat[:, : own * plane], contract, preferred_element_type=F32
         )
+        if ahead:
+            grads = grads + lax.dot_general(
+                adj_v[:, : ahead * plane], flat[:, own * plane :], contract, preferred_element_type=F32
+            )
         for ki in range(3):
             for kj in range(3):
                 tap = grads[ki * C : (ki + 1) * C, kj * C : (kj + 1) * C]
@@ -202,8 +227,19 @@
 
 
 def part_kernel(parts, sums, packed):
-    packed[:PART] = jnp.sum(parts[...].astype(F32), axis=0)
-    packed[PART:] = sums[...]
+    part = jnp.sum(parts[...].astype(F32), axis=0)
+    for i in range(4):
+        packed[i, :PART] = part
+        packed[i, PART:] = sums[...]
+
+
+def merge_kernel(flags, over_z, parts, backward):
+    part = jnp.sum(over_z[:, :PART], axis=0).astype(BF16)
+    for i in range(SIDE):
+        parts[i] = part
+    first = jnp.where(flags[2] == 0, over_z[0, PART:], over_z[1, PART:])
+    second = jnp.where(flags[2] == 0, over_z[2, PART:], over_z[3, PART:])
+    backward[...] = first + second
 
 
 def place_kernel(flags, mine, other, grad):
@@ -216,8 +252,19 @@
         grad[tap, half:] = jnp.where(core == 0, b, a)
 
 
-def conv_kernel(lat, kernel, window, output, tmp, taps, lat_v, kernel_v, window_v, sem):
-    from_kernel, from_window, from_lat = copies(sem, (kernel, kernel_v), (window, window_v), (lat, lat_v))
+def conv_kernel(
+    flags, lat, near, far, kernel, window, totals, scales, output, tmp, taps, lat_v, kernel_v, window_v, sem
+):
+    from_kernel, from_window, from_lat = copies(
+        sem, (kernel, kernel_v), (window, window_v.at[:, HALO * W :]), (lat, lat_v)
+    )
+    center, inverse = center_inverse(totals, PER)
+    for f in range(HALO):
+        blocks = by_row(pick(flags[1] == 0, far[f], near[f]), tmp)
+        for h in range(H):
+            active = jnp.where(flags[0] > 0, activated(blocks[h], center, inverse, scales), 0.0)
+            for s, moved in enumerate(shifted(active)):
+                window_v[(s * H + h) * C : (s * H + h + 1) * C, f * W : (f + 1) * W] = moved.astype(BF16)
     taps[...] = jnp.zeros_like(taps)
     from_kernel.wait()
     for kt in range(3):
@@ -294,53 +341,59 @@
     return lax.all_to_all(parts, axes, 0, 0)
 
 
-def same_to_all(part, size, axes):
-    return exchange(jnp.broadcast_to(part, (size,) + part.shape), axes)
-
-
 def per_device(latents, norm_gain, norm_shift, kernel, cotangent):
     lat = latents.reshape(T, ROWS, W)
     cot = cotangent.reshape(T, ROWS, W)
     gain, shift = norm_gain.reshape(1, C), norm_shift.reshape(1, C)
-    slab = ("zh", "core")
+    zh, zm, core = (lax.axis_index(axis) for axis in ("zh", "zm", "core"))
+    flags = jnp.stack([zh * 2 + core, core, zm]).astype(jnp.int32)
     halo = shape(HALO, ROWS, W, dtype=BF16)
     frames = pltpu.VMEM((T, ROWS, W), BF16)
     tmp = pltpu.VMEM((ROWS, W), F32)
+    row = pltpu.VMEM((1, C), F32)
     window_scratch = pltpu.VMEM((3 * ROWS, (T + HALO) * W), BF16)
     taps = pltpu.VMEM((3, ROWS, 3 * ROWS), BF16)
     kernel_scratch = pltpu.VMEM((27, C, C), BF16)
     scaled_scratch = pltpu.VMEM((T, ROWS, W), F32)
-    own, tail, head = call(
+    own, to_near, to_far = call(
         start_kernel,
         (shape(8, W), halo, halo),
-        [pltpu.VMEM((T - HALO, ROWS, W), BF16), sems(3)],
+        [frames, sems(2), sems(2)],
+        flags,
         lat,
         cot,
-        far=(0, 1),
+        far=(1, 2),
+        scalars=1,
     )
     blocks, adj, scales = call(
         prepare_kernel,
         (shape(T * H, C, W), shape(3 * C, T * H * W, dtype=BF16), shape(2, C, W)),
-        [frames, frames, tmp, sems(2)],
+        [frames, frames, row, row, tmp, sems(4)],
         lat,
         cot,
         gain,
         shift,
-        far=(0, 1),
-    )
-    pair = own + swap(own, "core")
-    totals = jnp.concatenate([pair, swap(pair, "zh")], axis=0)
-    previous = lax.ppermute(tail, slab, [(i, i + 1) for i in range(SLABS - 1)])
-    following = lax.ppermute(head, slab, [(i + 1, i) for i in range(SLABS - 1)])
-    zh, core = lax.axis_index("zh"), lax.axis_index("core")
-    flags = jnp.stack([zh * 2 + core, core]).astype(jnp.int32)
+        far=(0, 1, 2, 3),
+    )
+    far = lax.ppermute(to_far, ("zh", "core"), [(1, 2), (2, 1)])
+    across, blocks = lax.optimization_barrier((swap(own, "zh"), blocks))
+    pair = own + across
+    near = swap(to_near, "core")
+    totals = jnp.concatenate([pair, swap(pair, "core")], axis=0)
     window, keep, send = call(
         grad_kernel,
-        (shape(3 * ROWS, (T + HALO) * W, dtype=BF16), shape(COMM, C), shape(COMM, C)),
-        [tmp, pltpu.VMEM((3 * C, (T + HALO) * H * W), BF16), window_scratch, sems(1)],
+        (shape(3 * ROWS, T * W, dtype=BF16), shape(COMM, C), shape(COMM, C)),
+        [
+            tmp,
+            pltpu.VMEM((3 * C, T * H * W), BF16),
+            pltpu.VMEM((3 * C, HALO * H * W), BF16),
+            pltpu.VMEM((3 * ROWS, T * W), BF16),
+            sems(1),
+        ],
         flags,
         blocks,
-        previous,
+        near,
+        far,
         adj,
         totals,
         scales,
@@ -354,35 +407,41 @@
         back_kernel,
         (shape(T, ROWS, W), shape(8, W)),
         [tmp, window_scratch, taps, frames, frames, kernel_scratch, scaled_scratch, sems(3)],
+        flags,
         lat,
         cot,
-        following,
+        near,
+        far,
         kernel,
         totals,
         scales,
-        far=(0, 1, 3),
+        far=(1, 2, 5),
         out_far=(0,),
+        scalars=1,
         flops=4 * 10**9,
     )
     sums = sums + swap(sums, "core")
-    packed = call(part_kernel, shape(PART + 8, C), [], parts, sums)
-    over_z = same_to_all(packed, 4, ("zh", "zm"))
-    part = jnp.sum(over_z[:, :PART], axis=0).astype(BF16)
-    zm = lax.axis_index("zm")
-    backward = jnp.sum(
-        jnp.where(lax.broadcasted_iota(jnp.int32, (2, 2, 8, C), 1) == zm, over_z[:, PART:].reshape(2, 2, 8, C), 0.0),
-        axis=(0, 1),
+    packed = call(part_kernel, shape(4, PART + 8, C), [], parts, sums)
+    over_z = exchange(packed, ("zh", "zm"))
+    part, backward = call(
+        merge_kernel, (shape(SIDE, PART, C, dtype=BF16), shape(8, C)), [], flags, over_z, scalars=1
     )
     part, window = lax.optimization_barrier((part, window))
-    mine = same_to_all(part, SIDE, ("y", "zn", "x")).reshape(COMM, C)
+    mine = exchange(part, ("y", "zn", "x")).reshape(COMM, C)
     output = call(
         conv_kernel,
         shape(T, ROWS, W, dtype=BF16),
         [tmp, taps, frames, kernel_scratch, window_scratch, sems(3)],
+        flags,
         lat,
+        near,
+        far,
         kernel,
         window,
-        far=(0, 1, 2),
+        totals,
+        scales,
+        far=(1, 4, 5),
+        scalars=1,
         flops=4 * 10**9,
     )
     mine, output = lax.optimization_barrier((mine, output))

time: 99.6 us -> 89.2 us (0.90)
  waiting for transfers between devices: 25.9 us -> 17.7 us
  starting transfers between devices: 33.8 us -> 29.2 us
  Pallas kernels: 24.5 us -> 27.5 us
  local copies, waits for them, and re-layouts: 2.24 us -> 0 us
  blocking collectives: 11.7 us -> 13.6 us
    ppermute x2 -> x1, waiting for transfers between devices: 14.9 us -> 0.01 us  [per_device(): far = lax.ppermute(to_far, ('zh', 'core'), [(1, 2), (2, 1)])]
    ppermute x2 -> x1, starting transfers between devices: 12.8 us -> 6.98 us  [per_device(): far = lax.ppermute(to_far, ('zh', 'core'), [(1, 2), (2, 1)])]
    all_to_all x2, waiting for transfers between devices: 3.26 us -> 8.64 us  [exchange(): return lax.all_to_all(parts, axes, 0, 0)]
    ppermute x5 -> x6, starting transfers between devices: 4.35 us -> 8.72 us  [swap(): return lax.ppermute(value, axis, [(0, 1), (1, 0)])]
    all_to_all x2, starting transfers between devices: 16.6 us -> 13.5 us  [exchange(): return lax.all_to_all(parts, axes, 0, 0)]
    pallas_call x9 -> x10, Pallas kernels: 24.5 us -> 27.5 us  [call(): pl.pallas_call(body, out_shape=shapes[0] if single else shapes, in_specs=...]
    all_to_all x1, blocking collectives: 11.7 us -> 13.6 us  [exchange(): return lax.all_to_all(parts, axes, 0, 0)]
    unnamed x4 -> x0, local copies, waits for them, and re-layouts: 1.31 us -> none
  transfers between devices with their start and end apart: 9 -> 9, of which waited for: 6 -> 6; matrix products, arithmetic and copies ran while one was open for 0% -> 0% of each run, Pallas kernels for 16% -> 19%
where the time goes in v3:
time: 89.2 us; the launch traced here: 88.8 us
  starting transfers between devices  29.2 us (33%)
  Pallas kernels  27.5 us (31%)
  waiting for transfers between devices  17.7 us (20%)
  blocking collectives  13.6 us (15%)
    pallas_call x10, Pallas kernels, call(): pl.pallas_call(body, out_shape=shapes[0] if single else shapes, in_specs=...  27.5 us
    all_to_all x1, blocking collectives, exchange(): return lax.all_to_all(parts, axes, 0, 0)  13.6 us
    all_to_all x2, starting transfers between devices, exchange(): return lax.all_to_all(parts, axes, 0, 0)  13.5 us
    ppermute x6, waiting for transfers between devices, swap(): return lax.ppermute(value, axis, [(0, 1), (1, 0)])  9.04 us
    ppermute x6, starting transfers between devices, swap(): return lax.ppermute(value, axis, [(0, 1), (1, 0)])  8.72 us
    all_to_all x2, waiting for transfers between devices, exchange(): return lax.all_to_all(parts, axes, 0, 0)  8.64 us
    ppermute x1, starting transfers between devices, per_device(): far = lax.ppermute(to_far, ('zh', 'core'), [(1, 2), (2, 1)])  6.98 us
  transfers between devices with their start and end apart: 9, of which 6 were waited for; matrix products, arithmetic and copies ran while one was open for 0% of the time, Pallas kernels for 19%

profile of v3, /device:TPU:1, one launch (start us, length us, event | category | flops | bytes accessed | tf_op | source)
XLA Modules:
  0.0 88.8 jit_solution(13120708472100701930)
XLA Ops:
  0.6 0.1 pad_add_fusion.flags
  0.7 2.0 %shard_map.76 = (f32[8,128]{1,0:T(8,128)S(1)}, bf16[2,512,128]{2,1,0:T(8,128)(2,1)S(1)}, bf16[2,512,128]{2,1,0:T(8,128)(2,1)S(1)}) custom-call(s32[3]{0:T(128)S(1)} %pad_add_fusion.flags, bf16[4,512,128]{2,1,0:T(8,128)(2,1)} %bitcast.13, bf16[4,512,128]{2,1,0:T(8,128)(2,1)} %bitcast.18), custom_call_target="tpu_custom_call" | custom-call | bytes 1048576 | tf_op jit(solution)/shard_map/pallas_call | solution.py:317
  2.7 3.3 %collective-permute-start.1 = (bf16[2,512,128]{2,1,0:T(8,128)(2,1)S(1)}, bf16[2,512,128]{2,1,0:T(8,128)(2,1)S(1)}, u32[]{:S(2)}, u32[]{:S(2)}) collective-permute-start(bf16[2,512,128]{2,1,0:T(8,128)(2,1)S(1)} %get-tuple-element.25), channel_id=1, source_target_pairs={{0,64},{64,0},{1,65},{65,1},{2,66},{66,2},{3,67},{67,3},{4,68},{68... | collective-permute-start | bytes 786440 | tf_op jit(solution)/shard_map/ppermute | solution.py:337
  6.0 7.0 %collective-permute-start.2 = (bf16[2,512,128]{2,1,0:T(8,128)(2,1)S(1)}, bf16[2,512,128]{2,1,0:T(8,128)(2,1)S(1)}, u32[]{:S(2)}, u32[]{:S(2)}) collective-permute-start(bf16[2,512,128]{2,1,0:T(8,128)(2,1)S(1)} %get-tuple-element.26), channel_id=1, source_target_pairs={{64,128},{128,64},{65,129},{129,65},{66,130},{130,66},{67,131},{13... | collective-permute-start | bytes 786440 | tf_op jit(solution)/shard_map/ppermute | solution.py:378
  13.0 0.1 collective-permute-start
  13.1 1.7 %shard_map.77 = (f32[16,128,128]{2,1,0:T(8,128)S(1)}, bf16[384,2048]{1,0:T(8,128)(2,1)S(1)}, f32[2,128,128]{2,1,0:T(8,128)S(1)}) custom-call(bf16[4,512,128]{2,1,0:T(8,128)(2,1)} %bitcast.14, bf16[4,512,128]{2,1,0:T(8,128)(2,1)} %bitcast.19, f32[1,128]{1,0:T(1,128)} %bitcast.22, f32[1,128]{1,0:T(1,128)} %bitcast.23), custom_call_target="tpu_custom_call" | custom-call | bytes 1048576 | tf_op jit(solution)/shard_map/pallas_call | solution.py:317
  14.8 4.7 %collective-permute-done = f32[8,128]{1,0:T(8,128)S(1)} collective-permute-done((f32[8,128]{1,0:T(8,128)S(1)}, f32[8,128]{1,0:T(8,128)S(1)}, u32[]{:S(2)}, u32[]{:S(2)}) %collective-permute-start) | collective-permute-done | bytes 4128 | tf_op jit(solution)/shard_map/ppermute | solution.py:337
  19.6 0.0 collective-permute-start.3
  19.6 1.2 %collective-permute-done.3 = f32[8,128]{1,0:T(8,128)S(1)} collective-permute-done((f32[8,128]{1,0:T(8,128)S(1)}, f32[8,128]{1,0:T(8,128)S(1)}, u32[]{:S(2)}, u32[]{:S(2)}) %collective-permute-start.3) | collective-permute-done | bytes 4128 | tf_op jit(solution)/shard_map/ppermute | solution.py:337
  20.8 0.0 collective-permute-done.1.near
  20.8 0.0 collective-permute-done.2.far
  20.8 3.9 %shard_map.78 = (bf16[1536,512]{1,0:T(8,128)(2,1)}, f32[1792,128]{1,0:T(8,128)S(1)}, f32[1792,128]{1,0:T(8,128)S(1)}) custom-call(s32[3]{0:T(128)S(1)} %pad_add_fusion.flags, f32[16,128,128]{2,1,0:T(8,128)S(1)} %get-tuple-element.24.blocks, bf16[2,512,128]{2,1,0:T(8,128)(2,1)S(1)} %collective-permute-done.1.near, ...), custom_call_target="tpu_custom_call" | custom-call | flops 4000000000 | bytes 1048576 | tf_op jit(solution)/shard_map/pallas_call | solution.py:317
  24.6 0.3 collective-permute-start.4
  24.9 2.3 %collective-permute-done.4.received = f32[1792,128]{1,0:T(8,128)S(1)} collective-permute-done((f32[1792,128]{1,0:T(8,128)S(1)}, f32[1792,128]{1,0:T(8,128)S(1)}, u32[]{:S(2)}, u32[]{:S(2)}) %collective-permute-start.4) | collective-permute-done | bytes 917536 | tf_op jit(solution)/shard_map/ppermute | solution.py:337
  27.2 1.1 %shard_map.79 = f32[1792,128]{1,0:T(8,128)} custom-call(f32[1792,128]{1,0:T(8,128)S(1)} %get-tuple-element.30.keep, f32[1792,128]{1,0:T(8,128)S(1)} %collective-permute-done.4.received), custom_call_target="tpu_custom_call" | custom-call | bytes 1048576 | tf_op jit(solution)/shard_map/pallas_call | solution.py:317
  28.3 8.0 %all-to-all-start = ((f32[32,56,128]{2,1,0:T(8,128)}), f32[32,56,128]{2,1,0:T(8,128)S(1)}, u32[]{:S(2)}, u32[]{:S(2)}) async-start(f32[32,56,128]{2,1,0:T(8,128)} %bitcast.7), calls=%async_computation | async-start | bytes 1835008 | tf_op jit(solution)/shard_map/all_to_all | solution.py:341
  36.3 6.9 %shard_map.80 = (f32[4,512,128]{2,1,0:T(8,128)}, f32[8,128]{1,0:T(8,128)S(1)}) custom-call(s32[3]{0:T(128)S(1)} %pad_add_fusion.flags, bf16[4,512,128]{2,1,0:T(8,128)(2,1)} %bitcast.15, bf16[4,512,128]{2,1,0:T(8,128)(2,1)} %bitcast.20, bf16[2,512,128]{2,1,0:T(8,128)(2,1)S(1)} %collective-permute-done.1.near, ...), custom_call_target="tpu_custom_call" | custom-call | flops 4000000000 | bytes 1048576 | tf_op jit(solution)/shard_map/pallas_call | solution.py:317
  43.2 0.7 collective-permute-start.5
  43.9 0.8 collective-permute-done.5
  44.8 6.0 %all-to-all-done.parts = f32[32,56,128]{2,1,0:T(8,128)S(1)} async-done(((f32[32,56,128]{2,1,0:T(8,128)}), f32[32,56,128]{2,1,0:T(8,128)S(1)}, u32[]{:S(2)}, u32[]{:S(2)}) %all-to-all-start) | async-done | bytes 917536 | tf_op jit(solution)/shard_map/all_to_all | solution.py:341
  50.7 0.1 shard_map.81
  50.8 13.6 %all_to_all.15.over_z = f32[4,64,128]{2,1,0:T(8,128)S(1)} all-to-all(f32[4,64,128]{2,1,0:T(8,128)S(1)} %shard_map.81), channel_id=1, replica_groups=mesh['zh'=2,'core'=2,'y'=4,'zm'=2,'zn'=2,'x'=4] {'zh','zm'}, dimensions={0} | all-to-all | bytes 262144 | tf_op jit(solution)/shard_map/all_to_all | solution.py:341
  64.3 1.3 %shard_map.82 = (bf16[32,56,128]{2,1,0:T(8,128)(2,1)}, f32[8,128]{1,0:T(8,128)S(1)}) custom-call(s32[3]{0:T(128)S(1)} %pad_add_fusion.flags, f32[4,64,128]{2,1,0:T(8,128)S(1)} %all_to_all.15.over_z), custom_call_target="tpu_custom_call" | custom-call | bytes 1048576 | tf_op jit(solution)/shard_map/pallas_call | solution.py:317
  65.7 5.5 %all-to-all-start.2 = ((bf16[32,56,128]{2,1,0:T(8,128)(2,1)}), bf16[32,56,128]{2,1,0:T(8,128)(2,1)S(1)}, u32[]{:S(2)}, u32[]{:S(2)}) async-start(bf16[32,56,128]{2,1,0:T(8,128)(2,1)} %get-tuple-element.35), calls=%async_computation.2 | async-start | bytes 917504 | tf_op jit(solution)/shard_map/all_to_all | solution.py:341
  71.2 5.9 %shard_map.83 = bf16[4,512,128]{2,1,0:T(8,128)(2,1)} custom-call(s32[3]{0:T(128)S(1)} %pad_add_fusion.flags, bf16[4,512,128]{2,1,0:T(8,128)(2,1)} %bitcast.16, bf16[2,512,128]{2,1,0:T(8,128)(2,1)S(1)} %collective-permute-done.1.near, bf16[2,512,128]{2,1,0:T(8,128)(2,1)S(1)} %collective-permute-done.2.far, bf16[27,128,128]{2,1,0:T(8,128)(2,1)} %kernel.3, ...), custom_call_target="tpu_custom_call" | custom-call | flops 4000000000 | bytes 1048576 | tf_op jit(solution)/shard_map/pallas_call | solution.py:317
  77.0 2.7 %all-to-all-done.2 = bf16[32,56,128]{2,1,0:T(8,128)(2,1)S(1)} async-done(((bf16[32,56,128]{2,1,0:T(8,128)(2,1)}), bf16[32,56,128]{2,1,0:T(8,128)(2,1)S(1)}, u32[]{:S(2)}, u32[]{:S(2)}) %all-to-all-start.2) | async-done | bytes 458784 | tf_op jit(solution)/shard_map/all_to_all | solution.py:341
  79.7 4.3 %collective-permute-start.6 = (bf16[1792,128]{1,0:T(8,128)(2,1)S(1)}, bf16[1792,128]{1,0:T(8,128)(2,1)S(1)}, u32[]{:S(2)}, u32[]{:S(2)}) collective-permute-start(bf16[1792,128]{1,0:T(8,128)(2,1)S(1)} %bitcast.11), channel_id=1, source_target_pairs={{0,64},{64,0},{1,65},{65,1},{2,66},{66,2},{3,67},{67,3},{4,68},{68... | collective-permute-start | bytes 1376264 | tf_op jit(solution)/shard_map/ppermute | solution.py:337
  84.1 2.8 %shard_map.84 = bf16[4,512,128]{2,1,0:T(8,128)(2,1)} custom-call(bf16[4,512,128]{2,1,0:T(8,128)(2,1)} %bitcast.17, bf16[4,512,128]{2,1,0:T(8,128)(2,1)} %bitcast.21, f32[16,128]{1,0:T(8,128)S(1)} %pad_maximum_fusion.totals, f32[8,128]{1,0:T(8,128)S(1)} %get-tuple-element.38.backward, f32[4,512,128]{2,1,0:T(8,128)} %get-tuple-element.39.scaled), custom_call_target="tpu_custom_call" | custom-call | flops 1000000000 | bytes 1048576 | tf_op jit(solution)/shard_map/pallas_call | solution.py:317
  86.9 0.0 collective-permute-done.6.other
  86.9 1.9 %shard_map.85 = f32[27,128,128]{2,1,0:T(8,128)} custom-call(s32[3]{0:T(128)S(1)} %pad_add_fusion.flags, bf16[1792,128]{1,0:T(8,128)(2,1)S(1)} %bitcast.12, bf16[1792,128]{1,0:T(8,128)(2,1)S(1)} %collective-permute-done.6.other), custom_call_target="tpu_custom_call" | custom-call | bytes 1048576 | tf_op jit(solution)/shard_map/pallas_call | solution.py:317
  (3 shorter events, 0.0 us)
Async XLA Ops:
  2.7 18.1 %collective-permute-start.1 = (bf16[2,512,128]{2,1,0:T(8,128)(2,1)S(1)}, bf16[2,512,128]{2,1,0:T(8,128)(2,1)S(1)}, u32[]{:S(2)}, u32[]{:S(2)}) collective-permute-start(bf16[2,512,128]{2,1,0:T(8,128)(2,1)S(1)} %get-tuple-element.25), channel_id=1, source_target_pairs={{0,64},{64,0},{1,65},{65,1},{2,66},{66,2},{3,67},{67,3},{4,68},{68... | collective-permute-start | bytes 786440 | tf_op jit(solution)/shard_map/ppermute | solution.py:337
  6.0 14.7 %collective-permute-start.2 = (bf16[2,512,128]{2,1,0:T(8,128)(2,1)S(1)}, bf16[2,512,128]{2,1,0:T(8,128)(2,1)S(1)}, u32[]{:S(2)}, u32[]{:S(2)}) collective-permute-start(bf16[2,512,128]{2,1,0:T(8,128)(2,1)S(1)} %get-tuple-element.26), channel_id=1, source_target_pairs={{64,128},{128,64},{65,129},{129,65},{66,130},{130,66},{67,131},{13... | collective-permute-start | bytes 786440 | tf_op jit(solution)/shard_map/ppermute | solution.py:378
  13.0 6.6 %collective-permute-start = (f32[8,128]{1,0:T(8,128)S(1)}, f32[8,128]{1,0:T(8,128)S(1)}, u32[]{:S(2)}, u32[]{:S(2)}) collective-permute-start(f32[8,128]{1,0:T(8,128)S(1)} %get-tuple-element.22), channel_id=1, source_target_pairs={{0,128},{128,0},{1,129},{129,1},{2,130},{130,2},{3,131},{131,3},{4... | collective-permute-start | bytes 12296 | tf_op jit(solution)/shard_map/ppermute | solution.py:337
  19.6 1.2 %collective-permute-start.3 = (f32[8,128]{1,0:T(8,128)S(1)}, f32[8,128]{1,0:T(8,128)S(1)}, u32[]{:S(2)}, u32[]{:S(2)}) collective-permute-start(f32[8,128]{1,0:T(8,128)S(1)} %add.10), channel_id=1, source_target_pairs={{0,64},{64,0},{1,65},{65,1},{2,66},{66,2},{3,67},{67,3},{4,68},{68... | collective-permute-start | bytes 12296 | tf_op jit(solution)/shard_map/ppermute | solution.py:337
  24.6 2.6 %collective-permute-start.4 = (f32[1792,128]{1,0:T(8,128)S(1)}, f32[1792,128]{1,0:T(8,128)S(1)}, u32[]{:S(2)}, u32[]{:S(2)}) collective-permute-start(f32[1792,128]{1,0:T(8,128)S(1)} %get-tuple-element.31), channel_id=1, source_target_pairs={{0,64},{64,0},{1,65},{65,1},{2,66},{66,2},{3,67},{67,3},{4,68},{68... | collective-permute-start | bytes 2752520 | tf_op jit(solution)/shard_map/ppermute | solution.py:337
  28.3 22.4 %all-to-all-start = ((f32[32,56,128]{2,1,0:T(8,128)}), f32[32,56,128]{2,1,0:T(8,128)S(1)}, u32[]{:S(2)}, u32[]{:S(2)}) async-start(f32[32,56,128]{2,1,0:T(8,128)} %bitcast.7), calls=%async_computation | async-start | bytes 1835008 | tf_op jit(solution)/shard_map/all_to_all | solution.py:341
  43.2 1.5 %collective-permute-start.5 = (f32[8,128]{1,0:T(8,128)S(1)}, f32[8,128]{1,0:T(8,128)S(1)}, u32[]{:S(2)}, u32[]{:S(2)}) collective-permute-start(f32[8,128]{1,0:T(8,128)S(1)} %get-tuple-element.32), channel_id=1, source_target_pairs={{0,64},{64,0},{1,65},{65,1},{2,66},{66,2},{3,67},{67,3},{4,68},{68... | collective-permute-start | bytes 12296 | tf_op jit(solution)/shard_map/ppermute | solution.py:337
  65.7 14.0 %all-to-all-start.2 = ((bf16[32,56,128]{2,1,0:T(8,128)(2,1)}), bf16[32,56,128]{2,1,0:T(8,128)(2,1)S(1)}, u32[]{:S(2)}, u32[]{:S(2)}) async-start(bf16[32,56,128]{2,1,0:T(8,128)(2,1)} %get-tuple-element.35), calls=%async_computation.2 | async-start | bytes 917504 | tf_op jit(solution)/shard_map/all_to_all | solution.py:341
  79.7 7.2 %collective-permute-start.6 = (bf16[1792,128]{1,0:T(8,128)(2,1)S(1)}, bf16[1792,128]{1,0:T(8,128)(2,1)S(1)}, u32[]{:S(2)}, u32[]{:S(2)}) collective-permute-start(bf16[1792,128]{1,0:T(8,128)(2,1)S(1)} %bitcast.11), channel_id=1, source_target_pairs={{0,64},{64,0},{1,65},{65,1},{2,66},{66,2},{3,67},{67,3},{4,68},{68... | collective-permute-start | bytes 1376264 | tf_op jit(solution)/shard_map/ppermute | solution.py:337

commit v4 on v3

--- a/solution.py
+++ b/solution.py
@@ -24,7 +24,7 @@
 PART = COMM // SIDE
 F32 = jnp.float32
 BF16 = jnp.bfloat16
-LIMIT = pltpu.CompilerParams(vmem_limit_bytes=24 * 1024 * 1024)
+MIB = 1024 * 1024
 
 
 def lanes():
@@ -71,23 +71,12 @@
     return started
 
 
-def start_kernel(flags, lat, cot, sums, near, far, lat_v, sem, halo_sem):
-    tail, head = lat.at[T - HALO :], cot.at[:HALO]
-
-    @pl.when(flags[1] == 0)
-    def _():
-        copies(halo_sem, (tail, near), (head, far))
-
-    @pl.when(flags[1] != 0)
-    def _():
-        copies(halo_sem, (head, near), (tail, far))
-
-    parts = copies(sem, (lat.at[: T // 2], lat_v.at[: T // 2]), (lat.at[T // 2 :], lat_v.at[T // 2 :]))
+def start_kernel(lat, sums, lat_v, sem):
+    parts = copies(sem, *((lat.at[t], lat_v.at[t]) for t in range(T)))
     total = jnp.zeros((ROWS, W), F32)
     square = jnp.zeros((ROWS, W), F32)
     for t in range(T):
-        if t % (T // 2) == 0:
-            parts[t // (T // 2)].wait()
+        parts[t].wait()
         x = lat_v[t].astype(F32)
         total = total + x
         square = square + x * x
@@ -95,8 +84,6 @@
     square = jnp.sum(jnp.sum(square.reshape(GROUPS, -1, W), axis=1), axis=1, keepdims=True)
     row = row_of(total, 0) + row_of(square, GROUPS)
     sums[...] = jnp.broadcast_to(row, (8, W))
-    pltpu.make_async_copy(tail, near, halo_sem.at[0]).wait()
-    pltpu.make_async_copy(head, far, halo_sem.at[1]).wait()
 
 
 def put_adjoint(adj, f, mine):
@@ -108,12 +95,20 @@
             adj[ki * C : (ki + 1) * C, (f * H + h) * W : (f * H + h + 1) * W] = block
 
 
-def prepare_kernel(lat, cot, gain, shift, blocks, adj, scales, lat_v, cot_v, gain_v, shift_v, tmp, sem):
-    from_lat, from_cot, *small = copies(sem, (lat, lat_v), (cot, cot_v), (gain, gain_v), (shift, shift_v))
+def prepare_kernel(lat, cot, gain, shift, adj, scales, head, tail, lat_v, cot_v, gain_v, shift_v, tmp, sem):
+    from_lat, from_cot, *small = copies(
+        sem,
+        (lat, lat_v),
+        (cot, cot_v),
+        (gain, gain_v),
+        (shift, shift_v),
+        (cot.at[:HALO], head),
+        (lat.at[T - HALO :], tail),
+    )
     from_lat.wait()
     for t in range(T):
         for h, block in enumerate(by_row(lat_v[t], tmp)):
-            blocks[t * H + h] = block
+            adj[3 * C :, (t * H + h) * W : (t * H + h + 1) * W] = block.astype(BF16)
     from_cot.wait()
     for t in range(T):
         put_adjoint(adj, t, by_row(cot_v[t], tmp))
@@ -128,17 +123,13 @@
     return [tmp[pl.ds(h, C, stride=H), :] for h in range(H)]
 
 
-def pick(condition, first, second):
-    return jnp.where(condition, first.astype(F32), second.astype(F32))
-
-
 def back_kernel(
-    flags, lat, cot, near, far, kernel, totals, scales, scaled, sums, tmp, window, taps, lat_v, cot_v, kernel_v, scaled_v, sem
+    lat, cot, following, kernel, totals, scales, scaled, sums, tmp, window, taps, lat_v, cot_v, kernel_v, scaled_v, sem
 ):
     from_cot, from_kernel, from_lat = copies(sem, (cot, cot_v), (kernel, kernel_v), (lat, lat_v))
     from_cot.wait()
     for f in range(T + HALO):
-        blocks = by_row(cot_v[f] if f < T else pick(flags[1] == 0, near[f - T], far[f - T]), tmp)
+        blocks = by_row(cot_v[f] if f < T else following[f - T], tmp)
         for h in range(H):
             for s, moved in enumerate(shifted(blocks[h])):
                 at = (s * H + h) * C
@@ -185,41 +176,59 @@
     return (normed * (1.0 / (1.0 + jnp.exp(-normed)))).astype(BF16).astype(F32)
 
 
-def grad_kernel(flags, blocks, near, far, adj, totals, scales, window, keep, send, tmp, flat, adj_v, window_v, sem):
-    core = flags[1]
+CONTRACT = (((1,), (1,)), ((), ()))
+PLANE = H * W
+
+
+def halves(core, grads):
+    half = C // 2
+    for ki in range(3):
+        for kj in range(3):
+            tap = grads[ki * C : (ki + 1) * C, kj * C : (kj + 1) * C]
+            low, high = tap[:half], tap[half:]
+            at = (3 * ki + kj) * half
+            yield at, jnp.where(core == 0, low, high), jnp.where(core == 0, high, low)
+
+
+def grad_kernel(flags, adj, totals, scales, window, keep, send, last, flat, window_v, sem):
     center, inverse = center_inverse(totals, PER)
-    for f in range(HALO):
-        put_adjoint(adj_v, f, by_row(pick(core == 0, near[f], far[f]), tmp))
     for t in range(T):
         for h in range(H):
-            for s, moved in enumerate(shifted(activated(blocks[t * H + h], center, inverse, scales))):
+            block = adj[3 * C :, (t * H + h) * W : (t * H + h + 1) * W].astype(F32)
+            for s, moved in enumerate(shifted(activated(block, center, inverse, scales))):
                 moved = moved.astype(BF16)
                 window_v[(s * H + h) * C : (s * H + h + 1) * C, t * W : (t + 1) * W] = moved
                 flat[s * C : (s + 1) * C, (t * H + h) * W : (t * H + h + 1) * W] = moved
+                if t >= T - HALO:
+                    at = ((t - T + HALO) * H + h) * W
+                    last[s * C : (s + 1) * C, at : at + W] = moved
     (to_window,) = copies(sem, (window_v, window))
-    contract = (((1,), (1,)), ((), ()))
-    plane = H * W
-    half = C // 2
     for kt in range(3):
         ahead = 2 - kt
-        own = T - ahead
         grads = lax.dot_general(
-            adj[:, ahead * plane :], flat[:, : own * plane], contract, preferred_element_type=F32
+            adj[: 3 * C, ahead * PLANE :], flat[:, : (T - ahead) * PLANE], CONTRACT, preferred_element_type=F32
         )
-        if ahead:
-            grads = grads + lax.dot_general(
-                adj_v[:, : ahead * plane], flat[:, own * plane :], contract, preferred_element_type=F32
-            )
-        for ki in range(3):
-            for kj in range(3):
-                tap = grads[ki * C : (ki + 1) * C, kj * C : (kj + 1) * C]
-                low, high = tap[:half], tap[half:]
-                at = (9 * kt + 3 * ki + kj) * half
-                keep[at : at + half] = jnp.where(core == 0, low, high)
-                send[at : at + half] = jnp.where(core == 0, high, low)
+        for at, mine, other in halves(flags[1], grads):
+            at += 9 * kt * (C // 2)
+            keep[at : at + C // 2] = mine
+            send[at : at + C // 2] = other
     keep[HALF:] = jnp.zeros((COMM - HALF, C), F32)
     send[HALF:] = jnp.zeros((COMM - HALF, C), F32)
     to_window.wait()
+
+
+def edge_kernel(flags, keep_in, send_in, following, last, keep, send, tmp, adj):
+    for f in range(HALO):
+        put_adjoint(adj, f, by_row(following[f], tmp))
+    for kt in range(2):
+        ahead = 2 - kt
+        grads = lax.dot_general(
+            adj[:, : ahead * PLANE], last[:, (HALO - ahead) * PLANE :], CONTRACT, preferred_element_type=F32
+        )
+        for at, mine, other in halves(flags[1], grads):
+            at += 9 * kt * (C // 2)
+            keep[at : at + C // 2] = keep_in[at : at + C // 2] + mine
+            send[at : at + C // 2] = send_in[at : at + C // 2] + other
 
 
 def add_kernel(keep, received, chip):
@@ -253,14 +262,14 @@
 
 
 def conv_kernel(
-    flags, lat, near, far, kernel, window, totals, scales, output, tmp, taps, lat_v, kernel_v, window_v, sem
+    flags, lat, previous, kernel, window, totals, scales, output, tmp, taps, lat_v, kernel_v, window_v, sem
 ):
     from_kernel, from_window, from_lat = copies(
         sem, (kernel, kernel_v), (window, window_v.at[:, HALO * W :]), (lat, lat_v)
     )
     center, inverse = center_inverse(totals, PER)
     for f in range(HALO):
-        blocks = by_row(pick(flags[1] == 0, far[f], near[f]), tmp)
+        blocks = by_row(previous[f], tmp)
         for h in range(H):
             active = jnp.where(flags[0] > 0, activated(blocks[h], center, inverse, scales), 0.0)
             for s, moved in enumerate(shifted(active)):
@@ -308,7 +317,7 @@
 )
 
 
-def call(body, out, scratch, *operands, far=(), out_far=(), scalars=0, flops=0, moved=1 << 20):
+def call(body, out, scratch, *operands, far=(), out_far=(), scalars=0, flops=0, moved=1 << 20, aliases=(), limit=12):
     single = not isinstance(out, tuple)
     count = 1 if single else len(out)
     outs = tuple(HBM if i in out_far else VMEM for i in range(count))
@@ -320,7 +329,8 @@
         in_specs=[SMEM if i < scalars else HBM if i in far else VMEM for i in range(len(operands))],
         out_specs=outs[0] if single else outs,
         scratch_shapes=scratch,
-        compiler_params=LIMIT,
+        compiler_params=pltpu.CompilerParams(vmem_limit_bytes=limit * MIB),
+        input_output_aliases=dict(aliases),
         cost_estimate=pl.CostEstimate(flops=flops, bytes_accessed=moved, transcendentals=0),
     )(*operands)
 
@@ -347,6 +357,7 @@
     gain, shift = norm_gain.reshape(1, C), norm_shift.reshape(1, C)
     zh, zm, core = (lax.axis_index(axis) for axis in ("zh", "zm", "core"))
     flags = jnp.stack([zh * 2 + core, core, zm]).astype(jnp.int32)
+    slab = ("zh", "core")
     halo = shape(HALO, ROWS, W, dtype=BF16)
     frames = pltpu.VMEM((T, ROWS, W), BF16)
     tmp = pltpu.VMEM((ROWS, W), F32)
@@ -355,45 +366,32 @@
     taps = pltpu.VMEM((3, ROWS, 3 * ROWS), BF16)
     kernel_scratch = pltpu.VMEM((27, C, C), BF16)
     scaled_scratch = pltpu.VMEM((T, ROWS, W), F32)
-    own, to_near, to_far = call(
-        start_kernel,
-        (shape(8, W), halo, halo),
-        [frames, sems(2), sems(2)],
-        flags,
-        lat,
-        cot,
-        far=(1, 2),
-        scalars=1,
-    )
-    blocks, adj, scales = call(
+    own = call(start_kernel, shape(8, W), [frames, sems(T)], lat, far=(0,))
+    adj, scales, head, tail = call(
         prepare_kernel,
-        (shape(T * H, C, W), shape(3 * C, T * H * W, dtype=BF16), shape(2, C, W)),
-        [frames, frames, row, row, tmp, sems(4)],
+        (shape(4 * C, T * PLANE, dtype=BF16), shape(2, C, W), halo, halo),
+        [frames, frames, row, row, tmp, sems(6)],
         lat,
         cot,
         gain,
         shift,
         far=(0, 1, 2, 3),
-    )
-    far = lax.ppermute(to_far, ("zh", "core"), [(1, 2), (2, 1)])
-    across, blocks = lax.optimization_barrier((swap(own, "zh"), blocks))
+        out_far=(3,),
+    )
+    across, scales = lax.optimization_barrier((swap(own, "zh"), scales))
     pair = own + across
-    near = swap(to_near, "core")
+    following = lax.ppermute(head, slab, [(i + 1, i) for i in range(SLABS - 1)])
     totals = jnp.concatenate([pair, swap(pair, "core")], axis=0)
-    window, keep, send = call(
+    window, keep, send, last = call(
         grad_kernel,
-        (shape(3 * ROWS, T * W, dtype=BF16), shape(COMM, C), shape(COMM, C)),
-        [
-            tmp,
-            pltpu.VMEM((3 * C, T * H * W), BF16),
-            pltpu.VMEM((3 * C, HALO * H * W), BF16),
-            pltpu.VMEM((3 * ROWS, T * W), BF16),
-            sems(1),
-        ],
+        (
+            shape(3 * ROWS, T * W, dtype=BF16),
+            shape(COMM, C),
+            shape(COMM, C),
+            shape(3 * C, HALO * PLANE, dtype=BF16),
+        ),
+        [pltpu.VMEM((3 * C, T * PLANE), BF16), pltpu.VMEM((3 * ROWS, T * W), BF16), sems(1)],
         flags,
-        blocks,
-        near,
-        far,
         adj,
         totals,
         scales,
@@ -401,28 +399,41 @@
         scalars=1,
         flops=4 * 10**9,
     )
+    following, last = lax.optimization_barrier((following, last))
+    keep, send = call(
+        edge_kernel,
+        (shape(COMM, C), shape(COMM, C)),
+        [tmp, pltpu.VMEM((3 * C, HALO * PLANE), BF16)],
+        flags,
+        keep,
+        send,
+        following,
+        last,
+        scalars=1,
+        aliases=((1, 0), (2, 1)),
+    )
     chip = call(add_kernel, shape(COMM, C, dtype=WIRE), [], keep, swap(send, "core"))
     parts = exchange(chip.reshape(SIDE, PART, C), ("y", "zn", "x"))
     scaled, sums = call(
         back_kernel,
         (shape(T, ROWS, W), shape(8, W)),
         [tmp, window_scratch, taps, frames, frames, kernel_scratch, scaled_scratch, sems(3)],
-        flags,
         lat,
         cot,
-        near,
-        far,
+        following,
         kernel,
         totals,
         scales,
-        far=(1, 2, 5),
+        far=(0, 1, 3),
         out_far=(0,),
-        scalars=1,
+        limit=20,
         flops=4 * 10**9,
     )
+    sums, tail = lax.optimization_barrier((sums, tail))
+    previous = lax.ppermute(tail, slab, [(i, i + 1) for i in range(SLABS - 1)])
     sums = sums + swap(sums, "core")
     packed = call(part_kernel, shape(4, PART + 8, C), [], parts, sums)
-    over_z = exchange(packed, ("zh", "zm"))
+    over_z, previous = lax.optimization_barrier((exchange(packed, ("zh", "zm")), previous))
     part, backward = call(
         merge_kernel, (shape(SIDE, PART, C, dtype=BF16), shape(8, C)), [], flags, over_z, scalars=1
     )
@@ -434,13 +445,13 @@
         [tmp, taps, frames, kernel_scratch, window_scratch, sems(3)],
         flags,
         lat,
-        near,
-        far,
+        previous,
         kernel,
         window,
         totals,
         scales,
-        far=(1, 4, 5),
+        far=(1, 3, 4),
+        limit=20,
         scalars=1,
         flops=4 * 10**9,
     )

time: 89.2 us -> 99.3 us (1.11)
  blocking collectives: 13.6 us -> 0 us
  starting transfers between devices: 29.2 us -> 39.3 us
  Pallas kernels: 27.5 us -> 35.2 us
  waiting for transfers between devices: 17.7 us -> 23.4 us
    all_to_all x1 -> x0, blocking collectives: 13.6 us -> none  [exchange(): return lax.all_to_all(parts, axes, 0, 0)]
    pallas_call x10 -> x11, Pallas kernels: 27.5 us -> 35.2 us  [call(): pl.pallas_call(body, out_shape=shapes[0] if single else shapes, in_specs=...]
    ppermute x6 -> x5, starting transfers between devices: 8.72 us -> 15.4 us  [swap(): return lax.ppermute(value, axis, [(0, 1), (1, 0)])]
    all_to_all x2 -> x3, waiting for transfers between devices: 8.64 us -> 14.6 us  [exchange(): return lax.all_to_all(parts, axes, 0, 0)]
    all_to_all x2 -> x3, starting transfers between devices: 13.5 us -> 19 us  [exchange(): return lax.all_to_all(parts, axes, 0, 0)]
    ppermute x6 -> x5, waiting for transfers between devices: 9.04 us -> 4.45 us  [swap(): return lax.ppermute(value, axis, [(0, 1), (1, 0)])]
    ppermute x1 -> x2, waiting for transfers between devices: 0.01 us -> 4.36 us  [the longest x1 4.35 us: per_device(): following = lax.ppermute(head, slab, [(i + 1, i) for i in range(SLABS - 1)])]
    ppermute x1 -> x2, starting transfers between devices: 6.98 us -> 4.89 us  [the longest x1 2.86 us: per_device(): following = lax.ppermute(head, slab, [(i + 1, i) for i in range(SLABS - 1)])]
  transfers between devices with their start and end apart: 9 -> 10, of which waited for: 6 -> 7; matrix products, arithmetic and copies ran while one was open for 0% -> 0% of each run, Pallas kernels for 19% -> 28%
where the time goes in v4:
time: 99.3 us; the launch traced here: 98.8 us
  starting transfers between devices  39.3 us (40%)
  Pallas kernels  35.2 us (35%)
  waiting for transfers between devices  23.4 us (24%)
    pallas_call x11, Pallas kernels, call(): pl.pallas_call(body, out_shape=shapes[0] if single else shapes, in_specs=...  35.2 us
    all_to_all x3, starting transfers between devices, exchange(): return lax.all_to_all(parts, axes, 0, 0)  19 us
    ppermute x5, starting transfers between devices, swap(): return lax.ppermute(value, axis, [(0, 1), (1, 0)])  15.4 us
    all_to_all x3, waiting for transfers between devices, exchange(): return lax.all_to_all(parts, axes, 0, 0)  14.6 us
    ppermute x5, waiting for transfers between devices, swap(): return lax.ppermute(value, axis, [(0, 1), (1, 0)])  4.45 us
    ppermute x1, waiting for transfers between devices, per_device(): following = lax.ppermute(head, slab, [(i + 1, i) for i in range(SLABS - 1)])  4.35 us
    ppermute x1, starting transfers between devices, per_device(): following = lax.ppermute(head, slab, [(i + 1, i) for i in range(SLABS - 1)])  2.86 us
    ppermute x1, starting transfers between devices, per_device(): previous = lax.ppermute(tail, slab, [(i, i + 1) for i in range(SLABS - 1)])  2.03 us
  transfers between devices with their start and end apart: 10, of which 7 were waited for; matrix products, arithmetic and copies ran while one was open for 0% of the time, Pallas kernels for 28%

profile of v4, /device:TPU:1, one launch (start us, length us, event | category | flops | bytes accessed | tf_op | source)
XLA Modules:
  0.0 98.8 jit_solution(3069038961835806917)
XLA Ops:
  0.6 1.3 %shard_map.77 = f32[8,128]{1,0:T(8,128)S(1)} custom-call(bf16[4,512,128]{2,1,0:T(8,128)(2,1)} %bitcast.13), custom_call_target="tpu_custom_call" | custom-call | bytes 1048576 | tf_op jit(solution)/shard_map/pallas_call | solution.py:326
  2.0 7.8 %collective-permute-start = (f32[8,128]{1,0:T(8,128)S(1)}, f32[8,128]{1,0:T(8,128)S(1)}, u32[]{:S(2)}, u32[]{:S(2)}) collective-permute-start(f32[8,128]{1,0:T(8,128)S(1)} %shard_map.77), channel_id=1, source_target_pairs={{0,128},{128,0},{1,129},{129,1},{2,130},{130,2},{3,131},{131,3},{4... | collective-permute-start | bytes 12296 | tf_op jit(solution)/shard_map/ppermute | solution.py:347
  9.8 9.2 %shard_map.76 = (bf16[512,2048]{1,0:T(8,128)(2,1)S(1)}, f32[2,128,128]{2,1,0:T(8,128)S(1)}, bf16[2,512,128]{2,1,0:T(8,128)(2,1)S(1)}, bf16[2,512,128]{2,1,0:T(8,128)(2,1)}) custom-call(bf16[4,512,128]{2,1,0:T(8,128)(2,1)} %bitcast.14, bf16[4,512,128]{2,1,0:T(8,128)(2,1)} %bitcast.18, f32[1,128]{1,0:T(1,128)} %bitcast.21, f32[1,128]{1,0:T(1,128)} %bitcast.22), custom_call_target="tpu_custom_call" | custom-call | bytes 1048576 | tf_op jit(solution)/shard_map/pallas_call | solution.py:326
  19.0 2.9 %collective-permute-start.2 = (bf16[2,512,128]{2,1,0:T(8,128)(2,1)S(1)}, bf16[2,512,128]{2,1,0:T(8,128)(2,1)S(1)}, u32[]{:S(2)}, u32[]{:S(2)}) collective-permute-start(bf16[2,512,128]{2,1,0:T(8,128)(2,1)S(1)} %get-tuple-element.35), channel_id=1, source_target_pairs={{64,0},{128,64},{192,128},{65,1},{129,65},{193,129},{66,2},{130,66... | collective-permute-start | bytes 786440 | tf_op jit(solution)/shard_map/ppermute | solution.py:383
  21.9 0.0 collective-permute-done
  21.9 0.1 collective-permute-start.1
  22.0 0.1 pad_add_fusion.flags
  22.1 1.1 %collective-permute-done.1 = f32[8,128]{1,0:T(8,128)S(1)} collective-permute-done((f32[8,128]{1,0:T(8,128)S(1)}, f32[8,128]{1,0:T(8,128)S(1)}, u32[]{:S(2)}, u32[]{:S(2)}) %collective-permute-start.1) | collective-permute-done | bytes 4128 | tf_op jit(solution)/shard_map/ppermute | solution.py:347
  23.2 3.2 %shard_map.78 = (bf16[1536,512]{1,0:T(8,128)(2,1)}, f32[1792,128]{1,0:T(8,128)S(1)}, f32[1792,128]{1,0:T(8,128)S(1)}, bf16[384,1024]{1,0:T(8,128)(2,1)S(1)}) custom-call(s32[3]{0:T(128)S(1)} %pad_add_fusion.flags, bf16[512,2048]{1,0:T(8,128)(2,1)S(1)} %get-tuple-element.29.adj, f32[16,128]{1,0:T(8,128)S(1)} %pad_maximum_fusion.totals, ...), custom_call_target="tpu_custom_call" | custom-call | flops 4000000000 | bytes 1048576 | tf_op jit(solution)/shard_map/pallas_call | solution.py:326
  26.3 4.4 %collective-permute-done.2.following = bf16[2,512,128]{2,1,0:T(8,128)(2,1)S(1)} collective-permute-done((bf16[2,512,128]{2,1,0:T(8,128)(2,1)S(1)}, bf16[2,512,128]{2,1,0:T(8,128)(2,1)S(1)}, u32[]{:S(2)}, u32[]{:S(2)}) %collective-permute-start.2) | collective-permute-done | bytes 262176 | tf_op jit(solution)/shard_map/ppermute | solution.py:383
  30.7 1.4 %shard_map.79 = (f32[1792,128]{1,0:T(8,128)S(1)}, f32[1792,128]{1,0:T(8,128)S(1)}) custom-call(s32[3]{0:T(128)S(1)} %pad_add_fusion.flags, f32[1792,128]{1,0:T(8,128)S(1)} %get-tuple-element.33.keep_in, f32[1792,128]{1,0:T(8,128)S(1)} %get-tuple-element.34.send_in, ...), custom_call_target="tpu_custom_call", output_to_operand_aliasing={{0}: (1, {}), {1}: (2, {})} | custom-call | bytes 1048576 | tf_op jit(solution)/shard_map/pallas_call | solution.py:326
  32.1 0.1 collective-permute-start.3
  32.2 2.5 %collective-permute-done.3.received = f32[1792,128]{1,0:T(8,128)S(1)} collective-permute-done((f32[1792,128]{1,0:T(8,128)S(1)}, f32[1792,128]{1,0:T(8,128)S(1)}, u32[]{:S(2)}, u32[]{:S(2)}) %collective-permute-start.3) | collective-permute-done | bytes 917536 | tf_op jit(solution)/shard_map/ppermute | solution.py:347
  34.7 1.1 %shard_map.80 = f32[1792,128]{1,0:T(8,128)} custom-call(f32[1792,128]{1,0:T(8,128)S(1)} %get-tuple-element.39.keep, f32[1792,128]{1,0:T(8,128)S(1)} %collective-permute-done.3.received), custom_call_target="tpu_custom_call" | custom-call | bytes 1048576 | tf_op jit(solution)/shard_map/pallas_call | solution.py:326
  35.8 10.2 %all-to-all-start = ((f32[32,56,128]{2,1,0:T(8,128)}), f32[32,56,128]{2,1,0:T(8,128)S(1)}, u32[]{:S(2)}, u32[]{:S(2)}) async-start(f32[32,56,128]{2,1,0:T(8,128)} %bitcast.7), calls=%async_computation | async-start | bytes 1835008 | tf_op jit(solution)/shard_map/all_to_all | solution.py:351
  46.0 0.0 copy-start
  46.0 6.4 %shard_map.81 = (f32[4,512,128]{2,1,0:T(8,128)}, f32[8,128]{1,0:T(8,128)S(1)}) custom-call(bf16[4,512,128]{2,1,0:T(8,128)(2,1)} %bitcast.15, bf16[4,512,128]{2,1,0:T(8,128)(2,1)} %bitcast.19, bf16[2,512,128]{2,1,0:T(8,128)(2,1)S(1)} %collective-permute-done.2.following, bf16[27,128,128]{2,1,0:T(8,128)(2,1)} %kernel.3, f32[16,128]{1,0:T(8,128)S(1)} %pad_maximum_fusion.totals, ...), custom_call_target="tpu_custom_call" | custom-call | flops 4000000000 | bytes 1048576 | tf_op jit(solution)/shard_map/pallas_call | solution.py:326
  52.4 0.0 copy-done
  52.4 2.0 %collective-permute-start.5 = (bf16[2,512,128]{2,1,0:T(8,128)(2,1)S(1)}, bf16[2,512,128]{2,1,0:T(8,128)(2,1)S(1)}, u32[]{:S(2)}, u32[]{:S(2)}) collective-permute-start(bf16[2,512,128]{2,1,0:T(8,128)(2,1)S(1)} %copy-done), channel_id=1, source_target_pairs={{0,64},{64,128},{128,192},{1,65},{65,129},{129,193},{2,66},{66,130... | collective-permute-start | bytes 786440 | tf_op jit(solution)/shard_map/ppermute | solution.py:433
  54.4 0.5 collective-permute-start.4
  54.9 0.9 collective-permute-done.4
  55.8 4.8 %all-to-all-done.parts = f32[32,56,128]{2,1,0:T(8,128)S(1)} async-done(((f32[32,56,128]{2,1,0:T(8,128)}), f32[32,56,128]{2,1,0:T(8,128)S(1)}, u32[]{:S(2)}, u32[]{:S(2)}) %all-to-all-start) | async-done | bytes 917536 | tf_op jit(solution)/shard_map/all_to_all | solution.py:351
  60.6 0.7 shard_map.82
  61.3 3.3 %all-to-all-start.1 = ((f32[4,64,128]{2,1,0:T(8,128)}), f32[4,64,128]{2,1,0:T(8,128)S(1)}, u32[]{:S(2)}, u32[]{:S(2)}) async-start(f32[4,64,128]{2,1,0:T(8,128)} %shard_map.82), calls=%async_computation.1 | async-start | bytes 262144 | tf_op jit(solution)/shard_map/all_to_all | solution.py:351
  64.7 0.0 collective-permute-done.5.previous
  64.7 7.2 %all-to-all-done.1.over_z = f32[4,64,128]{2,1,0:T(8,128)S(1)} async-done(((f32[4,64,128]{2,1,0:T(8,128)}), f32[4,64,128]{2,1,0:T(8,128)S(1)}, u32[]{:S(2)}, u32[]{:S(2)}) %all-to-all-start.1) | async-done | bytes 131104 | tf_op jit(solution)/shard_map/all_to_all | solution.py:351
  71.9 1.3 %shard_map.83 = (bf16[32,56,128]{2,1,0:T(8,128)(2,1)}, f32[8,128]{1,0:T(8,128)S(1)}) custom-call(s32[3]{0:T(128)S(1)} %pad_add_fusion.flags, f32[4,64,128]{2,1,0:T(8,128)S(1)} %all-to-all-done.1.over_z), custom_call_target="tpu_custom_call" | custom-call | bytes 1048576 | tf_op jit(solution)/shard_map/pallas_call | solution.py:326
  73.2 5.5 %all-to-all-start.2 = ((bf16[32,56,128]{2,1,0:T(8,128)(2,1)}), bf16[32,56,128]{2,1,0:T(8,128)(2,1)S(1)}, u32[]{:S(2)}, u32[]{:S(2)}) async-start(bf16[32,56,128]{2,1,0:T(8,128)(2,1)} %get-tuple-element.48), calls=%async_computation.2 | async-start | bytes 917504 | tf_op jit(solution)/shard_map/all_to_all | solution.py:351
  78.7 5.9 %shard_map.84 = bf16[4,512,128]{2,1,0:T(8,128)(2,1)} custom-call(s32[3]{0:T(128)S(1)} %pad_add_fusion.flags, bf16[4,512,128]{2,1,0:T(8,128)(2,1)} %bitcast.16, bf16[2,512,128]{2,1,0:T(8,128)(2,1)S(1)} %collective-permute-done.5.previous, bf16[27,128,128]{2,1,0:T(8,128)(2,1)} %kernel.3, bf16[1536,512]{1,0:T(8,128)(2,1)} %get-tuple-element.50.window, ...), custom_call_target="tpu_custom_call" | custom-call | flops 4000000000 | bytes 1048576 | tf_op jit(solution)/shard_map/pallas_call | solution.py:326
  84.6 2.6 %all-to-all-done.2 = bf16[32,56,128]{2,1,0:T(8,128)(2,1)S(1)} async-done(((bf16[32,56,128]{2,1,0:T(8,128)(2,1)}), bf16[32,56,128]{2,1,0:T(8,128)(2,1)S(1)}, u32[]{:S(2)}, u32[]{:S(2)}) %all-to-all-start.2) | async-done | bytes 458784 | tf_op jit(solution)/shard_map/all_to_all | solution.py:351
  87.2 6.9 %collective-permute-start.6 = (bf16[1792,128]{1,0:T(8,128)(2,1)S(1)}, bf16[1792,128]{1,0:T(8,128)(2,1)S(1)}, u32[]{:S(2)}, u32[]{:S(2)}) collective-permute-start(bf16[1792,128]{1,0:T(8,128)(2,1)S(1)} %bitcast.11), channel_id=1, source_target_pairs={{0,64},{64,0},{1,65},{65,1},{2,66},{66,2},{3,67},{67,3},{4,68},{68... | collective-permute-start | bytes 1376264 | tf_op jit(solution)/shard_map/ppermute | solution.py:347
  94.1 2.8 %shard_map.85 = bf16[4,512,128]{2,1,0:T(8,128)(2,1)} custom-call(bf16[4,512,128]{2,1,0:T(8,128)(2,1)} %bitcast.17, bf16[4,512,128]{2,1,0:T(8,128)(2,1)} %bitcast.20, f32[16,128]{1,0:T(8,128)S(1)} %pad_maximum_fusion.totals, f32[8,128]{1,0:T(8,128)S(1)} %get-tuple-element.52.backward, f32[4,512,128]{2,1,0:T(8,128)} %get-tuple-element.53.scaled), custom_call_target="tpu_custom_call" | custom-call | flops 1000000000 | bytes 1048576 | tf_op jit(solution)/shard_map/pallas_call | solution.py:326
  96.9 0.0 collective-permute-done.6.other
  96.9 1.9 %shard_map.86 = f32[27,128,128]{2,1,0:T(8,128)} custom-call(s32[3]{0:T(128)S(1)} %pad_add_fusion.flags, bf16[1792,128]{1,0:T(8,128)(2,1)S(1)} %bitcast.12, bf16[1792,128]{1,0:T(8,128)(2,1)S(1)} %collective-permute-done.6.other), custom_call_target="tpu_custom_call" | custom-call | bytes 1048576 | tf_op jit(solution)/shard_map/pallas_call | solution.py:326
  (3 shorter events, 0.0 us)
Async XLA Ops:
  2.0 19.9 %collective-permute-start = (f32[8,128]{1,0:T(8,128)S(1)}, f32[8,128]{1,0:T(8,128)S(1)}, u32[]{:S(2)}, u32[]{:S(2)}) collective-permute-start(f32[8,128]{1,0:T(8,128)S(1)} %shard_map.77), channel_id=1, source_target_pairs={{0,128},{128,0},{1,129},{129,1},{2,130},{130,2},{3,131},{131,3},{4... | collective-permute-start | bytes 12296 | tf_op jit(solution)/shard_map/ppermute | solution.py:347
  19.0 11.7 %collective-permute-start.2 = (bf16[2,512,128]{2,1,0:T(8,128)(2,1)S(1)}, bf16[2,512,128]{2,1,0:T(8,128)(2,1)S(1)}, u32[]{:S(2)}, u32[]{:S(2)}) collective-permute-start(bf16[2,512,128]{2,1,0:T(8,128)(2,1)S(1)} %get-tuple-element.35), channel_id=1, source_target_pairs={{64,0},{128,64},{192,128},{65,1},{129,65},{193,129},{66,2},{130,66... | collective-permute-start | bytes 786440 | tf_op jit(solution)/shard_map/ppermute | solution.py:383
  21.9 1.3 %collective-permute-start.1 = (f32[8,128]{1,0:T(8,128)S(1)}, f32[8,128]{1,0:T(8,128)S(1)}, u32[]{:S(2)}, u32[]{:S(2)}) collective-permute-start(f32[8,128]{1,0:T(8,128)S(1)} %add.10), channel_id=1, source_target_pairs={{0,64},{64,0},{1,65},{65,1},{2,66},{66,2},{3,67},{67,3},{4,68},{68... | collective-permute-start | bytes 12296 | tf_op jit(solution)/shard_map/ppermute | solution.py:347
  32.1 2.6 %collective-permute-start.3 = (f32[1792,128]{1,0:T(8,128)S(1)}, f32[1792,128]{1,0:T(8,128)S(1)}, u32[]{:S(2)}, u32[]{:S(2)}) collective-permute-start(f32[1792,128]{1,0:T(8,128)S(1)} %get-tuple-element.40), channel_id=1, source_target_pairs={{0,64},{64,0},{1,65},{65,1},{2,66},{66,2},{3,67},{67,3},{4,68},{68... | collective-permute-start | bytes 2752520 | tf_op jit(solution)/shard_map/ppermute | solution.py:347
  35.8 24.8 %all-to-all-start = ((f32[32,56,128]{2,1,0:T(8,128)}), f32[32,56,128]{2,1,0:T(8,128)S(1)}, u32[]{:S(2)}, u32[]{:S(2)}) async-start(f32[32,56,128]{2,1,0:T(8,128)} %bitcast.7), calls=%async_computation | async-start | bytes 1835008 | tf_op jit(solution)/shard_map/all_to_all | solution.py:351
  46.0 6.4 %copy-start = (bf16[2,512,128]{2,1,0:T(8,128)(2,1)S(1)}, bf16[2,512,128]{2,1,0:T(8,128)(2,1)}, u32[]{:S(2)}) copy-start(bf16[2,512,128]{2,1,0:T(8,128)(2,1)} %get-tuple-element.44) | copy-start | bytes 786436
  52.4 12.3 %collective-permute-start.5 = (bf16[2,512,128]{2,1,0:T(8,128)(2,1)S(1)}, bf16[2,512,128]{2,1,0:T(8,128)(2,1)S(1)}, u32[]{:S(2)}, u32[]{:S(2)}) collective-permute-start(bf16[2,512,128]{2,1,0:T(8,128)(2,1)S(1)} %copy-done), channel_id=1, source_target_pairs={{0,64},{64,128},{128,192},{1,65},{65,129},{129,193},{2,66},{66,130... | collective-permute-start | bytes 786440 | tf_op jit(solution)/shard_map/ppermute | solution.py:433
  54.4 1.4 %collective-permute-start.4 = (f32[8,128]{1,0:T(8,128)S(1)}, f32[8,128]{1,0:T(8,128)S(1)}, u32[]{:S(2)}, u32[]{:S(2)}) collective-permute-start(f32[8,128]{1,0:T(8,128)S(1)} %get-tuple-element.43), channel_id=1, source_target_pairs={{0,64},{64,0},{1,65},{65,1},{2,66},{66,2},{3,67},{67,3},{4,68},{68... | collective-permute-start | bytes 12296 | tf_op jit(solution)/shard_map/ppermute | solution.py:347
  61.3 10.5 %all-to-all-start.1 = ((f32[4,64,128]{2,1,0:T(8,128)}), f32[4,64,128]{2,1,0:T(8,128)S(1)}, u32[]{:S(2)}, u32[]{:S(2)}) async-start(f32[4,64,128]{2,1,0:T(8,128)} %shard_map.82), calls=%async_computation.1 | async-start | bytes 262144 | tf_op jit(solution)/shard_map/all_to_all | solution.py:351
  73.2 13.9 %all-to-all-start.2 = ((bf16[32,56,128]{2,1,0:T(8,128)(2,1)}), bf16[32,56,128]{2,1,0:T(8,128)(2,1)S(1)}, u32[]{:S(2)}, u32[]{:S(2)}) async-start(bf16[32,56,128]{2,1,0:T(8,128)(2,1)} %get-tuple-element.48), calls=%async_computation.2 | async-start | bytes 917504 | tf_op jit(solution)/shard_map/all_to_all | solution.py:351
  87.2 9.7 %collective-permute-start.6 = (bf16[1792,128]{1,0:T(8,128)(2,1)S(1)}, bf16[1792,128]{1,0:T(8,128)(2,1)S(1)}, u32[]{:S(2)}, u32[]{:S(2)}) collective-permute-start(bf16[1792,128]{1,0:T(8,128)(2,1)S(1)} %bitcast.11), channel_id=1, source_target_pairs={{0,64},{64,0},{1,65},{65,1},{2,66},{66,2},{3,67},{67,3},{4,68},{68... | collective-permute-start | bytes 1376264 | tf_op jit(solution)/shard_map/ppermute | solution.py:347

commit v5 on v4

--- a/solution.py
+++ b/solution.py
@@ -95,7 +95,7 @@
             adj[ki * C : (ki + 1) * C, (f * H + h) * W : (f * H + h + 1) * W] = block
 
 
-def prepare_kernel(lat, cot, gain, shift, adj, scales, head, tail, lat_v, cot_v, gain_v, shift_v, tmp, sem):
+def prepare_kernel(lat, cot, gain, shift, adj, scales, head, tail, lat_v, cot_v, gain_v, shift_v, tmp, sem, tail_sem):
     from_lat, from_cot, *small = copies(
         sem,
         (lat, lat_v),
@@ -103,9 +103,9 @@
         (gain, gain_v),
         (shift, shift_v),
         (cot.at[:HALO], head),
-        (lat.at[T - HALO :], tail),
     )
     from_lat.wait()
+    (to_tail,) = copies(tail_sem, (lat_v.at[T - HALO :], tail))
     for t in range(T):
         for h, block in enumerate(by_row(lat_v[t], tmp)):
             adj[3 * C :, (t * H + h) * W : (t * H + h + 1) * W] = block.astype(BF16)
@@ -116,6 +116,7 @@
         copy.wait()
     scales[0] = jnp.broadcast_to(channel_column(gain_v[...]), (C, W))
     scales[1] = jnp.broadcast_to(channel_column(shift_v[...]), (C, W))
+    to_tail.wait()
 
 
 def by_row(frame, tmp):
@@ -251,14 +252,26 @@
     backward[...] = first + second
 
 
-def place_kernel(flags, mine, other, grad):
+def place_kernel(flags, half_grad, grad, grad_v, sem, first):
     half = C // 2
-    core = flags[1]
-    for tap in range(27):
-        a = mine[tap * half : (tap + 1) * half].astype(F32)
-        b = other[tap * half : (tap + 1) * half].astype(F32)
-        grad[tap, :half] = jnp.where(core == 0, a, b)
-        grad[tap, half:] = jnp.where(core == 0, b, a)
+    core = flags[1] if first else 1 - flags[1]
+    at = pl.multiple_of(core * half, half)
+    started = []
+    for kt in range(3):
+        rows_of = half_grad[9 * kt * half : 9 * (kt + 1) * half].astype(F32)
+        grad_v[9 * kt : 9 * (kt + 1)] = rows_of.reshape(9, half, C)
+        taps = pl.ds(9 * kt, 9)
+        started += copies(sem.at[pl.ds(kt, 1)], (grad_v.at[taps], grad.at[taps, pl.ds(at, half)]))
+    for copy in started:
+        copy.wait()
+
+
+def place_first(flags, half_grad, grad, grad_v, sem):
+    place_kernel(flags, half_grad, grad, grad_v, sem, True)
+
+
+def place_second(flags, half_grad, grad_in, grad, grad_v, sem):
+    place_kernel(flags, half_grad, grad, grad_v, sem, False)
 
 
 def conv_kernel(
@@ -370,7 +383,7 @@
     adj, scales, head, tail = call(
         prepare_kernel,
         (shape(4 * C, T * PLANE, dtype=BF16), shape(2, C, W), halo, halo),
-        [frames, frames, row, row, tmp, sems(6)],
+        [frames, frames, row, row, tmp, sems(5), sems(1)],
         lat,
         cot,
         gain,
@@ -433,12 +446,6 @@
     previous = lax.ppermute(tail, slab, [(i, i + 1) for i in range(SLABS - 1)])
     sums = sums + swap(sums, "core")
     packed = call(part_kernel, shape(4, PART + 8, C), [], parts, sums)
-    over_z, previous = lax.optimization_barrier((exchange(packed, ("zh", "zm")), previous))
-    part, backward = call(
-        merge_kernel, (shape(SIDE, PART, C, dtype=BF16), shape(8, C)), [], flags, over_z, scalars=1
-    )
-    part, window = lax.optimization_barrier((part, window))
-    mine = exchange(part, ("y", "zn", "x")).reshape(COMM, C)
     output = call(
         conv_kernel,
         shape(T, ROWS, W, dtype=BF16),
@@ -455,8 +462,10 @@
         scalars=1,
         flops=4 * 10**9,
     )
-    mine, output = lax.optimization_barrier((mine, output))
-    other = swap(mine, "core")
+    over_z, output = lax.optimization_barrier((exchange(packed, ("zh", "zm")), output))
+    part, backward = call(
+        merge_kernel, (shape(SIDE, PART, C, dtype=BF16), shape(8, C)), [], flags, over_z, scalars=1
+    )
     result = call(
         adjoint_kernel,
         shape(T, ROWS, W, dtype=BF16),
@@ -469,7 +478,24 @@
         far=(0, 1, 4),
         flops=10**9,
     )
-    kernel_grad = call(place_kernel, shape(27, C, C), [], flags, mine, other, scalars=1)
+    mine, result = lax.optimization_barrier((exchange(part, ("y", "zn", "x")).reshape(COMM, C), result))
+    other = swap(mine, "core")
+    half_scratch = [pltpu.VMEM((27, C // 2, C), F32), sems(3)]
+    kernel_grad = call(
+        place_first, shape(27, C, C), half_scratch, flags, mine, out_far=(0,), scalars=1, flops=10**9
+    )
+    kernel_grad = call(
+        place_second,
+        shape(27, C, C),
+        half_scratch,
+        flags,
+        other,
+        kernel_grad,
+        far=(2,),
+        out_far=(0,),
+        scalars=1,
+        aliases=((2, 0),),
+    )
     return output.reshape(latents.shape), result.reshape(latents.shape), kernel_grad
 
 

time: 99.3 us -> 90 us (0.906)
  Pallas kernels: 35.2 us -> 28.9 us
  waiting for transfers between devices: 23.4 us -> 20.5 us
    pallas_call x11 -> x12, Pallas kernels: 35.2 us -> 28.9 us  [call(): pl.pallas_call(body, out_shape=shapes[0] if single else shapes, in_specs=...]
    all_to_all x3, waiting for transfers between devices: 14.6 us -> 11.7 us  [exchange(): return lax.all_to_all(parts, axes, 0, 0)]
  transfers between devices with their start and end apart: 10 -> 10, of which waited for: 7 -> 7; matrix products, arithmetic and copies ran while one was open for 0% -> 0% of each run, Pallas kernels for 28% -> 25%
where the time goes in v5:
time: 90 us; the launch traced here: 89.5 us
  starting transfers between devices  38.9 us (43%)
  Pallas kernels  28.9 us (32%)
  waiting for transfers between devices  20.5 us (23%)
  between operations  0.97 us (1%)
    pallas_call x12, Pallas kernels, call(): pl.pallas_call(body, out_shape=shapes[0] if single else shapes, in_specs=...  28.9 us
    all_to_all x3, starting transfers between devices, exchange(): return lax.all_to_all(parts, axes, 0, 0)  19.2 us
    ppermute x5, starting transfers between devices, swap(): return lax.ppermute(value, axis, [(0, 1), (1, 0)])  14.8 us
    all_to_all x3, waiting for transfers between devices, exchange(): return lax.all_to_all(parts, axes, 0, 0)  11.7 us
    ppermute x5, waiting for transfers between devices, swap(): return lax.ppermute(value, axis, [(0, 1), (1, 0)])  4.45 us
    ppermute x1, waiting for transfers between devices, per_device(): following = lax.ppermute(head, slab, [(i + 1, i) for i in range(SLABS - 1)])  4.35 us
    ppermute x1, starting transfers between devices, per_device(): following = lax.ppermute(head, slab, [(i + 1, i) for i in range(SLABS - 1)])  2.86 us
    ppermute x1, starting transfers between devices, per_device(): previous = lax.ppermute(tail, slab, [(i, i + 1) for i in range(SLABS - 1)])  2.03 us
  transfers between devices with their start and end apart: 10, of which 7 were waited for; matrix products, arithmetic and copies ran while one was open for 0% of the time, Pallas kernels for 25%

profile of v5, /device:TPU:1, one launch (start us, length us, event | category | flops | bytes accessed | tf_op | source)
XLA Modules:
  0.0 89.5 jit_solution(4263920251805619600)
XLA Ops:
  0.6 1.3 %shard_map.77 = f32[8,128]{1,0:T(8,128)S(1)} custom-call(bf16[4,512,128]{2,1,0:T(8,128)(2,1)} %bitcast.13), custom_call_target="tpu_custom_call" | custom-call | bytes 1048576 | tf_op jit(solution)/shard_map/pallas_call | solution.py:339
  2.0 7.8 %collective-permute-start = (f32[8,128]{1,0:T(8,128)S(1)}, f32[8,128]{1,0:T(8,128)S(1)}, u32[]{:S(2)}, u32[]{:S(2)}) collective-permute-start(f32[8,128]{1,0:T(8,128)S(1)} %shard_map.77), channel_id=1, source_target_pairs={{0,128},{128,0},{1,129},{129,1},{2,130},{130,2},{3,131},{131,3},{4... | collective-permute-start | bytes 12296 | tf_op jit(solution)/shard_map/ppermute | solution.py:360
  9.8 1.8 %shard_map.76 = (bf16[512,2048]{1,0:T(8,128)(2,1)S(1)}, f32[2,128,128]{2,1,0:T(8,128)S(1)}, bf16[2,512,128]{2,1,0:T(8,128)(2,1)S(1)}, bf16[2,512,128]{2,1,0:T(8,128)(2,1)}) custom-call(bf16[4,512,128]{2,1,0:T(8,128)(2,1)} %bitcast.14, bf16[4,512,128]{2,1,0:T(8,128)(2,1)} %bitcast.18, f32[1,128]{1,0:T(1,128)} %bitcast.21, f32[1,128]{1,0:T(1,128)} %bitcast.22), custom_call_target="tpu_custom_call" | custom-call | bytes 1048576 | tf_op jit(solution)/shard_map/pallas_call | solution.py:339
  11.6 2.9 %collective-permute-start.2 = (bf16[2,512,128]{2,1,0:T(8,128)(2,1)S(1)}, bf16[2,512,128]{2,1,0:T(8,128)(2,1)S(1)}, u32[]{:S(2)}, u32[]{:S(2)}) collective-permute-start(bf16[2,512,128]{2,1,0:T(8,128)(2,1)S(1)} %get-tuple-element.33), channel_id=1, source_target_pairs={{64,0},{128,64},{192,128},{65,1},{129,65},{193,129},{66,2},{130,66... | collective-permute-start | bytes 786440 | tf_op jit(solution)/shard_map/ppermute | solution.py:396
  14.5 0.0 collective-permute-done
  14.5 0.1 collective-permute-start.1
  14.6 0.1 pad_add_fusion.flags
  14.7 1.1 %collective-permute-done.1 = f32[8,128]{1,0:T(8,128)S(1)} collective-permute-done((f32[8,128]{1,0:T(8,128)S(1)}, f32[8,128]{1,0:T(8,128)S(1)}, u32[]{:S(2)}, u32[]{:S(2)}) %collective-permute-start.1) | collective-permute-done | bytes 4128 | tf_op jit(solution)/shard_map/ppermute | solution.py:360
  15.7 3.2 %shard_map.78 = (bf16[1536,512]{1,0:T(8,128)(2,1)}, f32[1792,128]{1,0:T(8,128)S(1)}, f32[1792,128]{1,0:T(8,128)S(1)}, bf16[384,1024]{1,0:T(8,128)(2,1)S(1)}) custom-call(s32[3]{0:T(128)S(1)} %pad_add_fusion.flags, bf16[512,2048]{1,0:T(8,128)(2,1)S(1)} %get-tuple-element.27.adj, f32[16,128]{1,0:T(8,128)S(1)} %pad_maximum_fusion.totals, ...), custom_call_target="tpu_custom_call" | custom-call | flops 4000000000 | bytes 1048576 | tf_op jit(solution)/shard_map/pallas_call | solution.py:339
  18.9 4.4 %collective-permute-done.2.following = bf16[2,512,128]{2,1,0:T(8,128)(2,1)S(1)} collective-permute-done((bf16[2,512,128]{2,1,0:T(8,128)(2,1)S(1)}, bf16[2,512,128]{2,1,0:T(8,128)(2,1)S(1)}, u32[]{:S(2)}, u32[]{:S(2)}) %collective-permute-start.2) | collective-permute-done | bytes 262176 | tf_op jit(solution)/shard_map/ppermute | solution.py:396
  23.3 1.4 %shard_map.79 = (f32[1792,128]{1,0:T(8,128)S(1)}, f32[1792,128]{1,0:T(8,128)S(1)}) custom-call(s32[3]{0:T(128)S(1)} %pad_add_fusion.flags, f32[1792,128]{1,0:T(8,128)S(1)} %get-tuple-element.31.keep_in, f32[1792,128]{1,0:T(8,128)S(1)} %get-tuple-element.32.send_in, ...), custom_call_target="tpu_custom_call", output_to_operand_aliasing={{0}: (1, {}), {1}: (2, {})} | custom-call | bytes 1048576 | tf_op jit(solution)/shard_map/pallas_call | solution.py:339
  24.7 0.1 collective-permute-start.3
  24.8 2.5 %collective-permute-done.3.received = f32[1792,128]{1,0:T(8,128)S(1)} collective-permute-done((f32[1792,128]{1,0:T(8,128)S(1)}, f32[1792,128]{1,0:T(8,128)S(1)}, u32[]{:S(2)}, u32[]{:S(2)}) %collective-permute-start.3) | collective-permute-done | bytes 917536 | tf_op jit(solution)/shard_map/ppermute | solution.py:360
  27.3 1.1 %shard_map.80 = f32[1792,128]{1,0:T(8,128)} custom-call(f32[1792,128]{1,0:T(8,128)S(1)} %get-tuple-element.37.keep, f32[1792,128]{1,0:T(8,128)S(1)} %collective-permute-done.3.received), custom_call_target="tpu_custom_call" | custom-call | bytes 1048576 | tf_op jit(solution)/shard_map/pallas_call | solution.py:339
  28.4 10.2 %all-to-all-start = ((f32[32,56,128]{2,1,0:T(8,128)}), f32[32,56,128]{2,1,0:T(8,128)S(1)}, u32[]{:S(2)}, u32[]{:S(2)}) async-start(f32[32,56,128]{2,1,0:T(8,128)} %bitcast.7), calls=%async_computation | async-start | bytes 1835008 | tf_op jit(solution)/shard_map/all_to_all | solution.py:364
  38.6 0.0 copy-start
  38.6 6.4 %shard_map.81 = (f32[4,512,128]{2,1,0:T(8,128)}, f32[8,128]{1,0:T(8,128)S(1)}) custom-call(bf16[4,512,128]{2,1,0:T(8,128)(2,1)} %bitcast.15, bf16[4,512,128]{2,1,0:T(8,128)(2,1)} %bitcast.19, bf16[2,512,128]{2,1,0:T(8,128)(2,1)S(1)} %collective-permute-done.2.following, bf16[27,128,128]{2,1,0:T(8,128)(2,1)} %kernel.3, f32[16,128]{1,0:T(8,128)S(1)} %pad_maximum_fusion.totals, ...), custom_call_target="tpu_custom_call" | custom-call | flops 4000000000 | bytes 1048576 | tf_op jit(solution)/shard_map/pallas_call | solution.py:339
  45.0 0.0 copy-done
  45.0 2.0 %collective-permute-start.5 = (bf16[2,512,128]{2,1,0:T(8,128)(2,1)S(1)}, bf16[2,512,128]{2,1,0:T(8,128)(2,1)S(1)}, u32[]{:S(2)}, u32[]{:S(2)}) collective-permute-start(bf16[2,512,128]{2,1,0:T(8,128)(2,1)S(1)} %copy-done), channel_id=1, source_target_pairs={{0,64},{64,128},{128,192},{1,65},{65,129},{129,193},{2,66},{66,130... | collective-permute-start | bytes 786440 | tf_op jit(solution)/shard_map/ppermute | solution.py:446
  47.0 0.5 collective-permute-start.4
  47.5 0.9 %collective-permute-done.4 = f32[8,128]{1,0:T(8,128)S(1)} collective-permute-done((f32[8,128]{1,0:T(8,128)S(1)}, f32[8,128]{1,0:T(8,128)S(1)}, u32[]{:S(2)}, u32[]{:S(2)}) %collective-permute-start.4) | collective-permute-done | bytes 4128 | tf_op jit(solution)/shard_map/ppermute | solution.py:360
  48.4 4.8 %all-to-all-done.parts = f32[32,56,128]{2,1,0:T(8,128)S(1)} async-done(((f32[32,56,128]{2,1,0:T(8,128)}), f32[32,56,128]{2,1,0:T(8,128)S(1)}, u32[]{:S(2)}, u32[]{:S(2)}) %all-to-all-start) | async-done | bytes 917536 | tf_op jit(solution)/shard_map/all_to_all | solution.py:364
  53.2 0.7 shard_map.82
  53.9 3.5 %all-to-all-start.1 = ((f32[4,64,128]{2,1,0:T(8,128)}), f32[4,64,128]{2,1,0:T(8,128)S(1)}, u32[]{:S(2)}, u32[]{:S(2)}) async-start(f32[4,64,128]{2,1,0:T(8,128)} %shard_map.82), calls=%async_computation.1 | async-start | bytes 262144 | tf_op jit(solution)/shard_map/all_to_all | solution.py:364
  57.4 0.0 collective-permute-done.5.previous
  57.5 5.9 %shard_map.83 = bf16[4,512,128]{2,1,0:T(8,128)(2,1)} custom-call(s32[3]{0:T(128)S(1)} %pad_add_fusion.flags, bf16[4,512,128]{2,1,0:T(8,128)(2,1)} %bitcast.16, bf16[2,512,128]{2,1,0:T(8,128)(2,1)S(1)} %collective-permute-done.5.previous, bf16[27,128,128]{2,1,0:T(8,128)(2,1)} %kernel.3, bf16[1536,512]{1,0:T(8,128)(2,1)} %get-tuple-element.43.window, ...), custom_call_target="tpu_custom_call" | custom-call | flops 4000000000 | bytes 1048576 | tf_op jit(solution)/shard_map/pallas_call | solution.py:339
  63.3 1.1 %all-to-all-done.1.over_z = f32[4,64,128]{2,1,0:T(8,128)S(1)} async-done(((f32[4,64,128]{2,1,0:T(8,128)}), f32[4,64,128]{2,1,0:T(8,128)S(1)}, u32[]{:S(2)}, u32[]{:S(2)}) %all-to-all-start.1) | async-done | bytes 131104 | tf_op jit(solution)/shard_map/all_to_all | solution.py:364
  64.5 1.3 %shard_map.84 = (bf16[32,56,128]{2,1,0:T(8,128)(2,1)}, f32[8,128]{1,0:T(8,128)S(1)}) custom-call(s32[3]{0:T(128)S(1)} %pad_add_fusion.flags, f32[4,64,128]{2,1,0:T(8,128)S(1)} %all-to-all-done.1.over_z), custom_call_target="tpu_custom_call" | custom-call | bytes 1048576 | tf_op jit(solution)/shard_map/pallas_call | solution.py:339
  65.8 5.5 %all-to-all-start.2 = ((bf16[32,56,128]{2,1,0:T(8,128)(2,1)}), bf16[32,56,128]{2,1,0:T(8,128)(2,1)S(1)}, u32[]{:S(2)}, u32[]{:S(2)}) async-start(bf16[32,56,128]{2,1,0:T(8,128)(2,1)} %get-tuple-element.46), calls=%async_computation.2 | async-start | bytes 917504 | tf_op jit(solution)/shard_map/all_to_all | solution.py:364
  71.4 2.8 %shard_map.85 = bf16[4,512,128]{2,1,0:T(8,128)(2,1)} custom-call(bf16[4,512,128]{2,1,0:T(8,128)(2,1)} %bitcast.17, bf16[4,512,128]{2,1,0:T(8,128)(2,1)} %bitcast.20, f32[16,128]{1,0:T(8,128)S(1)} %pad_maximum_fusion.totals, f32[8,128]{1,0:T(8,128)S(1)} %get-tuple-element.47.backward, f32[4,512,128]{2,1,0:T(8,128)} %get-tuple-element.48.scaled), custom_call_target="tpu_custom_call" | custom-call | flops 1000000000 | bytes 1048576 | tf_op jit(solution)/shard_map/pallas_call | solution.py:339
  74.2 5.8 %all-to-all-done.2 = bf16[32,56,128]{2,1,0:T(8,128)(2,1)S(1)} async-done(((bf16[32,56,128]{2,1,0:T(8,128)(2,1)}), bf16[32,56,128]{2,1,0:T(8,128)(2,1)S(1)}, u32[]{:S(2)}, u32[]{:S(2)}) %all-to-all-start.2) | async-done | bytes 458784 | tf_op jit(solution)/shard_map/all_to_all | solution.py:364
  80.0 6.3 %collective-permute-start.6 = (bf16[1792,128]{1,0:T(8,128)(2,1)S(1)}, bf16[1792,128]{1,0:T(8,128)(2,1)S(1)}, u32[]{:S(2)}, u32[]{:S(2)}) collective-permute-start(bf16[1792,128]{1,0:T(8,128)(2,1)S(1)} %bitcast.11), channel_id=1, source_target_pairs={{0,64},{64,0},{1,65},{65,1},{2,66},{66,2},{3,67},{67,3},{4,68},{68... | collective-permute-start | bytes 1376264 | tf_op jit(solution)/shard_map/ppermute | solution.py:360
  86.3 1.5 %shard_map.86.grad_in = f32[27,128,128]{2,1,0:T(8,128)} custom-call(s32[3]{0:T(128)S(1)} %pad_add_fusion.flags, bf16[1792,128]{1,0:T(8,128)(2,1)S(1)} %bitcast.12), custom_call_target="tpu_custom_call" | custom-call | flops 1000000000 | bytes 1048576 | tf_op jit(solution)/shard_map/pallas_call | solution.py:339
  87.8 0.0 collective-permute-done.6.half_grad
  87.8 1.5 %shard_map.87 = f32[27,128,128]{2,1,0:T(8,128)} custom-call(s32[3]{0:T(128)S(1)} %pad_add_fusion.flags, bf16[1792,128]{1,0:T(8,128)(2,1)S(1)} %collective-permute-done.6.half_grad, f32[27,128,128]{2,1,0:T(8,128)} %shard_map.86.grad_in), custom_call_target="tpu_custom_call", output_to_operand_aliasing={{}: (2, {})} | custom-call | bytes 1048576 | tf_op jit(solution)/shard_map/pallas_call | solution.py:339
  (3 shorter events, 0.0 us)
Async XLA Ops:
  2.0 12.5 %collective-permute-start = (f32[8,128]{1,0:T(8,128)S(1)}, f32[8,128]{1,0:T(8,128)S(1)}, u32[]{:S(2)}, u32[]{:S(2)}) collective-permute-start(f32[8,128]{1,0:T(8,128)S(1)} %shard_map.77), channel_id=1, source_target_pairs={{0,128},{128,0},{1,129},{129,1},{2,130},{130,2},{3,131},{131,3},{4... | collective-permute-start | bytes 12296 | tf_op jit(solution)/shard_map/ppermute | solution.py:360
  11.6 11.7 %collective-permute-start.2 = (bf16[2,512,128]{2,1,0:T(8,128)(2,1)S(1)}, bf16[2,512,128]{2,1,0:T(8,128)(2,1)S(1)}, u32[]{:S(2)}, u32[]{:S(2)}) collective-permute-start(bf16[2,512,128]{2,1,0:T(8,128)(2,1)S(1)} %get-tuple-element.33), channel_id=1, source_target_pairs={{64,0},{128,64},{192,128},{65,1},{129,65},{193,129},{66,2},{130,66... | collective-permute-start | bytes 786440 | tf_op jit(solution)/shard_map/ppermute | solution.py:396
  14.5 1.3 %collective-permute-start.1 = (f32[8,128]{1,0:T(8,128)S(1)}, f32[8,128]{1,0:T(8,128)S(1)}, u32[]{:S(2)}, u32[]{:S(2)}) collective-permute-start(f32[8,128]{1,0:T(8,128)S(1)} %add.10), channel_id=1, source_target_pairs={{0,64},{64,0},{1,65},{65,1},{2,66},{66,2},{3,67},{67,3},{4,68},{68... | collective-permute-start | bytes 12296 | tf_op jit(solution)/shard_map/ppermute | solution.py:360
  24.7 2.6 %collective-permute-start.3 = (f32[1792,128]{1,0:T(8,128)S(1)}, f32[1792,128]{1,0:T(8,128)S(1)}, u32[]{:S(2)}, u32[]{:S(2)}) collective-permute-start(f32[1792,128]{1,0:T(8,128)S(1)} %get-tuple-element.38), channel_id=1, source_target_pairs={{0,64},{64,0},{1,65},{65,1},{2,66},{66,2},{3,67},{67,3},{4,68},{68... | collective-permute-start | bytes 2752520 | tf_op jit(solution)/shard_map/ppermute | solution.py:360
  28.4 24.8 %all-to-all-start = ((f32[32,56,128]{2,1,0:T(8,128)}), f32[32,56,128]{2,1,0:T(8,128)S(1)}, u32[]{:S(2)}, u32[]{:S(2)}) async-start(f32[32,56,128]{2,1,0:T(8,128)} %bitcast.7), calls=%async_computation | async-start | bytes 1835008 | tf_op jit(solution)/shard_map/all_to_all | solution.py:364
  38.6 6.4 %copy-start = (bf16[2,512,128]{2,1,0:T(8,128)(2,1)S(1)}, bf16[2,512,128]{2,1,0:T(8,128)(2,1)}, u32[]{:S(2)}) copy-start(bf16[2,512,128]{2,1,0:T(8,128)(2,1)} %get-tuple-element.42) | copy-start | bytes 786436
  45.0 12.5 %collective-permute-start.5 = (bf16[2,512,128]{2,1,0:T(8,128)(2,1)S(1)}, bf16[2,512,128]{2,1,0:T(8,128)(2,1)S(1)}, u32[]{:S(2)}, u32[]{:S(2)}) collective-permute-start(bf16[2,512,128]{2,1,0:T(8,128)(2,1)S(1)} %copy-done), channel_id=1, source_target_pairs={{0,64},{64,128},{128,192},{1,65},{65,129},{129,193},{2,66},{66,130... | collective-permute-start | bytes 786440 | tf_op jit(solution)/shard_map/ppermute | solution.py:446
  47.0 1.4 %collective-permute-start.4 = (f32[8,128]{1,0:T(8,128)S(1)}, f32[8,128]{1,0:T(8,128)S(1)}, u32[]{:S(2)}, u32[]{:S(2)}) collective-permute-start(f32[8,128]{1,0:T(8,128)S(1)} %get-tuple-element.41), channel_id=1, source_target_pairs={{0,64},{64,0},{1,65},{65,1},{2,66},{66,2},{3,67},{67,3},{4,68},{68... | collective-permute-start | bytes 12296 | tf_op jit(solution)/shard_map/ppermute | solution.py:360
  53.9 10.5 %all-to-all-start.1 = ((f32[4,64,128]{2,1,0:T(8,128)}), f32[4,64,128]{2,1,0:T(8,128)S(1)}, u32[]{:S(2)}, u32[]{:S(2)}) async-start(f32[4,64,128]{2,1,0:T(8,128)} %shard_map.82), calls=%async_computation.1 | async-start | bytes 262144 | tf_op jit(solution)/shard_map/all_to_all | solution.py:364
  65.8 14.2 %all-to-all-start.2 = ((bf16[32,56,128]{2,1,0:T(8,128)(2,1)}), bf16[32,56,128]{2,1,0:T(8,128)(2,1)S(1)}, u32[]{:S(2)}, u32[]{:S(2)}) async-start(bf16[32,56,128]{2,1,0:T(8,128)(2,1)} %get-tuple-element.46), calls=%async_computation.2 | async-start | bytes 917504 | tf_op jit(solution)/shard_map/all_to_all | solution.py:364
  80.0 7.8 %collective-permute-start.6 = (bf16[1792,128]{1,0:T(8,128)(2,1)S(1)}, bf16[1792,128]{1,0:T(8,128)(2,1)S(1)}, u32[]{:S(2)}, u32[]{:S(2)}) collective-permute-start(bf16[1792,128]{1,0:T(8,128)(2,1)S(1)} %bitcast.11), channel_id=1, source_target_pairs={{0,64},{64,0},{1,65},{65,1},{2,66},{66,2},{3,67},{67,3},{4,68},{68... | collective-permute-start | bytes 1376264 | tf_op jit(solution)/shard_map/ppermute | solution.py:360

commit v6 on v5

--- a/solution.py
+++ b/solution.py
@@ -95,17 +95,21 @@
             adj[ki * C : (ki + 1) * C, (f * H + h) * W : (f * H + h + 1) * W] = block
 
 
-def prepare_kernel(lat, cot, gain, shift, adj, scales, head, tail, lat_v, cot_v, gain_v, shift_v, tmp, sem, tail_sem):
-    from_lat, from_cot, *small = copies(
-        sem,
-        (lat, lat_v),
-        (cot, cot_v),
-        (gain, gain_v),
-        (shift, shift_v),
-        (cot.at[:HALO], head),
-    )
+def prepare_kernel(
+    flags, lat, cot, gain, shift, adj, scales, near, far, lat_v, cot_v, gain_v, shift_v, tmp, sem, halo_sem
+):
+    tail, head = lat.at[T - HALO :], cot.at[:HALO]
+
+    @pl.when(flags[1] == 0)
+    def _():
+        copies(halo_sem, (tail, near), (head, far))
+
+    @pl.when(flags[1] != 0)
+    def _():
+        copies(halo_sem, (head, near), (tail, far))
+
+    from_lat, from_cot, *small = copies(sem, (lat, lat_v), (cot, cot_v), (gain, gain_v), (shift, shift_v))
     from_lat.wait()
-    (to_tail,) = copies(tail_sem, (lat_v.at[T - HALO :], tail))
     for t in range(T):
         for h, block in enumerate(by_row(lat_v[t], tmp)):
             adj[3 * C :, (t * H + h) * W : (t * H + h + 1) * W] = block.astype(BF16)
@@ -116,7 +120,12 @@
         copy.wait()
     scales[0] = jnp.broadcast_to(channel_column(gain_v[...]), (C, W))
     scales[1] = jnp.broadcast_to(channel_column(shift_v[...]), (C, W))
-    to_tail.wait()
+    pltpu.make_async_copy(tail, near, halo_sem.at[0]).wait()
+    pltpu.make_async_copy(head, far, halo_sem.at[1]).wait()
+
+
+def pick(condition, first, second):
+    return jnp.where(condition, first.astype(F32), second.astype(F32))
 
 
 def by_row(frame, tmp):
@@ -125,12 +134,12 @@
 
 
 def back_kernel(
-    lat, cot, following, kernel, totals, scales, scaled, sums, tmp, window, taps, lat_v, cot_v, kernel_v, scaled_v, sem
+    flags, lat, cot, near, far, kernel, totals, scales, scaled, sums, tmp, window, taps, lat_v, cot_v, kernel_v, scaled_v, sem
 ):
     from_cot, from_kernel, from_lat = copies(sem, (cot, cot_v), (kernel, kernel_v), (lat, lat_v))
     from_cot.wait()
     for f in range(T + HALO):
-        blocks = by_row(cot_v[f] if f < T else following[f - T], tmp)
+        blocks = by_row(cot_v[f] if f < T else pick(flags[1] == 0, near[f - T], far[f - T]), tmp)
         for h in range(H):
             for s, moved in enumerate(shifted(blocks[h])):
                 at = (s * H + h) * C
@@ -218,9 +227,9 @@
     to_window.wait()
 
 
-def edge_kernel(flags, keep_in, send_in, following, last, keep, send, tmp, adj):
+def edge_kernel(flags, keep_in, send_in, near, far, last, keep, send, tmp, adj):
     for f in range(HALO):
-        put_adjoint(adj, f, by_row(following[f], tmp))
+        put_adjoint(adj, f, by_row(pick(flags[1] == 0, near[f], far[f]), tmp))
     for kt in range(2):
         ahead = 2 - kt
         grads = lax.dot_general(
@@ -237,19 +246,16 @@
 
 
 def part_kernel(parts, sums, packed):
-    part = jnp.sum(parts[...].astype(F32), axis=0)
-    for i in range(4):
-        packed[i, :PART] = part
-        packed[i, PART:] = sums[...]
-
-
-def merge_kernel(flags, over_z, parts, backward):
-    part = jnp.sum(over_z[:, :PART], axis=0).astype(BF16)
+    packed[:PART] = jnp.sum(parts[...].astype(F32), axis=0)
+    packed[PART:] = sums[...]
+
+
+def merge_kernel(own, one, two, three, parts, backward):
+    total = (own[...] + one[...]) + (two[...] + three[...])
+    part = total[:PART].astype(BF16)
     for i in range(SIDE):
         parts[i] = part
-    first = jnp.where(flags[2] == 0, over_z[0, PART:], over_z[1, PART:])
-    second = jnp.where(flags[2] == 0, over_z[2, PART:], over_z[3, PART:])
-    backward[...] = first + second
+    backward[...] = own[PART:] + two[PART:]
 
 
 def place_kernel(flags, half_grad, grad, grad_v, sem, first):
@@ -275,14 +281,14 @@
 
 
 def conv_kernel(
-    flags, lat, previous, kernel, window, totals, scales, output, tmp, taps, lat_v, kernel_v, window_v, sem
+    flags, lat, near, far, kernel, window, totals, scales, output, tmp, taps, lat_v, kernel_v, window_v, output_v, sem, out_sem
 ):
     from_kernel, from_window, from_lat = copies(
         sem, (kernel, kernel_v), (window, window_v.at[:, HALO * W :]), (lat, lat_v)
     )
     center, inverse = center_inverse(totals, PER)
     for f in range(HALO):
-        blocks = by_row(previous[f], tmp)
+        blocks = by_row(pick(flags[1] == 0, far[f], near[f]), tmp)
         for h in range(H):
             active = jnp.where(flags[0] > 0, activated(blocks[h], center, inverse, scales), 0.0)
             for s, moved in enumerate(shifted(active)):
@@ -303,24 +309,45 @@
     for f in range(1, 3):
         total = total + jnp.dot(taps[f], window_v[:, f * W : (f + T) * W], preferred_element_type=F32)
     from_lat.wait()
+    started = []
     for t in range(T):
         for h in range(H):
             tmp[pl.ds(h, C, stride=H), :] = total[h * C : (h + 1) * C, t * W : (t + 1) * W]
-        output[t] = (lat_v[t].astype(F32) + tmp[...]).astype(BF16)
-
-
-def adjoint_kernel(lat, cot, totals, backward, scaled, result, lat_v, cot_v, scaled_v, sem):
-    started = copies(sem, (lat, lat_v), (cot, cot_v), (scaled, scaled_v))
+        output_v[t] = (lat_v[t].astype(F32) + tmp[...]).astype(BF16)
+        started += copies(out_sem.at[pl.ds(t, 1)], (output_v.at[t], output.at[t]))
+    for copy in started:
+        copy.wait()
+
+
+def adjoint_kernel(
+    lat, cot, totals, backward, scaled, result, lat_v, cot_v, scaled_v, result_v, lat_sem, cot_sem, scaled_sem, out_sem
+):
+    fetched = list(
+        zip(
+            *(
+                copies(sem, *((source.at[t], target.at[t]) for t in range(T)))
+                for sem, source, target in (
+                    (lat_sem, lat, lat_v),
+                    (cot_sem, cot, cot_v),
+                    (scaled_sem, scaled, scaled_v),
+                )
+            )
+        )
+    )
     center, inverse = center_inverse(totals, PER * H)
     row = backward[...][0:1] / MEMBERS
     first = group_column(row, 0, PER * H)
     second = group_column(row, GROUPS, PER * H)
+    started = []
+    for t in range(T):
+        for copy in fetched[t]:
+            copy.wait()
+        unit = (lat_v[t].astype(F32) - center) * inverse
+        value = cot_v[t].astype(F32) + inverse * (scaled_v[t] - first - unit * second)
+        result_v[t] = value.astype(BF16)
+        started += copies(out_sem.at[pl.ds(t, 1)], (result_v.at[t], result.at[t]))
     for copy in started:
         copy.wait()
-    for t in range(T):
-        unit = (lat_v[t].astype(F32) - center) * inverse
-        value = cot_v[t].astype(F32) + inverse * (scaled_v[t] - first - unit * second)
-        result[t] = value.astype(BF16)
 
 
 VMEM, HBM, SMEM = (
@@ -368,9 +395,8 @@
     lat = latents.reshape(T, ROWS, W)
     cot = cotangent.reshape(T, ROWS, W)
     gain, shift = norm_gain.reshape(1, C), norm_shift.reshape(1, C)
-    zh, zm, core = (lax.axis_index(axis) for axis in ("zh", "zm", "core"))
-    flags = jnp.stack([zh * 2 + core, core, zm]).astype(jnp.int32)
-    slab = ("zh", "core")
+    zh, core = lax.axis_index("zh"), lax.axis_index("core")
+    flags = jnp.stack([zh * 2 + core, core]).astype(jnp.int32)
     halo = shape(HALO, ROWS, W, dtype=BF16)
     frames = pltpu.VMEM((T, ROWS, W), BF16)
     tmp = pltpu.VMEM((ROWS, W), F32)
@@ -380,20 +406,23 @@
     kernel_scratch = pltpu.VMEM((27, C, C), BF16)
     scaled_scratch = pltpu.VMEM((T, ROWS, W), F32)
     own = call(start_kernel, shape(8, W), [frames, sems(T)], lat, far=(0,))
-    adj, scales, head, tail = call(
+    gain, own = lax.optimization_barrier((gain, own))
+    adj, scales, to_near, to_far = call(
         prepare_kernel,
         (shape(4 * C, T * PLANE, dtype=BF16), shape(2, C, W), halo, halo),
-        [frames, frames, row, row, tmp, sems(5), sems(1)],
+        [frames, frames, row, row, tmp, sems(4), sems(2)],
+        flags,
         lat,
         cot,
         gain,
         shift,
-        far=(0, 1, 2, 3),
-        out_far=(3,),
+        far=(1, 2, 3, 4),
+        scalars=1,
     )
     across, scales = lax.optimization_barrier((swap(own, "zh"), scales))
     pair = own + across
-    following = lax.ppermute(head, slab, [(i + 1, i) for i in range(SLABS - 1)])
+    far = lax.ppermute(to_far, ("zh", "core"), [(1, 2), (2, 1)])
+    near = swap(to_near, "core")
     totals = jnp.concatenate([pair, swap(pair, "core")], axis=0)
     window, keep, send, last = call(
         grad_kernel,
@@ -410,9 +439,9 @@
         scales,
         out_far=(0,),
         scalars=1,
-        flops=4 * 10**9,
-    )
-    following, last = lax.optimization_barrier((following, last))
+        flops=2 * 10**9,
+    )
+    near, far, last = lax.optimization_barrier((near, far, last))
     keep, send = call(
         edge_kernel,
         (shape(COMM, C), shape(COMM, C)),
@@ -420,7 +449,8 @@
         flags,
         keep,
         send,
-        following,
+        near,
+        far,
         last,
         scalars=1,
         aliases=((1, 0), (2, 1)),
@@ -431,54 +461,61 @@
         back_kernel,
         (shape(T, ROWS, W), shape(8, W)),
         [tmp, window_scratch, taps, frames, frames, kernel_scratch, scaled_scratch, sems(3)],
+        flags,
         lat,
         cot,
-        following,
+        near,
+        far,
         kernel,
         totals,
         scales,
-        far=(0, 1, 3),
+        far=(1, 2, 5),
         out_far=(0,),
+        scalars=1,
         limit=20,
         flops=4 * 10**9,
     )
-    sums, tail = lax.optimization_barrier((sums, tail))
-    previous = lax.ppermute(tail, slab, [(i, i + 1) for i in range(SLABS - 1)])
     sums = sums + swap(sums, "core")
-    packed = call(part_kernel, shape(4, PART + 8, C), [], parts, sums)
+    packed = call(part_kernel, shape(PART + 8, C), [], parts, sums)
+    others = [lax.ppermute(packed, ("zh", "zm"), [(i, i ^ flip) for i in range(4)]) for flip in (1, 2, 3)]
+    part, backward = call(
+        merge_kernel, (shape(SIDE, PART, C, dtype=BF16), shape(8, C)), [], packed, *others
+    )
+    part, window = lax.optimization_barrier((part, window))
     output = call(
         conv_kernel,
         shape(T, ROWS, W, dtype=BF16),
-        [tmp, taps, frames, kernel_scratch, window_scratch, sems(3)],
+        [tmp, taps, frames, kernel_scratch, window_scratch, frames, sems(3), sems(T)],
         flags,
         lat,
-        previous,
+        near,
+        far,
         kernel,
         window,
         totals,
         scales,
-        far=(1, 3, 4),
+        far=(1, 4, 5),
+        out_far=(0,),
         limit=20,
         scalars=1,
         flops=4 * 10**9,
     )
-    over_z, output = lax.optimization_barrier((exchange(packed, ("zh", "zm")), output))
-    part, backward = call(
-        merge_kernel, (shape(SIDE, PART, C, dtype=BF16), shape(8, C)), [], flags, over_z, scalars=1
-    )
     result = call(
         adjoint_kernel,
         shape(T, ROWS, W, dtype=BF16),
-        [frames, frames, scaled_scratch, sems(3)],
+        [frames, frames, scaled_scratch, frames, sems(T), sems(T), sems(T), sems(T)],
         lat,
         cot,
         totals,
         backward,
         scaled,
         far=(0, 1, 4),
+        out_far=(0,),
         flops=10**9,
     )
-    mine, result = lax.optimization_barrier((exchange(part, ("y", "zn", "x")).reshape(COMM, C), result))
+    mine, output, result = lax.optimization_barrier(
+        (exchange(part, ("y", "zn", "x")).reshape(COMM, C), output, result)
+    )
     other = swap(mine, "core")
     half_scratch = [pltpu.VMEM((27, C // 2, C), F32), sems(3)]
     kernel_grad = call(

time: 90 us -> 87.7 us (0.974)
  waiting for transfers between devices: 20.5 us -> 15.8 us
  starting transfers between devices: 38.9 us -> 42 us
    ppermute x2 -> x4, starting transfers between devices: 4.89 us -> 12.6 us  [the longest x1 6.83 us: per_device(): far = lax.ppermute(to_far, ('zh', 'core'), [(1, 2), (2, 1)])]
    all_to_all x3 -> x2, waiting for transfers between devices: 11.7 us -> 6.82 us  [exchange(): return lax.all_to_all(parts, axes, 0, 0)]
    all_to_all x3 -> x2, starting transfers between devices: 19.2 us -> 16.3 us  [exchange(): return lax.all_to_all(parts, axes, 0, 0)]
    ppermute x5 -> x6, starting transfers between devices: 14.8 us -> 13.1 us  [swap(): return lax.ppermute(value, axis, [(0, 1), (1, 0)])]
    ppermute x2 -> x4, waiting for transfers between devices: 4.36 us -> 5.72 us  [the longest x3 4.06 us: per_device(): lax.ppermute(packed, ('zh', 'zm'), [(i, i ^ flip) for i in range(4)])]
    ppermute x5 -> x6, waiting for transfers between devices: 4.45 us -> 3.29 us  [swap(): return lax.ppermute(value, axis, [(0, 1), (1, 0)])]
  transfers between devices with their start and end apart: 10 -> 12, of which waited for: 7 -> 6; matrix products, arithmetic and copies ran while one was open for 0% -> 0% of each run, Pallas kernels for 25% -> 25%
where the time goes in v6:
time: 87.7 us; the launch traced here: 87.3 us
  starting transfers between devices  42 us (48%)
  Pallas kernels  28.4 us (32%)
  waiting for transfers between devices  15.8 us (18%)
  between operations  0.94 us (1%)
    pallas_call x12, Pallas kernels, call(): pl.pallas_call(body, out_shape=shapes[0] if single else shapes, in_specs=...  28.4 us
    all_to_all x2, starting transfers between devices, exchange(): return lax.all_to_all(parts, axes, 0, 0)  16.3 us
    ppermute x6, starting transfers between devices, swap(): return lax.ppermute(value, axis, [(0, 1), (1, 0)])  13.1 us
    ppermute x1, starting transfers between devices, per_device(): far = lax.ppermute(to_far, ('zh', 'core'), [(1, 2), (2, 1)])  6.83 us
    all_to_all x2, waiting for transfers between devices, exchange(): return lax.all_to_all(parts, axes, 0, 0)  6.82 us
    ppermute x3, starting transfers between devices, per_device(): lax.ppermute(packed, ('zh', 'zm'), [(i, i ^ flip) for i in range(4)])  5.74 us
    ppermute x3, waiting for transfers between devices, per_device(): lax.ppermute(packed, ('zh', 'zm'), [(i, i ^ flip) for i in range(4)])  4.06 us
    ppermute x6, waiting for transfers between devices, swap(): return lax.ppermute(value, axis, [(0, 1), (1, 0)])  3.29 us
  transfers between devices with their start and end apart: 12, of which 6 were waited for; matrix products, arithmetic and copies ran while one was open for 0% of the time, Pallas kernels for 25%

profile of v6, /device:TPU:1, one launch (start us, length us, event | category | flops | bytes accessed | tf_op | source)
XLA Modules:
  0.0 87.3 jit_solution(16189993643991480964)
XLA Ops:
  0.6 1.3 %shard_map.76 = f32[8,128]{1,0:T(8,128)S(1)} custom-call(bf16[4,512,128]{2,1,0:T(8,128)(2,1)} %bitcast.12), custom_call_target="tpu_custom_call" | custom-call | bytes 1048576 | tf_op jit(solution)/shard_map/pallas_call | solution.py:366
  2.0 7.8 %collective-permute-start = (f32[8,128]{1,0:T(8,128)S(1)}, f32[8,128]{1,0:T(8,128)S(1)}, u32[]{:S(2)}, u32[]{:S(2)}) collective-permute-start(f32[8,128]{1,0:T(8,128)S(1)} %shard_map.76), channel_id=1, source_target_pairs={{0,128},{128,0},{1,129},{129,1},{2,130},{130,2},{3,131},{131,3},{4... | collective-permute-start | bytes 12296 | tf_op jit(solution)/shard_map/ppermute | solution.py:387
  9.8 0.1 pad_add_fusion.flags
  9.9 2.3 %shard_map.77 = (bf16[512,2048]{1,0:T(8,128)(2,1)S(1)}, f32[2,128,128]{2,1,0:T(8,128)S(1)}, bf16[2,512,128]{2,1,0:T(8,128)(2,1)S(1)}, bf16[2,512,128]{2,1,0:T(8,128)(2,1)S(1)}) custom-call(s32[2]{0:T(128)S(1)} %pad_add_fusion.flags, bf16[4,512,128]{2,1,0:T(8,128)(2,1)} %bitcast.13, bf16[4,512,128]{2,1,0:T(8,128)(2,1)} %bitcast.17, f32[1,128]{1,0:T(1,128)} %bitcast.20, ...), custom_call_target="tpu_custom_call" | custom-call | bytes 1048576 | tf_op jit(solution)/shard_map/pallas_call | solution.py:366
  12.2 0.0 collective-permute-done
  12.2 1.2 %collective-permute-start.1 = (f32[8,128]{1,0:T(8,128)S(1)}, f32[8,128]{1,0:T(8,128)S(1)}, u32[]{:S(2)}, u32[]{:S(2)}) collective-permute-start(f32[8,128]{1,0:T(8,128)S(1)} %add.10), channel_id=1, source_target_pairs={{0,64},{64,0},{1,65},{65,1},{2,66},{66,2},{3,67},{67,3},{4,68},{68... | collective-permute-start | bytes 12296 | tf_op jit(solution)/shard_map/ppermute | solution.py:387
  13.3 0.1 collective-permute-start.2
  13.4 6.8 %collective-permute-start.3 = (bf16[2,512,128]{2,1,0:T(8,128)(2,1)S(1)}, bf16[2,512,128]{2,1,0:T(8,128)(2,1)S(1)}, u32[]{:S(2)}, u32[]{:S(2)}) collective-permute-start(bf16[2,512,128]{2,1,0:T(8,128)(2,1)S(1)} %get-tuple-element.38), channel_id=1, source_target_pairs={{64,128},{128,64},{65,129},{129,65},{66,130},{130,66},{67,131},{13... | collective-permute-start | bytes 786440 | tf_op jit(solution)/shard_map/ppermute | solution.py:424
  20.3 0.0 collective-permute-done.1
  20.3 3.1 %shard_map.78 = (bf16[1536,512]{1,0:T(8,128)(2,1)}, f32[1792,128]{1,0:T(8,128)S(1)}, f32[1792,128]{1,0:T(8,128)S(1)}, bf16[384,1024]{1,0:T(8,128)(2,1)S(1)}) custom-call(s32[2]{0:T(128)S(1)} %pad_add_fusion.flags, bf16[512,2048]{1,0:T(8,128)(2,1)S(1)} %get-tuple-element.30.adj, f32[16,128]{1,0:T(8,128)S(1)} %pad_maximum_fusion.totals, ...), custom_call_target="tpu_custom_call" | custom-call | flops 2000000000 | bytes 1048576 | tf_op jit(solution)/shard_map/pallas_call | solution.py:366
  23.5 0.0 collective-permute-done.2.near
  23.5 1.7 %collective-permute-done.3.far = bf16[2,512,128]{2,1,0:T(8,128)(2,1)S(1)} collective-permute-done((bf16[2,512,128]{2,1,0:T(8,128)(2,1)S(1)}, bf16[2,512,128]{2,1,0:T(8,128)(2,1)S(1)}, u32[]{:S(2)}, u32[]{:S(2)}) %collective-permute-start.3) | collective-permute-done | bytes 262176 | tf_op jit(solution)/shard_map/ppermute | solution.py:424
  25.1 1.4 %shard_map.79 = (f32[1792,128]{1,0:T(8,128)S(1)}, f32[1792,128]{1,0:T(8,128)S(1)}) custom-call(s32[2]{0:T(128)S(1)} %pad_add_fusion.flags, f32[1792,128]{1,0:T(8,128)S(1)} %get-tuple-element.35.keep_in, f32[1792,128]{1,0:T(8,128)S(1)} %get-tuple-element.36.send_in, ...), custom_call_target="tpu_custom_call", output_to_operand_aliasing={{0}: (1, {}), {1}: (2, {})} | custom-call | bytes 1048576 | tf_op jit(solution)/shard_map/pallas_call | solution.py:366
  26.6 0.1 collective-permute-start.4
  26.7 2.5 %collective-permute-done.4.received = f32[1792,128]{1,0:T(8,128)S(1)} collective-permute-done((f32[1792,128]{1,0:T(8,128)S(1)}, f32[1792,128]{1,0:T(8,128)S(1)}, u32[]{:S(2)}, u32[]{:S(2)}) %collective-permute-start.4) | collective-permute-done | bytes 917536 | tf_op jit(solution)/shard_map/ppermute | solution.py:387
  29.1 1.1 %shard_map.80 = f32[1792,128]{1,0:T(8,128)} custom-call(f32[1792,128]{1,0:T(8,128)S(1)} %get-tuple-element.43.keep, f32[1792,128]{1,0:T(8,128)S(1)} %collective-permute-done.4.received), custom_call_target="tpu_custom_call" | custom-call | bytes 1048576 | tf_op jit(solution)/shard_map/pallas_call | solution.py:366
  30.2 10.2 %all-to-all-start = ((f32[32,56,128]{2,1,0:T(8,128)}), f32[32,56,128]{2,1,0:T(8,128)S(1)}, u32[]{:S(2)}, u32[]{:S(2)}) async-start(f32[32,56,128]{2,1,0:T(8,128)} %bitcast.6), calls=%async_computation | async-start | bytes 1835008 | tf_op jit(solution)/shard_map/all_to_all | solution.py:391
  40.5 6.9 %shard_map.81 = (f32[4,512,128]{2,1,0:T(8,128)}, f32[8,128]{1,0:T(8,128)S(1)}) custom-call(s32[2]{0:T(128)S(1)} %pad_add_fusion.flags, bf16[4,512,128]{2,1,0:T(8,128)(2,1)} %bitcast.14, bf16[4,512,128]{2,1,0:T(8,128)(2,1)} %bitcast.18, bf16[2,512,128]{2,1,0:T(8,128)(2,1)S(1)} %collective-permute-done.2.near, ...), custom_call_target="tpu_custom_call" | custom-call | flops 4000000000 | bytes 1048576 | tf_op jit(solution)/shard_map/pallas_call | solution.py:366
  47.4 0.5 collective-permute-start.5
  47.9 0.8 collective-permute-done.5
  48.7 6.4 %all-to-all-done.parts = f32[32,56,128]{2,1,0:T(8,128)S(1)} async-done(((f32[32,56,128]{2,1,0:T(8,128)}), f32[32,56,128]{2,1,0:T(8,128)S(1)}, u32[]{:S(2)}, u32[]{:S(2)}) %all-to-all-start) | async-done | bytes 917536 | tf_op jit(solution)/shard_map/all_to_all | solution.py:391
  55.1 0.1 shard_map.82.own
  55.2 3.1 %collective-permute-start.8 = (f32[64,128]{1,0:T(8,128)S(1)}, f32[64,128]{1,0:T(8,128)S(1)}, u32[]{:S(2)}, u32[]{:S(2)}) collective-permute-start(f32[64,128]{1,0:T(8,128)S(1)} %shard_map.82.own), channel_id=1, source_target_pairs={{0,136},{8,128},{128,8},{136,0},{1,137},{9,129},{129,9},{137,1},{2... | collective-permute-start | bytes 98312 | tf_op jit(solution)/shard_map/ppermute | solution.py:480
  58.3 1.4 %collective-permute-start.7 = (f32[64,128]{1,0:T(8,128)S(1)}, f32[64,128]{1,0:T(8,128)S(1)}, u32[]{:S(2)}, u32[]{:S(2)}) collective-permute-start(f32[64,128]{1,0:T(8,128)S(1)} %shard_map.82.own), channel_id=1, source_target_pairs={{0,128},{8,136},{128,0},{136,8},{1,129},{9,137},{129,1},{137,9},{2... | collective-permute-start | bytes 98312 | tf_op jit(solution)/shard_map/ppermute | solution.py:480
  59.7 1.2 %collective-permute-start.6 = (f32[64,128]{1,0:T(8,128)S(1)}, f32[64,128]{1,0:T(8,128)S(1)}, u32[]{:S(2)}, u32[]{:S(2)}) collective-permute-start(f32[64,128]{1,0:T(8,128)S(1)} %shard_map.82.own), channel_id=1, source_target_pairs={{0,8},{8,0},{128,136},{136,128},{1,9},{9,1},{129,137},{137,129},{2... | collective-permute-start | bytes 98312 | tf_op jit(solution)/shard_map/ppermute | solution.py:480
  60.9 0.0 collective-permute-done.8.three
  60.9 4.1 %collective-permute-done.7.two = f32[64,128]{1,0:T(8,128)S(1)} collective-permute-done((f32[64,128]{1,0:T(8,128)S(1)}, f32[64,128]{1,0:T(8,128)S(1)}, u32[]{:S(2)}, u32[]{:S(2)}) %collective-permute-start.7) | collective-permute-done | bytes 32800 | tf_op jit(solution)/shard_map/ppermute | solution.py:480
  65.0 0.0 collective-permute-done.6.one
  65.0 0.9 shard_map.83
  65.8 6.0 %all-to-all-start.1 = ((bf16[32,56,128]{2,1,0:T(8,128)(2,1)}), bf16[32,56,128]{2,1,0:T(8,128)(2,1)S(1)}, u32[]{:S(2)}, u32[]{:S(2)}) async-start(bf16[32,56,128]{2,1,0:T(8,128)(2,1)} %get-tuple-element.48), calls=%async_computation.1 | async-start | bytes 917504 | tf_op jit(solution)/shard_map/all_to_all | solution.py:391
  71.9 2.6 %shard_map.85 = bf16[4,512,128]{2,1,0:T(8,128)(2,1)} custom-call(bf16[4,512,128]{2,1,0:T(8,128)(2,1)} %bitcast.15, bf16[4,512,128]{2,1,0:T(8,128)(2,1)} %bitcast.19, f32[16,128]{1,0:T(8,128)S(1)} %pad_maximum_fusion.totals, f32[8,128]{1,0:T(8,128)S(1)} %get-tuple-element.50.backward, f32[4,512,128]{2,1,0:T(8,128)} %get-tuple-element.51.scaled), custom_call_target="tpu_custom_call" | custom-call | flops 1000000000 | bytes 1048576 | tf_op jit(solution)/shard_map/pallas_call | solution.py:366
  74.4 5.8 %shard_map.84 = bf16[4,512,128]{2,1,0:T(8,128)(2,1)} custom-call(s32[2]{0:T(128)S(1)} %pad_add_fusion.flags, bf16[4,512,128]{2,1,0:T(8,128)(2,1)} %bitcast.16, bf16[2,512,128]{2,1,0:T(8,128)(2,1)S(1)} %collective-permute-done.2.near, bf16[2,512,128]{2,1,0:T(8,128)(2,1)S(1)} %collective-permute-done.3.far, bf16[27,128,128]{2,1,0:T(8,128)(2,1)} %kernel.3, ...), custom_call_target="tpu_custom_call" | custom-call | flops 4000000000 | bytes 1048576 | tf_op jit(solution)/shard_map/pallas_call | solution.py:366
  80.2 0.5 all-to-all-done.1
  80.7 3.4 %collective-permute-start.9 = (bf16[1792,128]{1,0:T(8,128)(2,1)S(1)}, bf16[1792,128]{1,0:T(8,128)(2,1)S(1)}, u32[]{:S(2)}, u32[]{:S(2)}) collective-permute-start(bf16[1792,128]{1,0:T(8,128)(2,1)S(1)} %bitcast.10), channel_id=1, source_target_pairs={{0,64},{64,0},{1,65},{65,1},{2,66},{66,2},{3,67},{67,3},{4,68},{68... | collective-permute-start | bytes 1376264 | tf_op jit(solution)/shard_map/ppermute | solution.py:387
  84.1 1.5 %shard_map.86.grad_in = f32[27,128,128]{2,1,0:T(8,128)} custom-call(s32[2]{0:T(128)S(1)} %pad_add_fusion.flags, bf16[1792,128]{1,0:T(8,128)(2,1)S(1)} %bitcast.11), custom_call_target="tpu_custom_call" | custom-call | flops 1000000000 | bytes 1048576 | tf_op jit(solution)/shard_map/pallas_call | solution.py:366
  85.6 0.0 collective-permute-done.9.half_grad
  85.6 1.5 %shard_map.87 = f32[27,128,128]{2,1,0:T(8,128)} custom-call(s32[2]{0:T(128)S(1)} %pad_add_fusion.flags, bf16[1792,128]{1,0:T(8,128)(2,1)S(1)} %collective-permute-done.9.half_grad, f32[27,128,128]{2,1,0:T(8,128)} %shard_map.86.grad_in), custom_call_target="tpu_custom_call", output_to_operand_aliasing={{}: (2, {})} | custom-call | bytes 1048576 | tf_op jit(solution)/shard_map/pallas_call | solution.py:366
  (3 shorter events, 0.0 us)
Async XLA Ops:
  2.0 10.2 %collective-permute-start = (f32[8,128]{1,0:T(8,128)S(1)}, f32[8,128]{1,0:T(8,128)S(1)}, u32[]{:S(2)}, u32[]{:S(2)}) collective-permute-start(f32[8,128]{1,0:T(8,128)S(1)} %shard_map.76), channel_id=1, source_target_pairs={{0,128},{128,0},{1,129},{129,1},{2,130},{130,2},{3,131},{131,3},{4... | collective-permute-start | bytes 12296 | tf_op jit(solution)/shard_map/ppermute | solution.py:387
  12.2 8.1 %collective-permute-start.1 = (f32[8,128]{1,0:T(8,128)S(1)}, f32[8,128]{1,0:T(8,128)S(1)}, u32[]{:S(2)}, u32[]{:S(2)}) collective-permute-start(f32[8,128]{1,0:T(8,128)S(1)} %add.10), channel_id=1, source_target_pairs={{0,64},{64,0},{1,65},{65,1},{2,66},{66,2},{3,67},{67,3},{4,68},{68... | collective-permute-start | bytes 12296 | tf_op jit(solution)/shard_map/ppermute | solution.py:387
  13.3 10.1 %collective-permute-start.2 = (bf16[2,512,128]{2,1,0:T(8,128)(2,1)S(1)}, bf16[2,512,128]{2,1,0:T(8,128)(2,1)S(1)}, u32[]{:S(2)}, u32[]{:S(2)}) collective-permute-start(bf16[2,512,128]{2,1,0:T(8,128)(2,1)S(1)} %get-tuple-element.37), channel_id=1, source_target_pairs={{0,64},{64,0},{1,65},{65,1},{2,66},{66,2},{3,67},{67,3},{4,68},{68... | collective-permute-start | bytes 786440 | tf_op jit(solution)/shard_map/ppermute | solution.py:387
  13.4 11.7 %collective-permute-start.3 = (bf16[2,512,128]{2,1,0:T(8,128)(2,1)S(1)}, bf16[2,512,128]{2,1,0:T(8,128)(2,1)S(1)}, u32[]{:S(2)}, u32[]{:S(2)}) collective-permute-start(bf16[2,512,128]{2,1,0:T(8,128)(2,1)S(1)} %get-tuple-element.38), channel_id=1, source_target_pairs={{64,128},{128,64},{65,129},{129,65},{66,130},{130,66},{67,131},{13... | collective-permute-start | bytes 786440 | tf_op jit(solution)/shard_map/ppermute | solution.py:424
  26.6 2.6 %collective-permute-start.4 = (f32[1792,128]{1,0:T(8,128)S(1)}, f32[1792,128]{1,0:T(8,128)S(1)}, u32[]{:S(2)}, u32[]{:S(2)}) collective-permute-start(f32[1792,128]{1,0:T(8,128)S(1)} %get-tuple-element.44), channel_id=1, source_target_pairs={{0,64},{64,0},{1,65},{65,1},{2,66},{66,2},{3,67},{67,3},{4,68},{68... | collective-permute-start | bytes 2752520 | tf_op jit(solution)/shard_map/ppermute | solution.py:387
  30.2 24.9 %all-to-all-start = ((f32[32,56,128]{2,1,0:T(8,128)}), f32[32,56,128]{2,1,0:T(8,128)S(1)}, u32[]{:S(2)}, u32[]{:S(2)}) async-start(f32[32,56,128]{2,1,0:T(8,128)} %bitcast.6), calls=%async_computation | async-start | bytes 1835008 | tf_op jit(solution)/shard_map/all_to_all | solution.py:391
  47.4 1.3 %collective-permute-start.5 = (f32[8,128]{1,0:T(8,128)S(1)}, f32[8,128]{1,0:T(8,128)S(1)}, u32[]{:S(2)}, u32[]{:S(2)}) collective-permute-start(f32[8,128]{1,0:T(8,128)S(1)} %get-tuple-element.45), channel_id=1, source_target_pairs={{0,64},{64,0},{1,65},{65,1},{2,66},{66,2},{3,67},{67,3},{4,68},{68... | collective-permute-start | bytes 12296 | tf_op jit(solution)/shard_map/ppermute | solution.py:387
  55.2 5.7 %collective-permute-start.8 = (f32[64,128]{1,0:T(8,128)S(1)}, f32[64,128]{1,0:T(8,128)S(1)}, u32[]{:S(2)}, u32[]{:S(2)}) collective-permute-start(f32[64,128]{1,0:T(8,128)S(1)} %shard_map.82.own), channel_id=1, source_target_pairs={{0,136},{8,128},{128,8},{136,0},{1,137},{9,129},{129,9},{137,1},{2... | collective-permute-start | bytes 98312 | tf_op jit(solution)/shard_map/ppermute | solution.py:480
  58.3 6.7 %collective-permute-start.7 = (f32[64,128]{1,0:T(8,128)S(1)}, f32[64,128]{1,0:T(8,128)S(1)}, u32[]{:S(2)}, u32[]{:S(2)}) collective-permute-start(f32[64,128]{1,0:T(8,128)S(1)} %shard_map.82.own), channel_id=1, source_target_pairs={{0,128},{8,136},{128,0},{136,8},{1,129},{9,137},{129,1},{137,9},{2... | collective-permute-start | bytes 98312 | tf_op jit(solution)/shard_map/ppermute | solution.py:480
  59.7 5.2 %collective-permute-start.6 = (f32[64,128]{1,0:T(8,128)S(1)}, f32[64,128]{1,0:T(8,128)S(1)}, u32[]{:S(2)}, u32[]{:S(2)}) collective-permute-start(f32[64,128]{1,0:T(8,128)S(1)} %shard_map.82.own), channel_id=1, source_target_pairs={{0,8},{8,0},{128,136},{136,128},{1,9},{9,1},{129,137},{137,129},{2... | collective-permute-start | bytes 98312 | tf_op jit(solution)/shard_map/ppermute | solution.py:480
  65.8 14.9 %all-to-all-start.1 = ((bf16[32,56,128]{2,1,0:T(8,128)(2,1)}), bf16[32,56,128]{2,1,0:T(8,128)(2,1)S(1)}, u32[]{:S(2)}, u32[]{:S(2)}) async-start(bf16[32,56,128]{2,1,0:T(8,128)(2,1)} %get-tuple-element.48), calls=%async_computation.1 | async-start | bytes 917504 | tf_op jit(solution)/shard_map/all_to_all | solution.py:391
  80.7 4.9 %collective-permute-start.9 = (bf16[1792,128]{1,0:T(8,128)(2,1)S(1)}, bf16[1792,128]{1,0:T(8,128)(2,1)S(1)}, u32[]{:S(2)}, u32[]{:S(2)}) collective-permute-start(bf16[1792,128]{1,0:T(8,128)(2,1)S(1)} %bitcast.10), channel_id=1, source_target_pairs={{0,64},{64,0},{1,65},{65,1},{2,66},{66,2},{3,67},{67,3},{4,68},{68... | collective-permute-start | bytes 1376264 | tf_op jit(solution)/shard_map/ppermute | solution.py:387

commit v7 on v6

--- a/solution.py
+++ b/solution.py
@@ -124,6 +124,17 @@
     pltpu.make_async_copy(head, far, halo_sem.at[1]).wait()
 
 
+def clear(taps):
+    zero = jnp.zeros((C, C), BF16)
+    for f in range(3):
+        for s in range(3):
+            for h in range(H):
+                for other in range(H):
+                    if abs(h - other) > 1:
+                        at = (s * H + other) * C
+                        taps[f, h * C : (h + 1) * C, at : at + C] = zero
+
+
 def pick(condition, first, second):
     return jnp.where(condition, first.astype(F32), second.astype(F32))
 
@@ -144,7 +155,7 @@
             for s, moved in enumerate(shifted(blocks[h])):
                 at = (s * H + h) * C
                 window[at : at + C, f * W : (f + 1) * W] = moved.astype(BF16)
-    taps[...] = jnp.zeros_like(taps)
+    clear(taps)
     from_kernel.wait()
     for kt in range(3):
         for ki in range(3):
@@ -293,7 +304,7 @@
             active = jnp.where(flags[0] > 0, activated(blocks[h], center, inverse, scales), 0.0)
             for s, moved in enumerate(shifted(active)):
                 window_v[(s * H + h) * C : (s * H + h + 1) * C, f * W : (f + 1) * W] = moved.astype(BF16)
-    taps[...] = jnp.zeros_like(taps)
+    clear(taps)
     from_kernel.wait()
     for kt in range(3):
         for ki in range(3):
@@ -419,9 +430,12 @@
         far=(1, 2, 3, 4),
         scalars=1,
     )
+    slab = ("zh", "core")
+    before = lax.ppermute(to_far, slab, [(1, 2), (2, 1)])
+    far = before
     across, scales = lax.optimization_barrier((swap(own, "zh"), scales))
     pair = own + across
-    far = lax.ppermute(to_far, ("zh", "core"), [(1, 2), (2, 1)])
+    to_near, pair = lax.optimization_barrier((to_near, pair))
     near = swap(to_near, "core")
     totals = jnp.concatenate([pair, swap(pair, "core")], axis=0)
     window, keep, send, last = call(

time: 87.7 us -> 84.3 us (0.961)
  starting transfers between devices: 42 us -> 36.6 us
  waiting for transfers between devices: 15.8 us -> 18 us
    ppermute x1, starting transfers between devices: 6.83 us -> 3.07 us  [per_device(): before = lax.ppermute(to_far, slab, [(1, 2), (2, 1)])]
    ppermute x1, waiting for transfers between devices: 1.66 us -> 4.6 us  [per_device(): before = lax.ppermute(to_far, slab, [(1, 2), (2, 1)])]
    ppermute x3, waiting for transfers between devices: 4.06 us -> 2.55 us  [per_device(): lax.ppermute(packed, ('zh', 'zm'), [(i, i ^ flip) for i in range(4)])]
    all_to_all x2, starting transfers between devices: 16.3 us -> 15 us  [exchange(): return lax.all_to_all(parts, axes, 0, 0)]
  transfers between devices with their start and end apart: 12 -> 12, of which waited for: 6 -> 8; matrix products, arithmetic and copies ran while one was open for 0% -> 0% of each run, Pallas kernels for 25% -> 26%
where the time goes in v7:
time: 84.3 us; the launch traced here: 83.9 us
  starting transfers between devices  36.6 us (43%)
  Pallas kernels  28.3 us (34%)
  waiting for transfers between devices  18 us (21%)
  between operations  0.94 us (1%)
    pallas_call x12, Pallas kernels, call(): pl.pallas_call(body, out_shape=shapes[0] if single else shapes, in_specs=...  28.3 us
    all_to_all x2, starting transfers between devices, exchange(): return lax.all_to_all(parts, axes, 0, 0)  15 us
    ppermute x6, starting transfers between devices, swap(): return lax.ppermute(value, axis, [(0, 1), (1, 0)])  12.7 us
    all_to_all x2, waiting for transfers between devices, exchange(): return lax.all_to_all(parts, axes, 0, 0)  6.89 us
    ppermute x3, starting transfers between devices, per_device(): lax.ppermute(packed, ('zh', 'zm'), [(i, i ^ flip) for i in range(4)])  5.74 us
    ppermute x1, waiting for transfers between devices, per_device(): before = lax.ppermute(to_far, slab, [(1, 2), (2, 1)])  4.6 us
    ppermute x6, waiting for transfers between devices, swap(): return lax.ppermute(value, axis, [(0, 1), (1, 0)])  3.94 us
    ppermute x1, starting transfers between devices, per_device(): before = lax.ppermute(to_far, slab, [(1, 2), (2, 1)])  3.07 us
  transfers between devices with their start and end apart: 12, of which 8 were waited for; matrix products, arithmetic and copies ran while one was open for 0% of the time, Pallas kernels for 26%

profile of v7, /device:TPU:1, one launch (start us, length us, event | category | flops | bytes accessed | tf_op | source)
XLA Modules:
  0.0 83.9 jit_solution(15879327767700878861)
XLA Ops:
  0.6 1.3 %shard_map.76 = f32[8,128]{1,0:T(8,128)S(1)} custom-call(bf16[4,512,128]{2,1,0:T(8,128)(2,1)} %bitcast.12), custom_call_target="tpu_custom_call" | custom-call | bytes 1048576 | tf_op jit(solution)/shard_map/pallas_call | solution.py:377
  2.0 7.8 %collective-permute-start = (f32[8,128]{1,0:T(8,128)S(1)}, f32[8,128]{1,0:T(8,128)S(1)}, u32[]{:S(2)}, u32[]{:S(2)}) collective-permute-start(f32[8,128]{1,0:T(8,128)S(1)} %shard_map.76), channel_id=1, source_target_pairs={{0,128},{128,0},{1,129},{129,1},{2,130},{130,2},{3,131},{131,3},{4... | collective-permute-start | bytes 12296 | tf_op jit(solution)/shard_map/ppermute | solution.py:398
  9.8 0.1 pad_add_fusion.flags
  9.9 2.3 %shard_map.77 = (bf16[512,2048]{1,0:T(8,128)(2,1)S(1)}, f32[2,128,128]{2,1,0:T(8,128)S(1)}, bf16[2,512,128]{2,1,0:T(8,128)(2,1)S(1)}, bf16[2,512,128]{2,1,0:T(8,128)(2,1)S(1)}) custom-call(s32[2]{0:T(128)S(1)} %pad_add_fusion.flags, bf16[4,512,128]{2,1,0:T(8,128)(2,1)} %bitcast.13, bf16[4,512,128]{2,1,0:T(8,128)(2,1)} %bitcast.17, f32[1,128]{1,0:T(1,128)} %bitcast.20, ...), custom_call_target="tpu_custom_call" | custom-call | bytes 1048576 | tf_op jit(solution)/shard_map/pallas_call | solution.py:377
  12.2 3.1 %collective-permute-start.3 = (bf16[2,512,128]{2,1,0:T(8,128)(2,1)S(1)}, bf16[2,512,128]{2,1,0:T(8,128)(2,1)S(1)}, u32[]{:S(2)}, u32[]{:S(2)}) collective-permute-start(bf16[2,512,128]{2,1,0:T(8,128)(2,1)S(1)} %get-tuple-element.42), channel_id=1, source_target_pairs={{64,128},{128,64},{65,129},{129,65},{66,130},{130,66},{67,131},{13... | collective-permute-start | bytes 786440 | tf_op jit(solution)/shard_map/ppermute | solution.py:434
  15.2 0.0 collective-permute-done
  15.3 0.1 collective-permute-start.1
  15.4 0.5 collective-permute-start.2
  15.9 0.7 collective-permute-done.1
  16.5 3.1 %shard_map.78 = (bf16[1536,512]{1,0:T(8,128)(2,1)}, f32[1792,128]{1,0:T(8,128)S(1)}, f32[1792,128]{1,0:T(8,128)S(1)}, bf16[384,1024]{1,0:T(8,128)(2,1)S(1)}) custom-call(s32[2]{0:T(128)S(1)} %pad_add_fusion.flags, bf16[512,2048]{1,0:T(8,128)(2,1)S(1)} %get-tuple-element.32.adj, f32[16,128]{1,0:T(8,128)S(1)} %constant_dynamic-update-slice_fusion.totals, ...), custom_call_target="tpu_custom_call" | custom-call | flops 2000000000 | bytes 1048576 | tf_op jit(solution)/shard_map/pallas_call | solution.py:377
  19.7 4.6 %collective-permute-done.3.far = bf16[2,512,128]{2,1,0:T(8,128)(2,1)S(1)} collective-permute-done((bf16[2,512,128]{2,1,0:T(8,128)(2,1)S(1)}, bf16[2,512,128]{2,1,0:T(8,128)(2,1)S(1)}, u32[]{:S(2)}, u32[]{:S(2)}) %collective-permute-start.3) | collective-permute-done | bytes 262176 | tf_op jit(solution)/shard_map/ppermute | solution.py:434
  24.3 0.0 collective-permute-done.2.near
  24.3 1.4 %shard_map.79 = (f32[1792,128]{1,0:T(8,128)S(1)}, f32[1792,128]{1,0:T(8,128)S(1)}) custom-call(s32[2]{0:T(128)S(1)} %pad_add_fusion.flags, f32[1792,128]{1,0:T(8,128)S(1)} %get-tuple-element.39.keep_in, f32[1792,128]{1,0:T(8,128)S(1)} %get-tuple-element.40.send_in, ...), custom_call_target="tpu_custom_call", output_to_operand_aliasing={{0}: (1, {}), {1}: (2, {})} | custom-call | bytes 1048576 | tf_op jit(solution)/shard_map/pallas_call | solution.py:377
  25.7 0.1 collective-permute-start.4
  25.8 2.5 %collective-permute-done.4.received = f32[1792,128]{1,0:T(8,128)S(1)} collective-permute-done((f32[1792,128]{1,0:T(8,128)S(1)}, f32[1792,128]{1,0:T(8,128)S(1)}, u32[]{:S(2)}, u32[]{:S(2)}) %collective-permute-start.4) | collective-permute-done | bytes 917536 | tf_op jit(solution)/shard_map/ppermute | solution.py:398
  28.3 1.1 %shard_map.80 = f32[1792,128]{1,0:T(8,128)} custom-call(f32[1792,128]{1,0:T(8,128)S(1)} %get-tuple-element.47.keep, f32[1792,128]{1,0:T(8,128)S(1)} %collective-permute-done.4.received), custom_call_target="tpu_custom_call" | custom-call | bytes 1048576 | tf_op jit(solution)/shard_map/pallas_call | solution.py:377
  29.4 9.8 %all-to-all-start = ((f32[32,56,128]{2,1,0:T(8,128)}), f32[32,56,128]{2,1,0:T(8,128)S(1)}, u32[]{:S(2)}, u32[]{:S(2)}) async-start(f32[32,56,128]{2,1,0:T(8,128)} %bitcast.6), calls=%async_computation | async-start | bytes 1835008 | tf_op jit(solution)/shard_map/all_to_all | solution.py:402
  39.2 6.8 %shard_map.81 = (f32[4,512,128]{2,1,0:T(8,128)}, f32[8,128]{1,0:T(8,128)S(1)}) custom-call(s32[2]{0:T(128)S(1)} %pad_add_fusion.flags, bf16[4,512,128]{2,1,0:T(8,128)(2,1)} %bitcast.14, bf16[4,512,128]{2,1,0:T(8,128)(2,1)} %bitcast.18, bf16[2,512,128]{2,1,0:T(8,128)(2,1)S(1)} %collective-permute-done.2.near, ...), custom_call_target="tpu_custom_call" | custom-call | flops 4000000000 | bytes 1048576 | tf_op jit(solution)/shard_map/pallas_call | solution.py:377
  46.0 0.5 collective-permute-start.5
  46.5 0.8 collective-permute-done.5
  47.3 6.4 %all-to-all-done.parts = f32[32,56,128]{2,1,0:T(8,128)S(1)} async-done(((f32[32,56,128]{2,1,0:T(8,128)}), f32[32,56,128]{2,1,0:T(8,128)S(1)}, u32[]{:S(2)}, u32[]{:S(2)}) %all-to-all-start) | async-done | bytes 917536 | tf_op jit(solution)/shard_map/all_to_all | solution.py:402
  53.8 0.1 shard_map.82.own
  53.9 0.4 collective-permute-start.8
  54.3 3.7 %collective-permute-start.7 = (f32[64,128]{1,0:T(8,128)S(1)}, f32[64,128]{1,0:T(8,128)S(1)}, u32[]{:S(2)}, u32[]{:S(2)}) collective-permute-start(f32[64,128]{1,0:T(8,128)S(1)} %shard_map.82.own), channel_id=1, source_target_pairs={{0,128},{8,136},{128,0},{136,8},{1,129},{9,137},{129,1},{137,9},{2... | collective-permute-start | bytes 98312 | tf_op jit(solution)/shard_map/ppermute | solution.py:494
  58.0 1.6 %collective-permute-start.6 = (f32[64,128]{1,0:T(8,128)S(1)}, f32[64,128]{1,0:T(8,128)S(1)}, u32[]{:S(2)}, u32[]{:S(2)}) collective-permute-start(f32[64,128]{1,0:T(8,128)S(1)} %shard_map.82.own), channel_id=1, source_target_pairs={{0,8},{8,0},{128,136},{136,128},{1,9},{9,1},{129,137},{137,129},{2... | collective-permute-start | bytes 98312 | tf_op jit(solution)/shard_map/ppermute | solution.py:494
  59.6 0.0 collective-permute-done.8.three
  59.6 1.8 %collective-permute-done.7.two = f32[64,128]{1,0:T(8,128)S(1)} collective-permute-done((f32[64,128]{1,0:T(8,128)S(1)}, f32[64,128]{1,0:T(8,128)S(1)}, u32[]{:S(2)}, u32[]{:S(2)}) %collective-permute-start.7) | collective-permute-done | bytes 32800 | tf_op jit(solution)/shard_map/ppermute | solution.py:494
  61.4 0.8 collective-permute-done.6.one
  62.1 0.9 %shard_map.83 = (bf16[32,56,128]{2,1,0:T(8,128)(2,1)}, f32[8,128]{1,0:T(8,128)S(1)}) custom-call(f32[64,128]{1,0:T(8,128)S(1)} %shard_map.82.own, f32[64,128]{1,0:T(8,128)S(1)} %collective-permute-done.6.one, f32[64,128]{1,0:T(8,128)S(1)} %collective-permute-done.7.two, f32[64,128]{1,0:T(8,128)S(1)} %collective-permute-done.8.three), custom_call_target="tpu_custom_call" | custom-call | bytes 1048576 | tf_op jit(solution)/shard_map/pallas_call | solution.py:377
  63.0 5.2 %all-to-all-start.1 = ((bf16[32,56,128]{2,1,0:T(8,128)(2,1)}), bf16[32,56,128]{2,1,0:T(8,128)(2,1)S(1)}, u32[]{:S(2)}, u32[]{:S(2)}) async-start(bf16[32,56,128]{2,1,0:T(8,128)(2,1)} %get-tuple-element.52), calls=%async_computation.1 | async-start | bytes 917504 | tf_op jit(solution)/shard_map/all_to_all | solution.py:402
  68.2 2.6 %shard_map.85 = bf16[4,512,128]{2,1,0:T(8,128)(2,1)} custom-call(bf16[4,512,128]{2,1,0:T(8,128)(2,1)} %bitcast.15, bf16[4,512,128]{2,1,0:T(8,128)(2,1)} %bitcast.19, f32[16,128]{1,0:T(8,128)S(1)} %constant_dynamic-update-slice_fusion.totals, f32[8,128]{1,0:T(8,128)S(1)} %get-tuple-element.54.backward, f32[4,512,128]{2,1,0:T(8,128)} %get-tuple-element.55.scaled), custom_call_target="tpu_custom_call" | custom-call | flops 1000000000 | bytes 1048576 | tf_op jit(solution)/shard_map/pallas_call | solution.py:377
  70.8 5.8 %shard_map.84 = bf16[4,512,128]{2,1,0:T(8,128)(2,1)} custom-call(s32[2]{0:T(128)S(1)} %pad_add_fusion.flags, bf16[4,512,128]{2,1,0:T(8,128)(2,1)} %bitcast.16, bf16[2,512,128]{2,1,0:T(8,128)(2,1)S(1)} %collective-permute-done.2.near, bf16[2,512,128]{2,1,0:T(8,128)(2,1)S(1)} %collective-permute-done.3.far, bf16[27,128,128]{2,1,0:T(8,128)(2,1)} %kernel.3, ...), custom_call_target="tpu_custom_call" | custom-call | flops 4000000000 | bytes 1048576 | tf_op jit(solution)/shard_map/pallas_call | solution.py:377
  76.6 0.4 all-to-all-done.1
  77.0 3.7 %collective-permute-start.9 = (bf16[1792,128]{1,0:T(8,128)(2,1)S(1)}, bf16[1792,128]{1,0:T(8,128)(2,1)S(1)}, u32[]{:S(2)}, u32[]{:S(2)}) collective-permute-start(bf16[1792,128]{1,0:T(8,128)(2,1)S(1)} %bitcast.10), channel_id=1, source_target_pairs={{0,64},{64,0},{1,65},{65,1},{2,66},{66,2},{3,67},{67,3},{4,68},{68... | collective-permute-start | bytes 1376264 | tf_op jit(solution)/shard_map/ppermute | solution.py:398
  80.7 1.5 %shard_map.86.grad_in = f32[27,128,128]{2,1,0:T(8,128)} custom-call(s32[2]{0:T(128)S(1)} %pad_add_fusion.flags, bf16[1792,128]{1,0:T(8,128)(2,1)S(1)} %bitcast.11), custom_call_target="tpu_custom_call" | custom-call | flops 1000000000 | bytes 1048576 | tf_op jit(solution)/shard_map/pallas_call | solution.py:377
  82.2 0.0 collective-permute-done.9.half_grad
  82.3 1.5 %shard_map.87 = f32[27,128,128]{2,1,0:T(8,128)} custom-call(s32[2]{0:T(128)S(1)} %pad_add_fusion.flags, bf16[1792,128]{1,0:T(8,128)(2,1)S(1)} %collective-permute-done.9.half_grad, f32[27,128,128]{2,1,0:T(8,128)} %shard_map.86.grad_in), custom_call_target="tpu_custom_call", output_to_operand_aliasing={{}: (2, {})} | custom-call | bytes 1048576 | tf_op jit(solution)/shard_map/pallas_call | solution.py:377
  (4 shorter events, 0.0 us)
Async XLA Ops:
  2.0 13.3 %collective-permute-start = (f32[8,128]{1,0:T(8,128)S(1)}, f32[8,128]{1,0:T(8,128)S(1)}, u32[]{:S(2)}, u32[]{:S(2)}) collective-permute-start(f32[8,128]{1,0:T(8,128)S(1)} %shard_map.76), channel_id=1, source_target_pairs={{0,128},{128,0},{1,129},{129,1},{2,130},{130,2},{3,131},{131,3},{4... | collective-permute-start | bytes 12296 | tf_op jit(solution)/shard_map/ppermute | solution.py:398
  12.2 12.1 %collective-permute-start.3 = (bf16[2,512,128]{2,1,0:T(8,128)(2,1)S(1)}, bf16[2,512,128]{2,1,0:T(8,128)(2,1)S(1)}, u32[]{:S(2)}, u32[]{:S(2)}) collective-permute-start(bf16[2,512,128]{2,1,0:T(8,128)(2,1)S(1)} %get-tuple-element.42), channel_id=1, source_target_pairs={{64,128},{128,64},{65,129},{129,65},{66,130},{130,66},{67,131},{13... | collective-permute-start | bytes 786440 | tf_op jit(solution)/shard_map/ppermute | solution.py:434
  15.3 1.3 %collective-permute-start.1 = (f32[8,128]{1,0:T(8,128)S(1)}, f32[8,128]{1,0:T(8,128)S(1)}, u32[]{:S(2)}, u32[]{:S(2)}) collective-permute-start(f32[8,128]{1,0:T(8,128)S(1)} %add.10), channel_id=1, source_target_pairs={{0,64},{64,0},{1,65},{65,1},{2,66},{66,2},{3,67},{67,3},{4,68},{68... | collective-permute-start | bytes 12296 | tf_op jit(solution)/shard_map/ppermute | solution.py:398
  15.4 8.9 %collective-permute-start.2 = (bf16[2,512,128]{2,1,0:T(8,128)(2,1)S(1)}, bf16[2,512,128]{2,1,0:T(8,128)(2,1)S(1)}, u32[]{:S(2)}, u32[]{:S(2)}) collective-permute-start(bf16[2,512,128]{2,1,0:T(8,128)(2,1)S(1)} %get-tuple-element.41), channel_id=1, source_target_pairs={{0,64},{64,0},{1,65},{65,1},{2,66},{66,2},{3,67},{67,3},{4,68},{68... | collective-permute-start | bytes 786440 | tf_op jit(solution)/shard_map/ppermute | solution.py:398
  25.7 2.6 %collective-permute-start.4 = (f32[1792,128]{1,0:T(8,128)S(1)}, f32[1792,128]{1,0:T(8,128)S(1)}, u32[]{:S(2)}, u32[]{:S(2)}) collective-permute-start(f32[1792,128]{1,0:T(8,128)S(1)} %get-tuple-element.48), channel_id=1, source_target_pairs={{0,64},{64,0},{1,65},{65,1},{2,66},{66,2},{3,67},{67,3},{4,68},{68... | collective-permute-start | bytes 2752520 | tf_op jit(solution)/shard_map/ppermute | solution.py:398
  29.4 24.4 %all-to-all-start = ((f32[32,56,128]{2,1,0:T(8,128)}), f32[32,56,128]{2,1,0:T(8,128)S(1)}, u32[]{:S(2)}, u32[]{:S(2)}) async-start(f32[32,56,128]{2,1,0:T(8,128)} %bitcast.6), calls=%async_computation | async-start | bytes 1835008 | tf_op jit(solution)/shard_map/all_to_all | solution.py:402
  46.0 1.3 %collective-permute-start.5 = (f32[8,128]{1,0:T(8,128)S(1)}, f32[8,128]{1,0:T(8,128)S(1)}, u32[]{:S(2)}, u32[]{:S(2)}) collective-permute-start(f32[8,128]{1,0:T(8,128)S(1)} %get-tuple-element.49), channel_id=1, source_target_pairs={{0,64},{64,0},{1,65},{65,1},{2,66},{66,2},{3,67},{67,3},{4,68},{68... | collective-permute-start | bytes 12296 | tf_op jit(solution)/shard_map/ppermute | solution.py:398
  53.9 5.7 %collective-permute-start.8 = (f32[64,128]{1,0:T(8,128)S(1)}, f32[64,128]{1,0:T(8,128)S(1)}, u32[]{:S(2)}, u32[]{:S(2)}) collective-permute-start(f32[64,128]{1,0:T(8,128)S(1)} %shard_map.82.own), channel_id=1, source_target_pairs={{0,136},{8,128},{128,8},{136,0},{1,137},{9,129},{129,9},{137,1},{2... | collective-permute-start | bytes 98312 | tf_op jit(solution)/shard_map/ppermute | solution.py:494
  54.3 7.1 %collective-permute-start.7 = (f32[64,128]{1,0:T(8,128)S(1)}, f32[64,128]{1,0:T(8,128)S(1)}, u32[]{:S(2)}, u32[]{:S(2)}) collective-permute-start(f32[64,128]{1,0:T(8,128)S(1)} %shard_map.82.own), channel_id=1, source_target_pairs={{0,128},{8,136},{128,0},{136,8},{1,129},{9,137},{129,1},{137,9},{2... | collective-permute-start | bytes 98312 | tf_op jit(solution)/shard_map/ppermute | solution.py:494
  58.0 4.2 %collective-permute-start.6 = (f32[64,128]{1,0:T(8,128)S(1)}, f32[64,128]{1,0:T(8,128)S(1)}, u32[]{:S(2)}, u32[]{:S(2)}) collective-permute-start(f32[64,128]{1,0:T(8,128)S(1)} %shard_map.82.own), channel_id=1, source_target_pairs={{0,8},{8,0},{128,136},{136,128},{1,9},{9,1},{129,137},{137,129},{2... | collective-permute-start | bytes 98312 | tf_op jit(solution)/shard_map/ppermute | solution.py:494
  63.0 14.0 %all-to-all-start.1 = ((bf16[32,56,128]{2,1,0:T(8,128)(2,1)}), bf16[32,56,128]{2,1,0:T(8,128)(2,1)S(1)}, u32[]{:S(2)}, u32[]{:S(2)}) async-start(bf16[32,56,128]{2,1,0:T(8,128)(2,1)} %get-tuple-element.52), calls=%async_computation.1 | async-start | bytes 917504 | tf_op jit(solution)/shard_map/all_to_all | solution.py:402
  77.0 5.2 %collective-permute-start.9 = (bf16[1792,128]{1,0:T(8,128)(2,1)S(1)}, bf16[1792,128]{1,0:T(8,128)(2,1)S(1)}, u32[]{:S(2)}, u32[]{:S(2)}) collective-permute-start(bf16[1792,128]{1,0:T(8,128)(2,1)S(1)} %bitcast.10), channel_id=1, source_target_pairs={{0,64},{64,0},{1,65},{65,1},{2,66},{66,2},{3,67},{67,3},{4,68},{68... | collective-permute-start | bytes 1376264 | tf_op jit(solution)/shard_map/ppermute | solution.py:398

commit v8 on v7

--- a/solution.py
+++ b/solution.py
@@ -489,13 +489,8 @@
         limit=20,
         flops=4 * 10**9,
     )
+    sums, window = lax.optimization_barrier((sums, window))
     sums = sums + swap(sums, "core")
-    packed = call(part_kernel, shape(PART + 8, C), [], parts, sums)
-    others = [lax.ppermute(packed, ("zh", "zm"), [(i, i ^ flip) for i in range(4)]) for flip in (1, 2, 3)]
-    part, backward = call(
-        merge_kernel, (shape(SIDE, PART, C, dtype=BF16), shape(8, C)), [], packed, *others
-    )
-    part, window = lax.optimization_barrier((part, window))
     output = call(
         conv_kernel,
         shape(T, ROWS, W, dtype=BF16),
@@ -514,6 +509,12 @@
         scalars=1,
         flops=4 * 10**9,
     )
+    parts, output = lax.optimization_barrier((parts, output))
+    packed = call(part_kernel, shape(PART + 8, C), [], parts, sums)
+    others = [lax.ppermute(packed, ("zh", "zm"), [(i, i ^ flip) for i in range(4)]) for flip in (1, 2, 3)]
+    part, backward = call(
+        merge_kernel, (shape(SIDE, PART, C, dtype=BF16), shape(8, C)), [], packed, *others
+    )
     result = call(
         adjoint_kernel,
         shape(T, ROWS, W, dtype=BF16),
@@ -527,9 +528,7 @@
         out_far=(0,),
         flops=10**9,
     )
-    mine, output, result = lax.optimization_barrier(
-        (exchange(part, ("y", "zn", "x")).reshape(COMM, C), output, result)
-    )
+    mine, result = lax.optimization_barrier((exchange(part, ("y", "zn", "x")).reshape(COMM, C), result))
     other = swap(mine, "core")
     half_scratch = [pltpu.VMEM((27, C // 2, C), F32), sems(3)]
     kernel_grad = call(

time: 84.3 us -> 85.7 us (1.017)
  starting transfers between devices: 36.6 us -> 37.5 us
    all_to_all x2, starting transfers between devices: 15 us -> 16.7 us  [exchange(): return lax.all_to_all(parts, axes, 0, 0)]
  transfers between devices with their start and end apart: 12 -> 12, of which waited for: 8 -> 7; matrix products, arithmetic and copies ran while one was open for 0% -> 0% of each run, Pallas kernels for 26% -> 26%
where the time goes in v8:
time: 85.7 us; the launch traced here: 85.2 us
  starting transfers between devices  37.5 us (44%)
  Pallas kernels  28.3 us (33%)
  waiting for transfers between devices  18.4 us (21%)
  between operations  0.95 us (1%)
    pallas_call x12, Pallas kernels, call(): pl.pallas_call(body, out_shape=shapes[0] if single else shapes, in_specs=...  28.3 us
    all_to_all x2, starting transfers between devices, exchange(): return lax.all_to_all(parts, axes, 0, 0)  16.7 us
    ppermute x6, starting transfers between devices, swap(): return lax.ppermute(value, axis, [(0, 1), (1, 0)])  12 us
    all_to_all x2, waiting for transfers between devices, exchange(): return lax.all_to_all(parts, axes, 0, 0)  7.75 us
    ppermute x3, starting transfers between devices, per_device(): lax.ppermute(packed, ('zh', 'zm'), [(i, i ^ flip) for i in range(4)])  5.74 us
    ppermute x1, waiting for transfers between devices, per_device(): before = lax.ppermute(to_far, slab, [(1, 2), (2, 1)])  4.59 us
    ppermute x6, waiting for transfers between devices, swap(): return lax.ppermute(value, axis, [(0, 1), (1, 0)])  3.12 us
    ppermute x1, starting transfers between devices, per_device(): before = lax.ppermute(to_far, slab, [(1, 2), (2, 1)])  3.07 us
  transfers between devices with their start and end apart: 12, of which 7 were waited for; matrix products, arithmetic and copies ran while one was open for 0% of the time, Pallas kernels for 26%

profile of v8, /device:TPU:1, one launch (start us, length us, event | category | flops | bytes accessed | tf_op | source)
XLA Modules:
  0.0 85.2 jit_solution(1183465346607438999)
XLA Ops:
  0.6 1.3 %shard_map.76 = f32[8,128]{1,0:T(8,128)S(1)} custom-call(bf16[4,512,128]{2,1,0:T(8,128)(2,1)} %bitcast.12), custom_call_target="tpu_custom_call" | custom-call | bytes 1048576 | tf_op jit(solution)/shard_map/pallas_call | solution.py:377
  2.0 7.8 %collective-permute-start = (f32[8,128]{1,0:T(8,128)S(1)}, f32[8,128]{1,0:T(8,128)S(1)}, u32[]{:S(2)}, u32[]{:S(2)}) collective-permute-start(f32[8,128]{1,0:T(8,128)S(1)} %shard_map.76), channel_id=1, source_target_pairs={{0,128},{128,0},{1,129},{129,1},{2,130},{130,2},{3,131},{131,3},{4... | collective-permute-start | bytes 12296 | tf_op jit(solution)/shard_map/ppermute | solution.py:398
  9.8 0.1 pad_add_fusion.flags
  9.9 2.3 %shard_map.77 = (bf16[512,2048]{1,0:T(8,128)(2,1)S(1)}, f32[2,128,128]{2,1,0:T(8,128)S(1)}, bf16[2,512,128]{2,1,0:T(8,128)(2,1)S(1)}, bf16[2,512,128]{2,1,0:T(8,128)(2,1)S(1)}) custom-call(s32[2]{0:T(128)S(1)} %pad_add_fusion.flags, bf16[4,512,128]{2,1,0:T(8,128)(2,1)} %bitcast.13, bf16[4,512,128]{2,1,0:T(8,128)(2,1)} %bitcast.17, f32[1,128]{1,0:T(1,128)} %bitcast.20, ...), custom_call_target="tpu_custom_call" | custom-call | bytes 1048576 | tf_op jit(solution)/shard_map/pallas_call | solution.py:377
  12.2 3.1 %collective-permute-start.3 = (bf16[2,512,128]{2,1,0:T(8,128)(2,1)S(1)}, bf16[2,512,128]{2,1,0:T(8,128)(2,1)S(1)}, u32[]{:S(2)}, u32[]{:S(2)}) collective-permute-start(bf16[2,512,128]{2,1,0:T(8,128)(2,1)S(1)} %get-tuple-element.43), channel_id=1, source_target_pairs={{64,128},{128,64},{65,129},{129,65},{66,130},{130,66},{67,131},{13... | collective-permute-start | bytes 786440 | tf_op jit(solution)/shard_map/ppermute | solution.py:434
  15.2 0.0 collective-permute-done
  15.3 0.1 collective-permute-start.1
  15.4 0.5 collective-permute-start.2
  15.9 0.7 collective-permute-done.1
  16.5 3.1 %shard_map.78 = (bf16[1536,512]{1,0:T(8,128)(2,1)}, f32[1792,128]{1,0:T(8,128)S(1)}, f32[1792,128]{1,0:T(8,128)S(1)}, bf16[384,1024]{1,0:T(8,128)(2,1)S(1)}) custom-call(s32[2]{0:T(128)S(1)} %pad_add_fusion.flags, bf16[512,2048]{1,0:T(8,128)(2,1)S(1)} %get-tuple-element.33.adj, f32[16,128]{1,0:T(8,128)S(1)} %constant_dynamic-update-slice_fusion.totals, ...), custom_call_target="tpu_custom_call" | custom-call | flops 2000000000 | bytes 1048576 | tf_op jit(solution)/shard_map/pallas_call | solution.py:377
  19.7 4.6 %collective-permute-done.3.far = bf16[2,512,128]{2,1,0:T(8,128)(2,1)S(1)} collective-permute-done((bf16[2,512,128]{2,1,0:T(8,128)(2,1)S(1)}, bf16[2,512,128]{2,1,0:T(8,128)(2,1)S(1)}, u32[]{:S(2)}, u32[]{:S(2)}) %collective-permute-start.3) | collective-permute-done | bytes 262176 | tf_op jit(solution)/shard_map/ppermute | solution.py:434
  24.3 0.0 collective-permute-done.2.near
  24.3 1.4 %shard_map.79 = (f32[1792,128]{1,0:T(8,128)S(1)}, f32[1792,128]{1,0:T(8,128)S(1)}) custom-call(s32[2]{0:T(128)S(1)} %pad_add_fusion.flags, f32[1792,128]{1,0:T(8,128)S(1)} %get-tuple-element.40.keep_in, f32[1792,128]{1,0:T(8,128)S(1)} %get-tuple-element.41.send_in, ...), custom_call_target="tpu_custom_call", output_to_operand_aliasing={{0}: (1, {}), {1}: (2, {})} | custom-call | bytes 1048576 | tf_op jit(solution)/shard_map/pallas_call | solution.py:377
  25.7 0.1 collective-permute-start.4
  25.8 2.5 %collective-permute-done.4.received = f32[1792,128]{1,0:T(8,128)S(1)} collective-permute-done((f32[1792,128]{1,0:T(8,128)S(1)}, f32[1792,128]{1,0:T(8,128)S(1)}, u32[]{:S(2)}, u32[]{:S(2)}) %collective-permute-start.4) | collective-permute-done | bytes 917536 | tf_op jit(solution)/shard_map/ppermute | solution.py:398
  28.3 1.1 %shard_map.80 = f32[1792,128]{1,0:T(8,128)} custom-call(f32[1792,128]{1,0:T(8,128)S(1)} %get-tuple-element.48.keep, f32[1792,128]{1,0:T(8,128)S(1)} %collective-permute-done.4.received), custom_call_target="tpu_custom_call" | custom-call | bytes 1048576 | tf_op jit(solution)/shard_map/pallas_call | solution.py:377
  29.4 9.8 %all-to-all-start = ((f32[32,56,128]{2,1,0:T(8,128)}), f32[32,56,128]{2,1,0:T(8,128)S(1)}, u32[]{:S(2)}, u32[]{:S(2)}) async-start(f32[32,56,128]{2,1,0:T(8,128)} %bitcast.6), calls=%async_computation | async-start | bytes 1835008 | tf_op jit(solution)/shard_map/all_to_all | solution.py:402
  39.2 6.8 %shard_map.81 = (f32[4,512,128]{2,1,0:T(8,128)}, f32[8,128]{1,0:T(8,128)S(1)}) custom-call(s32[2]{0:T(128)S(1)} %pad_add_fusion.flags, bf16[4,512,128]{2,1,0:T(8,128)(2,1)} %bitcast.14, bf16[4,512,128]{2,1,0:T(8,128)(2,1)} %bitcast.18, bf16[2,512,128]{2,1,0:T(8,128)(2,1)S(1)} %collective-permute-done.2.near, ...), custom_call_target="tpu_custom_call" | custom-call | flops 4000000000 | bytes 1048576 | tf_op jit(solution)/shard_map/pallas_call | solution.py:377
  46.0 0.7 collective-permute-start.5
  46.7 5.8 %shard_map.82 = bf16[4,512,128]{2,1,0:T(8,128)(2,1)} custom-call(s32[2]{0:T(128)S(1)} %pad_add_fusion.flags, bf16[4,512,128]{2,1,0:T(8,128)(2,1)} %bitcast.15, bf16[2,512,128]{2,1,0:T(8,128)(2,1)S(1)} %collective-permute-done.2.near, bf16[2,512,128]{2,1,0:T(8,128)(2,1)S(1)} %collective-permute-done.3.far, bf16[27,128,128]{2,1,0:T(8,128)(2,1)} %kernel.3, ...), custom_call_target="tpu_custom_call" | custom-call | flops 4000000000 | bytes 1048576 | tf_op jit(solution)/shard_map/pallas_call | solution.py:377
  52.5 0.0 collective-permute-done.5
  52.5 1.3 %all-to-all-done.parts = f32[32,56,128]{2,1,0:T(8,128)S(1)} async-done(((f32[32,56,128]{2,1,0:T(8,128)}), f32[32,56,128]{2,1,0:T(8,128)S(1)}, u32[]{:S(2)}, u32[]{:S(2)}) %all-to-all-start) | async-done | bytes 917536 | tf_op jit(solution)/shard_map/all_to_all | solution.py:402
  53.8 0.1 shard_map.83.own
  53.9 0.4 collective-permute-start.8
  54.3 3.7 %collective-permute-start.7 = (f32[64,128]{1,0:T(8,128)S(1)}, f32[64,128]{1,0:T(8,128)S(1)}, u32[]{:S(2)}, u32[]{:S(2)}) collective-permute-start(f32[64,128]{1,0:T(8,128)S(1)} %shard_map.83.own), channel_id=1, source_target_pairs={{0,128},{8,136},{128,0},{136,8},{1,129},{9,137},{129,1},{137,9},{2... | collective-permute-start | bytes 98312 | tf_op jit(solution)/shard_map/ppermute | solution.py:514
  58.0 1.6 %collective-permute-start.6 = (f32[64,128]{1,0:T(8,128)S(1)}, f32[64,128]{1,0:T(8,128)S(1)}, u32[]{:S(2)}, u32[]{:S(2)}) collective-permute-start(f32[64,128]{1,0:T(8,128)S(1)} %shard_map.83.own), channel_id=1, source_target_pairs={{0,8},{8,0},{128,136},{136,128},{1,9},{9,1},{129,137},{137,129},{2... | collective-permute-start | bytes 98312 | tf_op jit(solution)/shard_map/ppermute | solution.py:514
  59.6 0.0 collective-permute-done.8.three
  59.6 1.7 %collective-permute-done.7.two = f32[64,128]{1,0:T(8,128)S(1)} collective-permute-done((f32[64,128]{1,0:T(8,128)S(1)}, f32[64,128]{1,0:T(8,128)S(1)}, u32[]{:S(2)}, u32[]{:S(2)}) %collective-permute-start.7) | collective-permute-done | bytes 32800 | tf_op jit(solution)/shard_map/ppermute | solution.py:514
  61.3 1.2 %collective-permute-done.6.one = f32[64,128]{1,0:T(8,128)S(1)} collective-permute-done((f32[64,128]{1,0:T(8,128)S(1)}, f32[64,128]{1,0:T(8,128)S(1)}, u32[]{:S(2)}, u32[]{:S(2)}) %collective-permute-start.6) | collective-permute-done | bytes 32800 | tf_op jit(solution)/shard_map/ppermute | solution.py:514
  62.6 0.8 shard_map.84
  63.4 6.9 %all-to-all-start.1 = ((bf16[32,56,128]{2,1,0:T(8,128)(2,1)}), bf16[32,56,128]{2,1,0:T(8,128)(2,1)S(1)}, u32[]{:S(2)}, u32[]{:S(2)}) async-start(bf16[32,56,128]{2,1,0:T(8,128)(2,1)} %get-tuple-element.56), calls=%async_computation.1 | async-start | bytes 917504 | tf_op jit(solution)/shard_map/all_to_all | solution.py:402
  70.3 2.6 %shard_map.85 = bf16[4,512,128]{2,1,0:T(8,128)(2,1)} custom-call(bf16[4,512,128]{2,1,0:T(8,128)(2,1)} %bitcast.16, bf16[4,512,128]{2,1,0:T(8,128)(2,1)} %bitcast.19, f32[16,128]{1,0:T(8,128)S(1)} %constant_dynamic-update-slice_fusion.totals, f32[8,128]{1,0:T(8,128)S(1)} %get-tuple-element.57.backward, f32[4,512,128]{2,1,0:T(8,128)} %get-tuple-element.58.scaled), custom_call_target="tpu_custom_call" | custom-call | flops 1000000000 | bytes 1048576 | tf_op jit(solution)/shard_map/pallas_call | solution.py:377
  72.9 6.5 %all-to-all-done.1 = bf16[32,56,128]{2,1,0:T(8,128)(2,1)S(1)} async-done(((bf16[32,56,128]{2,1,0:T(8,128)(2,1)}), bf16[32,56,128]{2,1,0:T(8,128)(2,1)S(1)}, u32[]{:S(2)}, u32[]{:S(2)}) %all-to-all-start.1) | async-done | bytes 458784 | tf_op jit(solution)/shard_map/all_to_all | solution.py:402
  79.3 2.8 %collective-permute-start.9 = (bf16[1792,128]{1,0:T(8,128)(2,1)S(1)}, bf16[1792,128]{1,0:T(8,128)(2,1)S(1)}, u32[]{:S(2)}, u32[]{:S(2)}) collective-permute-start(bf16[1792,128]{1,0:T(8,128)(2,1)S(1)} %bitcast.10), channel_id=1, source_target_pairs={{0,64},{64,0},{1,65},{65,1},{2,66},{66,2},{3,67},{67,3},{4,68},{68... | collective-permute-start | bytes 1376264 | tf_op jit(solution)/shard_map/ppermute | solution.py:398
  82.1 1.5 %shard_map.86.grad_in = f32[27,128,128]{2,1,0:T(8,128)} custom-call(s32[2]{0:T(128)S(1)} %pad_add_fusion.flags, bf16[1792,128]{1,0:T(8,128)(2,1)S(1)} %bitcast.11), custom_call_target="tpu_custom_call" | custom-call | flops 1000000000 | bytes 1048576 | tf_op jit(solution)/shard_map/pallas_call | solution.py:377
  83.6 0.0 collective-permute-done.9.half_grad
  83.6 1.5 %shard_map.87 = f32[27,128,128]{2,1,0:T(8,128)} custom-call(s32[2]{0:T(128)S(1)} %pad_add_fusion.flags, bf16[1792,128]{1,0:T(8,128)(2,1)S(1)} %collective-permute-done.9.half_grad, f32[27,128,128]{2,1,0:T(8,128)} %shard_map.86.grad_in), custom_call_target="tpu_custom_call", output_to_operand_aliasing={{}: (2, {})} | custom-call | bytes 1048576 | tf_op jit(solution)/shard_map/pallas_call | solution.py:377
  (4 shorter events, 0.0 us)
Async XLA Ops:
  2.0 13.3 %collective-permute-start = (f32[8,128]{1,0:T(8,128)S(1)}, f32[8,128]{1,0:T(8,128)S(1)}, u32[]{:S(2)}, u32[]{:S(2)}) collective-permute-start(f32[8,128]{1,0:T(8,128)S(1)} %shard_map.76), channel_id=1, source_target_pairs={{0,128},{128,0},{1,129},{129,1},{2,130},{130,2},{3,131},{131,3},{4... | collective-permute-start | bytes 12296 | tf_op jit(solution)/shard_map/ppermute | solution.py:398
  12.2 12.1 %collective-permute-start.3 = (bf16[2,512,128]{2,1,0:T(8,128)(2,1)S(1)}, bf16[2,512,128]{2,1,0:T(8,128)(2,1)S(1)}, u32[]{:S(2)}, u32[]{:S(2)}) collective-permute-start(bf16[2,512,128]{2,1,0:T(8,128)(2,1)S(1)} %get-tuple-element.43), channel_id=1, source_target_pairs={{64,128},{128,64},{65,129},{129,65},{66,130},{130,66},{67,131},{13... | collective-permute-start | bytes 786440 | tf_op jit(solution)/shard_map/ppermute | solution.py:434
  15.3 1.3 %collective-permute-start.1 = (f32[8,128]{1,0:T(8,128)S(1)}, f32[8,128]{1,0:T(8,128)S(1)}, u32[]{:S(2)}, u32[]{:S(2)}) collective-permute-start(f32[8,128]{1,0:T(8,128)S(1)} %add.10), channel_id=1, source_target_pairs={{0,64},{64,0},{1,65},{65,1},{2,66},{66,2},{3,67},{67,3},{4,68},{68... | collective-permute-start | bytes 12296 | tf_op jit(solution)/shard_map/ppermute | solution.py:398
  15.4 8.9 %collective-permute-start.2 = (bf16[2,512,128]{2,1,0:T(8,128)(2,1)S(1)}, bf16[2,512,128]{2,1,0:T(8,128)(2,1)S(1)}, u32[]{:S(2)}, u32[]{:S(2)}) collective-permute-start(bf16[2,512,128]{2,1,0:T(8,128)(2,1)S(1)} %get-tuple-element.42), channel_id=1, source_target_pairs={{0,64},{64,0},{1,65},{65,1},{2,66},{66,2},{3,67},{67,3},{4,68},{68... | collective-permute-start | bytes 786440 | tf_op jit(solution)/shard_map/ppermute | solution.py:398
  25.7 2.6 %collective-permute-start.4 = (f32[1792,128]{1,0:T(8,128)S(1)}, f32[1792,128]{1,0:T(8,128)S(1)}, u32[]{:S(2)}, u32[]{:S(2)}) collective-permute-start(f32[1792,128]{1,0:T(8,128)S(1)} %get-tuple-element.49), channel_id=1, source_target_pairs={{0,64},{64,0},{1,65},{65,1},{2,66},{66,2},{3,67},{67,3},{4,68},{68... | collective-permute-start | bytes 2752520 | tf_op jit(solution)/shard_map/ppermute | solution.py:398
  29.4 24.4 %all-to-all-start = ((f32[32,56,128]{2,1,0:T(8,128)}), f32[32,56,128]{2,1,0:T(8,128)S(1)}, u32[]{:S(2)}, u32[]{:S(2)}) async-start(f32[32,56,128]{2,1,0:T(8,128)} %bitcast.6), calls=%async_computation | async-start | bytes 1835008 | tf_op jit(solution)/shard_map/all_to_all | solution.py:402
  46.0 6.5 %collective-permute-start.5 = (f32[8,128]{1,0:T(8,128)S(1)}, f32[8,128]{1,0:T(8,128)S(1)}, u32[]{:S(2)}, u32[]{:S(2)}) collective-permute-start(f32[8,128]{1,0:T(8,128)S(1)} %get-tuple-element.55), channel_id=1, source_target_pairs={{0,64},{64,0},{1,65},{65,1},{2,66},{66,2},{3,67},{67,3},{4,68},{68... | collective-permute-start | bytes 12296 | tf_op jit(solution)/shard_map/ppermute | solution.py:398
  53.9 5.7 %collective-permute-start.8 = (f32[64,128]{1,0:T(8,128)S(1)}, f32[64,128]{1,0:T(8,128)S(1)}, u32[]{:S(2)}, u32[]{:S(2)}) collective-permute-start(f32[64,128]{1,0:T(8,128)S(1)} %shard_map.83.own), channel_id=1, source_target_pairs={{0,136},{8,128},{128,8},{136,0},{1,137},{9,129},{129,9},{137,1},{2... | collective-permute-start | bytes 98312 | tf_op jit(solution)/shard_map/ppermute | solution.py:514
  54.3 7.1 %collective-permute-start.7 = (f32[64,128]{1,0:T(8,128)S(1)}, f32[64,128]{1,0:T(8,128)S(1)}, u32[]{:S(2)}, u32[]{:S(2)}) collective-permute-start(f32[64,128]{1,0:T(8,128)S(1)} %shard_map.83.own), channel_id=1, source_target_pairs={{0,128},{8,136},{128,0},{136,8},{1,129},{9,137},{129,1},{137,9},{2... | collective-permute-start | bytes 98312 | tf_op jit(solution)/shard_map/ppermute | solution.py:514
  58.0 4.6 %collective-permute-start.6 = (f32[64,128]{1,0:T(8,128)S(1)}, f32[64,128]{1,0:T(8,128)S(1)}, u32[]{:S(2)}, u32[]{:S(2)}) collective-permute-start(f32[64,128]{1,0:T(8,128)S(1)} %shard_map.83.own), channel_id=1, source_target_pairs={{0,8},{8,0},{128,136},{136,128},{1,9},{9,1},{129,137},{137,129},{2... | collective-permute-start | bytes 98312 | tf_op jit(solution)/shard_map/ppermute | solution.py:514
  63.4 15.9 %all-to-all-start.1 = ((bf16[32,56,128]{2,1,0:T(8,128)(2,1)}), bf16[32,56,128]{2,1,0:T(8,128)(2,1)S(1)}, u32[]{:S(2)}, u32[]{:S(2)}) async-start(bf16[32,56,128]{2,1,0:T(8,128)(2,1)} %get-tuple-element.56), calls=%async_computation.1 | async-start | bytes 917504 | tf_op jit(solution)/shard_map/all_to_all | solution.py:402
  79.3 4.3 %collective-permute-start.9 = (bf16[1792,128]{1,0:T(8,128)(2,1)S(1)}, bf16[1792,128]{1,0:T(8,128)(2,1)S(1)}, u32[]{:S(2)}, u32[]{:S(2)}) collective-permute-start(bf16[1792,128]{1,0:T(8,128)(2,1)S(1)} %bitcast.10), channel_id=1, source_target_pairs={{0,64},{64,0},{1,65},{65,1},{2,66},{66,2},{3,67},{67,3},{4,68},{68... | collective-permute-start | bytes 1376264 | tf_op jit(solution)/shard_map/ppermute | solution.py:398

commit v9 on v7

--- a/solution.py
+++ b/solution.py
@@ -95,19 +95,22 @@
             adj[ki * C : (ki + 1) * C, (f * H + h) * W : (f * H + h + 1) * W] = block
 
 
-def prepare_kernel(
-    flags, lat, cot, gain, shift, adj, scales, near, far, lat_v, cot_v, gain_v, shift_v, tmp, sem, halo_sem
-):
+def halo_kernel(flags, sums, lat, cot, near, far, sem):
     tail, head = lat.at[T - HALO :], cot.at[:HALO]
 
     @pl.when(flags[1] == 0)
     def _():
-        copies(halo_sem, (tail, near), (head, far))
+        copies(sem, (tail, near), (head, far))
 
     @pl.when(flags[1] != 0)
     def _():
-        copies(halo_sem, (head, near), (tail, far))
-
+        copies(sem, (head, near), (tail, far))
+
+    pltpu.make_async_copy(tail, near, sem.at[0]).wait()
+    pltpu.make_async_copy(head, far, sem.at[1]).wait()
+
+
+def prepare_kernel(lat, cot, gain, shift, adj, scales, lat_v, cot_v, gain_v, shift_v, tmp, sem):
     from_lat, from_cot, *small = copies(sem, (lat, lat_v), (cot, cot_v), (gain, gain_v), (shift, shift_v))
     from_lat.wait()
     for t in range(T):
@@ -120,8 +123,6 @@
         copy.wait()
     scales[0] = jnp.broadcast_to(channel_column(gain_v[...]), (C, W))
     scales[1] = jnp.broadcast_to(channel_column(shift_v[...]), (C, W))
-    pltpu.make_async_copy(tail, near, halo_sem.at[0]).wait()
-    pltpu.make_async_copy(head, far, halo_sem.at[1]).wait()
 
 
 def clear(taps):
@@ -291,11 +292,39 @@
     place_kernel(flags, half_grad, grad, grad_v, sem, False)
 
 
-def conv_kernel(
-    flags, lat, near, far, kernel, window, totals, scales, output, tmp, taps, lat_v, kernel_v, window_v, output_v, sem, out_sem
+def finish_kernel(
+    flags,
+    lat,
+    cot,
+    near,
+    far,
+    kernel,
+    window,
+    totals,
+    scales,
+    backward,
+    scaled,
+    output,
+    result,
+    tmp,
+    taps,
+    lat_v,
+    cot_v,
+    kernel_v,
+    window_v,
+    scaled_v,
+    output_v,
+    result_v,
+    sem,
+    out_sem,
 ):
-    from_kernel, from_window, from_lat = copies(
-        sem, (kernel, kernel_v), (window, window_v.at[:, HALO * W :]), (lat, lat_v)
+    from_kernel, from_window, from_lat, from_cot, from_scaled = copies(
+        sem,
+        (kernel, kernel_v),
+        (window, window_v.at[:, HALO * W :]),
+        (lat, lat_v),
+        (cot, cot_v),
+        (scaled, scaled_v),
     )
     center, inverse = center_inverse(totals, PER)
     for f in range(HALO):
@@ -319,44 +348,22 @@
     total = jnp.dot(taps[0], window_v[:, 0 : T * W], preferred_element_type=F32)
     for f in range(1, 3):
         total = total + jnp.dot(taps[f], window_v[:, f * W : (f + T) * W], preferred_element_type=F32)
-    from_lat.wait()
-    started = []
-    for t in range(T):
-        for h in range(H):
-            tmp[pl.ds(h, C, stride=H), :] = total[h * C : (h + 1) * C, t * W : (t + 1) * W]
-        output_v[t] = (lat_v[t].astype(F32) + tmp[...]).astype(BF16)
-        started += copies(out_sem.at[pl.ds(t, 1)], (output_v.at[t], output.at[t]))
-    for copy in started:
-        copy.wait()
-
-
-def adjoint_kernel(
-    lat, cot, totals, backward, scaled, result, lat_v, cot_v, scaled_v, result_v, lat_sem, cot_sem, scaled_sem, out_sem
-):
-    fetched = list(
-        zip(
-            *(
-                copies(sem, *((source.at[t], target.at[t]) for t in range(T)))
-                for sem, source, target in (
-                    (lat_sem, lat, lat_v),
-                    (cot_sem, cot, cot_v),
-                    (scaled_sem, scaled, scaled_v),
-                )
-            )
-        )
-    )
     center, inverse = center_inverse(totals, PER * H)
     row = backward[...][0:1] / MEMBERS
     first = group_column(row, 0, PER * H)
     second = group_column(row, GROUPS, PER * H)
+    for copy in (from_lat, from_cot, from_scaled):
+        copy.wait()
     started = []
     for t in range(T):
-        for copy in fetched[t]:
-            copy.wait()
-        unit = (lat_v[t].astype(F32) - center) * inverse
-        value = cot_v[t].astype(F32) + inverse * (scaled_v[t] - first - unit * second)
+        frame = lat_v[t].astype(F32)
+        value = cot_v[t].astype(F32) + inverse * (scaled_v[t] - first - (frame - center) * inverse * second)
         result_v[t] = value.astype(BF16)
-        started += copies(out_sem.at[pl.ds(t, 1)], (result_v.at[t], result.at[t]))
+        started += copies(out_sem.at[pl.ds(T + t, 1)], (result_v.at[t], result.at[t]))
+        for h in range(H):
+            tmp[pl.ds(h, C, stride=H), :] = total[h * C : (h + 1) * C, t * W : (t + 1) * W]
+        output_v[t] = (frame + tmp[...]).astype(BF16)
+        started += copies(out_sem.at[pl.ds(t, 1)], (output_v.at[t], output.at[t]))
     for copy in started:
         copy.wait()
 
@@ -417,18 +424,18 @@
     kernel_scratch = pltpu.VMEM((27, C, C), BF16)
     scaled_scratch = pltpu.VMEM((T, ROWS, W), F32)
     own = call(start_kernel, shape(8, W), [frames, sems(T)], lat, far=(0,))
-    gain, own = lax.optimization_barrier((gain, own))
-    adj, scales, to_near, to_far = call(
+    to_near, to_far = call(halo_kernel, (halo, halo), [sems(2)], flags, own, lat, cot, far=(2, 3), scalars=1)
+    gain, to_far = lax.optimization_barrier((gain, to_far))
+    adj, scales = call(
         prepare_kernel,
-        (shape(4 * C, T * PLANE, dtype=BF16), shape(2, C, W), halo, halo),
-        [frames, frames, row, row, tmp, sems(4), sems(2)],
-        flags,
+        (shape(4 * C, T * PLANE, dtype=BF16), shape(2, C, W)),
+        [frames, frames, row, row, tmp, sems(4)],
         lat,
         cot,
         gain,
         shift,
-        far=(1, 2, 3, 4),
-        scalars=1,
+        far=(0, 1, 2, 3),
+        flops=0,
     )
     slab = ("zh", "core")
     before = lax.ppermute(to_far, slab, [(1, 2), (2, 1)])
@@ -496,36 +503,27 @@
         merge_kernel, (shape(SIDE, PART, C, dtype=BF16), shape(8, C)), [], packed, *others
     )
     part, window = lax.optimization_barrier((part, window))
-    output = call(
-        conv_kernel,
-        shape(T, ROWS, W, dtype=BF16),
-        [tmp, taps, frames, kernel_scratch, window_scratch, frames, sems(3), sems(T)],
+    block = shape(T, ROWS, W, dtype=BF16)
+    output, result = call(
+        finish_kernel,
+        (block, block),
+        [tmp, taps, frames, frames, kernel_scratch, window_scratch, scaled_scratch, frames, frames, sems(5), sems(2 * T)],
         flags,
         lat,
+        cot,
         near,
         far,
         kernel,
         window,
         totals,
         scales,
-        far=(1, 4, 5),
-        out_far=(0,),
+        backward,
+        scaled,
+        far=(1, 2, 5, 6, 10),
+        out_far=(0, 1),
         limit=20,
         scalars=1,
         flops=4 * 10**9,
-    )
-    result = call(
-        adjoint_kernel,
-        shape(T, ROWS, W, dtype=BF16),
-        [frames, frames, scaled_scratch, frames, sems(T), sems(T), sems(T), sems(T)],
-        lat,
-        cot,
-        totals,
-        backward,
-        scaled,
-        far=(0, 1, 4),
-        out_far=(0,),
-        flops=10**9,
     )
     mine, output, result = lax.optimization_barrier(
         (exchange(part, ("y", "zn", "x")).reshape(COMM, C), output, result)

time: 84.3 us -> 83.4 us (0.989)
    all_to_all x2, waiting for transfers between devices: 6.89 us -> 8.73 us  [exchange(): return lax.all_to_all(parts, axes, 0, 0)]
    ppermute x1, waiting for transfers between devices: 4.6 us -> 2.86 us  [per_device(): before = lax.ppermute(to_far, slab, [(1, 2), (2, 1)])]
where the time goes in v9:
time: 83.4 us; the launch traced here: 83.1 us
  starting transfers between devices  36.5 us (44%)
  Pallas kernels  27.5 us (33%)
  waiting for transfers between devices  18 us (22%)
  between operations  0.94 us (1%)
    pallas_call x12, Pallas kernels, call(): pl.pallas_call(body, out_shape=shapes[0] if single else shapes, in_specs=...  27.5 us
    all_to_all x2, starting transfers between devices, exchange(): return lax.all_to_all(parts, axes, 0, 0)  15.1 us
    ppermute x6, starting transfers between devices, swap(): return lax.ppermute(value, axis, [(0, 1), (1, 0)])  12.7 us
    all_to_all x2, waiting for transfers between devices, exchange(): return lax.all_to_all(parts, axes, 0, 0)  8.73 us
    ppermute x3, starting transfers between devices, per_device(): lax.ppermute(packed, ('zh', 'zm'), [(i, i ^ flip) for i in range(4)])  5.74 us
    ppermute x6, waiting for transfers between devices, swap(): return lax.ppermute(value, axis, [(0, 1), (1, 0)])  3.94 us
    ppermute x1, starting transfers between devices, per_device(): before = lax.ppermute(to_far, slab, [(1, 2), (2, 1)])  2.95 us
    ppermute x1, waiting for transfers between devices, per_device(): before = lax.ppermute(to_far, slab, [(1, 2), (2, 1)])  2.86 us
  transfers between devices with their start and end apart: 12, of which 8 were waited for; matrix products, arithmetic and copies ran while one was open for 0% of the time, Pallas kernels for 26%

profile of v9, /device:TPU:1, one launch (start us, length us, event | category | flops | bytes accessed | tf_op | source)
XLA Modules:
  0.0 83.1 jit_solution(18154371062074350730)
XLA Ops:
  0.6 1.3 %shard_map.76.sums = f32[8,128]{1,0:T(8,128)S(1)} custom-call(bf16[4,512,128]{2,1,0:T(8,128)(2,1)} %bitcast.12), custom_call_target="tpu_custom_call" | custom-call | bytes 1048576 | tf_op jit(solution)/shard_map/pallas_call | solution.py:384
  2.0 7.8 %collective-permute-start = (f32[8,128]{1,0:T(8,128)S(1)}, f32[8,128]{1,0:T(8,128)S(1)}, u32[]{:S(2)}, u32[]{:S(2)}) collective-permute-start(f32[8,128]{1,0:T(8,128)S(1)} %shard_map.76.sums), channel_id=1, source_target_pairs={{0,128},{128,0},{1,129},{129,1},{2,130},{130,2},{3,131},{131,3},{4... | collective-permute-start | bytes 12296 | tf_op jit(solution)/shard_map/ppermute | solution.py:405
  9.8 0.1 pad_add_fusion.flags
  9.9 1.6 %shard_map.77 = (bf16[2,512,128]{2,1,0:T(8,128)(2,1)S(1)}, bf16[2,512,128]{2,1,0:T(8,128)(2,1)S(1)}) custom-call(s32[2]{0:T(128)S(1)} %pad_add_fusion.flags, f32[8,128]{1,0:T(8,128)S(1)} %shard_map.76.sums, bf16[4,512,128]{2,1,0:T(8,128)(2,1)} %bitcast.13, bf16[4,512,128]{2,1,0:T(8,128)(2,1)} %bitcast.17), custom_call_target="tpu_custom_call" | custom-call | bytes 1048576 | tf_op jit(solution)/shard_map/pallas_call | solution.py:384
  11.5 2.9 %collective-permute-start.3 = (bf16[2,512,128]{2,1,0:T(8,128)(2,1)S(1)}, bf16[2,512,128]{2,1,0:T(8,128)(2,1)S(1)}, u32[]{:S(2)}, u32[]{:S(2)}) collective-permute-start(bf16[2,512,128]{2,1,0:T(8,128)(2,1)S(1)} %get-tuple-element.44), channel_id=1, source_target_pairs={{64,128},{128,64},{65,129},{129,65},{66,130},{130,66},{67,131},{13... | collective-permute-start | bytes 786440 | tf_op jit(solution)/shard_map/ppermute | solution.py:441
  14.4 1.7 %shard_map.78 = (bf16[512,2048]{1,0:T(8,128)(2,1)S(1)}, f32[2,128,128]{2,1,0:T(8,128)S(1)}) custom-call(bf16[4,512,128]{2,1,0:T(8,128)(2,1)} %bitcast.14, bf16[4,512,128]{2,1,0:T(8,128)(2,1)} %bitcast.18, f32[1,128]{1,0:T(1,128)} %bitcast.21, f32[1,128]{1,0:T(1,128)} %bitcast.22), custom_call_target="tpu_custom_call" | custom-call | bytes 1048576 | tf_op jit(solution)/shard_map/pallas_call | solution.py:384
  16.2 0.0 collective-permute-done
  16.2 0.1 collective-permute-start.1
  16.3 0.5 collective-permute-start.2
  16.8 0.7 collective-permute-done.1
  17.4 3.1 %shard_map.79 = (bf16[1536,512]{1,0:T(8,128)(2,1)}, f32[1792,128]{1,0:T(8,128)S(1)}, f32[1792,128]{1,0:T(8,128)S(1)}, bf16[384,1024]{1,0:T(8,128)(2,1)S(1)}) custom-call(s32[2]{0:T(128)S(1)} %pad_add_fusion.flags, bf16[512,2048]{1,0:T(8,128)(2,1)S(1)} %get-tuple-element.35.adj, f32[16,128]{1,0:T(8,128)S(1)} %constant_dynamic-update-slice_fusion.totals, ...), custom_call_target="tpu_custom_call" | custom-call | flops 2000000000 | bytes 1048576 | tf_op jit(solution)/shard_map/pallas_call | solution.py:384
  20.6 2.9 %collective-permute-done.3.far = bf16[2,512,128]{2,1,0:T(8,128)(2,1)S(1)} collective-permute-done((bf16[2,512,128]{2,1,0:T(8,128)(2,1)S(1)}, bf16[2,512,128]{2,1,0:T(8,128)(2,1)S(1)}, u32[]{:S(2)}, u32[]{:S(2)}) %collective-permute-start.3) | collective-permute-done | bytes 262176 | tf_op jit(solution)/shard_map/ppermute | solution.py:441
  23.4 0.0 collective-permute-done.2.near
  23.4 1.4 %shard_map.80 = (f32[1792,128]{1,0:T(8,128)S(1)}, f32[1792,128]{1,0:T(8,128)S(1)}) custom-call(s32[2]{0:T(128)S(1)} %pad_add_fusion.flags, f32[1792,128]{1,0:T(8,128)S(1)} %get-tuple-element.41.keep_in, f32[1792,128]{1,0:T(8,128)S(1)} %get-tuple-element.42.send_in, ...), custom_call_target="tpu_custom_call", output_to_operand_aliasing={{0}: (1, {}), {1}: (2, {})} | custom-call | bytes 1048576 | tf_op jit(solution)/shard_map/pallas_call | solution.py:384
  24.9 0.1 collective-permute-start.4
  25.0 2.5 %collective-permute-done.4.received = f32[1792,128]{1,0:T(8,128)S(1)} collective-permute-done((f32[1792,128]{1,0:T(8,128)S(1)}, f32[1792,128]{1,0:T(8,128)S(1)}, u32[]{:S(2)}, u32[]{:S(2)}) %collective-permute-start.4) | collective-permute-done | bytes 917536 | tf_op jit(solution)/shard_map/ppermute | solution.py:405
  27.5 1.1 %shard_map.81 = f32[1792,128]{1,0:T(8,128)} custom-call(f32[1792,128]{1,0:T(8,128)S(1)} %get-tuple-element.49.keep, f32[1792,128]{1,0:T(8,128)S(1)} %collective-permute-done.4.received), custom_call_target="tpu_custom_call" | custom-call | bytes 1048576 | tf_op jit(solution)/shard_map/pallas_call | solution.py:384
  28.5 9.9 %all-to-all-start = ((f32[32,56,128]{2,1,0:T(8,128)}), f32[32,56,128]{2,1,0:T(8,128)S(1)}, u32[]{:S(2)}, u32[]{:S(2)}) async-start(f32[32,56,128]{2,1,0:T(8,128)} %bitcast.6), calls=%async_computation | async-start | bytes 1835008 | tf_op jit(solution)/shard_map/all_to_all | solution.py:409
  38.4 6.8 %shard_map.82 = (f32[4,512,128]{2,1,0:T(8,128)}, f32[8,128]{1,0:T(8,128)S(1)}) custom-call(s32[2]{0:T(128)S(1)} %pad_add_fusion.flags, bf16[4,512,128]{2,1,0:T(8,128)(2,1)} %bitcast.15, bf16[4,512,128]{2,1,0:T(8,128)(2,1)} %bitcast.19, bf16[2,512,128]{2,1,0:T(8,128)(2,1)S(1)} %collective-permute-done.2.near, ...), custom_call_target="tpu_custom_call" | custom-call | flops 4000000000 | bytes 1048576 | tf_op jit(solution)/shard_map/pallas_call | solution.py:384
  45.3 0.5 collective-permute-start.5
  45.8 0.8 collective-permute-done.5
  46.6 6.4 %all-to-all-done.parts = f32[32,56,128]{2,1,0:T(8,128)S(1)} async-done(((f32[32,56,128]{2,1,0:T(8,128)}), f32[32,56,128]{2,1,0:T(8,128)S(1)}, u32[]{:S(2)}, u32[]{:S(2)}) %all-to-all-start) | async-done | bytes 917536 | tf_op jit(solution)/shard_map/all_to_all | solution.py:409
  53.1 0.1 shard_map.83.own
  53.1 0.1 collective-permute-start.8
  53.2 3.9 %collective-permute-start.7 = (f32[64,128]{1,0:T(8,128)S(1)}, f32[64,128]{1,0:T(8,128)S(1)}, u32[]{:S(2)}, u32[]{:S(2)}) collective-permute-start(f32[64,128]{1,0:T(8,128)S(1)} %shard_map.83.own), channel_id=1, source_target_pairs={{0,128},{8,136},{128,0},{136,8},{1,129},{9,137},{129,1},{137,9},{2... | collective-permute-start | bytes 98312 | tf_op jit(solution)/shard_map/ppermute | solution.py:501
  57.2 1.7 %collective-permute-start.6 = (f32[64,128]{1,0:T(8,128)S(1)}, f32[64,128]{1,0:T(8,128)S(1)}, u32[]{:S(2)}, u32[]{:S(2)}) collective-permute-start(f32[64,128]{1,0:T(8,128)S(1)} %shard_map.83.own), channel_id=1, source_target_pairs={{0,8},{8,0},{128,136},{136,128},{1,9},{9,1},{129,137},{137,129},{2... | collective-permute-start | bytes 98312 | tf_op jit(solution)/shard_map/ppermute | solution.py:501
  58.9 0.0 collective-permute-done.8.three
  58.9 1.3 %collective-permute-done.7.two = f32[64,128]{1,0:T(8,128)S(1)} collective-permute-done((f32[64,128]{1,0:T(8,128)S(1)}, f32[64,128]{1,0:T(8,128)S(1)}, u32[]{:S(2)}, u32[]{:S(2)}) %collective-permute-start.7) | collective-permute-done | bytes 32800 | tf_op jit(solution)/shard_map/ppermute | solution.py:501
  60.1 1.2 %collective-permute-done.6.one = f32[64,128]{1,0:T(8,128)S(1)} collective-permute-done((f32[64,128]{1,0:T(8,128)S(1)}, f32[64,128]{1,0:T(8,128)S(1)}, u32[]{:S(2)}, u32[]{:S(2)}) %collective-permute-start.6) | collective-permute-done | bytes 32800 | tf_op jit(solution)/shard_map/ppermute | solution.py:501
  61.3 0.8 %shard_map.84 = (bf16[32,56,128]{2,1,0:T(8,128)(2,1)}, f32[8,128]{1,0:T(8,128)S(1)}) custom-call(f32[64,128]{1,0:T(8,128)S(1)} %shard_map.83.own, f32[64,128]{1,0:T(8,128)S(1)} %collective-permute-done.6.one, f32[64,128]{1,0:T(8,128)S(1)} %collective-permute-done.7.two, f32[64,128]{1,0:T(8,128)S(1)} %collective-permute-done.8.three), custom_call_target="tpu_custom_call" | custom-call | bytes 1048576 | tf_op jit(solution)/shard_map/pallas_call | solution.py:384
  62.1 5.2 %all-to-all-start.1 = ((bf16[32,56,128]{2,1,0:T(8,128)(2,1)}), bf16[32,56,128]{2,1,0:T(8,128)(2,1)S(1)}, u32[]{:S(2)}, u32[]{:S(2)}) async-start(bf16[32,56,128]{2,1,0:T(8,128)(2,1)} %get-tuple-element.54), calls=%async_computation.1 | async-start | bytes 917504 | tf_op jit(solution)/shard_map/all_to_all | solution.py:409
  67.4 6.5 %shard_map.85 = (bf16[4,512,128]{2,1,0:T(8,128)(2,1)}, bf16[4,512,128]{2,1,0:T(8,128)(2,1)}) custom-call(s32[2]{0:T(128)S(1)} %pad_add_fusion.flags, bf16[4,512,128]{2,1,0:T(8,128)(2,1)} %bitcast.16, bf16[4,512,128]{2,1,0:T(8,128)(2,1)} %bitcast.20, bf16[2,512,128]{2,1,0:T(8,128)(2,1)S(1)} %collective-permute-done.2.near, ...), custom_call_target="tpu_custom_call" | custom-call | flops 4000000000 | bytes 1048576 | tf_op jit(solution)/shard_map/pallas_call | solution.py:384
  73.9 2.3 %all-to-all-done.1 = bf16[32,56,128]{2,1,0:T(8,128)(2,1)S(1)} async-done(((bf16[32,56,128]{2,1,0:T(8,128)(2,1)}), bf16[32,56,128]{2,1,0:T(8,128)(2,1)S(1)}, u32[]{:S(2)}, u32[]{:S(2)}) %all-to-all-start.1) | async-done | bytes 458784 | tf_op jit(solution)/shard_map/all_to_all | solution.py:409
  76.2 3.7 %collective-permute-start.9 = (bf16[1792,128]{1,0:T(8,128)(2,1)S(1)}, bf16[1792,128]{1,0:T(8,128)(2,1)S(1)}, u32[]{:S(2)}, u32[]{:S(2)}) collective-permute-start(bf16[1792,128]{1,0:T(8,128)(2,1)S(1)} %bitcast.10), channel_id=1, source_target_pairs={{0,64},{64,0},{1,65},{65,1},{2,66},{66,2},{3,67},{67,3},{4,68},{68... | collective-permute-start | bytes 1376264 | tf_op jit(solution)/shard_map/ppermute | solution.py:405
  79.9 1.5 %shard_map.86.grad_in = f32[27,128,128]{2,1,0:T(8,128)} custom-call(s32[2]{0:T(128)S(1)} %pad_add_fusion.flags, bf16[1792,128]{1,0:T(8,128)(2,1)S(1)} %bitcast.11), custom_call_target="tpu_custom_call" | custom-call | flops 1000000000 | bytes 1048576 | tf_op jit(solution)/shard_map/pallas_call | solution.py:384
  81.4 0.0 collective-permute-done.9.half_grad
  81.4 1.5 %shard_map.87 = f32[27,128,128]{2,1,0:T(8,128)} custom-call(s32[2]{0:T(128)S(1)} %pad_add_fusion.flags, bf16[1792,128]{1,0:T(8,128)(2,1)S(1)} %collective-permute-done.9.half_grad, f32[27,128,128]{2,1,0:T(8,128)} %shard_map.86.grad_in), custom_call_target="tpu_custom_call", output_to_operand_aliasing={{}: (2, {})} | custom-call | bytes 1048576 | tf_op jit(solution)/shard_map/pallas_call | solution.py:384
  (4 shorter events, 0.0 us)
Async XLA Ops:
  2.0 14.2 %collective-permute-start = (f32[8,128]{1,0:T(8,128)S(1)}, f32[8,128]{1,0:T(8,128)S(1)}, u32[]{:S(2)}, u32[]{:S(2)}) collective-permute-start(f32[8,128]{1,0:T(8,128)S(1)} %shard_map.76.sums), channel_id=1, source_target_pairs={{0,128},{128,0},{1,129},{129,1},{2,130},{130,2},{3,131},{131,3},{4... | collective-permute-start | bytes 12296 | tf_op jit(solution)/shard_map/ppermute | solution.py:405
  11.5 12.0 %collective-permute-start.3 = (bf16[2,512,128]{2,1,0:T(8,128)(2,1)S(1)}, bf16[2,512,128]{2,1,0:T(8,128)(2,1)S(1)}, u32[]{:S(2)}, u32[]{:S(2)}) collective-permute-start(bf16[2,512,128]{2,1,0:T(8,128)(2,1)S(1)} %get-tuple-element.44), channel_id=1, source_target_pairs={{64,128},{128,64},{65,129},{129,65},{66,130},{130,66},{67,131},{13... | collective-permute-start | bytes 786440 | tf_op jit(solution)/shard_map/ppermute | solution.py:441
  16.2 1.3 %collective-permute-start.1 = (f32[8,128]{1,0:T(8,128)S(1)}, f32[8,128]{1,0:T(8,128)S(1)}, u32[]{:S(2)}, u32[]{:S(2)}) collective-permute-start(f32[8,128]{1,0:T(8,128)S(1)} %add.10), channel_id=1, source_target_pairs={{0,64},{64,0},{1,65},{65,1},{2,66},{66,2},{3,67},{67,3},{4,68},{68... | collective-permute-start | bytes 12296 | tf_op jit(solution)/shard_map/ppermute | solution.py:405
  16.3 7.2 %collective-permute-start.2 = (bf16[2,512,128]{2,1,0:T(8,128)(2,1)S(1)}, bf16[2,512,128]{2,1,0:T(8,128)(2,1)S(1)}, u32[]{:S(2)}, u32[]{:S(2)}) collective-permute-start(bf16[2,512,128]{2,1,0:T(8,128)(2,1)S(1)} %get-tuple-element.43), channel_id=1, source_target_pairs={{0,64},{64,0},{1,65},{65,1},{2,66},{66,2},{3,67},{67,3},{4,68},{68... | collective-permute-start | bytes 786440 | tf_op jit(solution)/shard_map/ppermute | solution.py:405
  24.9 2.6 %collective-permute-start.4 = (f32[1792,128]{1,0:T(8,128)S(1)}, f32[1792,128]{1,0:T(8,128)S(1)}, u32[]{:S(2)}, u32[]{:S(2)}) collective-permute-start(f32[1792,128]{1,0:T(8,128)S(1)} %get-tuple-element.50), channel_id=1, source_target_pairs={{0,64},{64,0},{1,65},{65,1},{2,66},{66,2},{3,67},{67,3},{4,68},{68... | collective-permute-start | bytes 2752520 | tf_op jit(solution)/shard_map/ppermute | solution.py:405
  28.5 24.5 %all-to-all-start = ((f32[32,56,128]{2,1,0:T(8,128)}), f32[32,56,128]{2,1,0:T(8,128)S(1)}, u32[]{:S(2)}, u32[]{:S(2)}) async-start(f32[32,56,128]{2,1,0:T(8,128)} %bitcast.6), calls=%async_computation | async-start | bytes 1835008 | tf_op jit(solution)/shard_map/all_to_all | solution.py:409
  45.3 1.3 %collective-permute-start.5 = (f32[8,128]{1,0:T(8,128)S(1)}, f32[8,128]{1,0:T(8,128)S(1)}, u32[]{:S(2)}, u32[]{:S(2)}) collective-permute-start(f32[8,128]{1,0:T(8,128)S(1)} %get-tuple-element.51), channel_id=1, source_target_pairs={{0,64},{64,0},{1,65},{65,1},{2,66},{66,2},{3,67},{67,3},{4,68},{68... | collective-permute-start | bytes 12296 | tf_op jit(solution)/shard_map/ppermute | solution.py:405
  53.1 5.7 %collective-permute-start.8 = (f32[64,128]{1,0:T(8,128)S(1)}, f32[64,128]{1,0:T(8,128)S(1)}, u32[]{:S(2)}, u32[]{:S(2)}) collective-permute-start(f32[64,128]{1,0:T(8,128)S(1)} %shard_map.83.own), channel_id=1, source_target_pairs={{0,136},{8,128},{128,8},{136,0},{1,137},{9,129},{129,9},{137,1},{2... | collective-permute-start | bytes 98312 | tf_op jit(solution)/shard_map/ppermute | solution.py:501
  53.2 6.9 %collective-permute-start.7 = (f32[64,128]{1,0:T(8,128)S(1)}, f32[64,128]{1,0:T(8,128)S(1)}, u32[]{:S(2)}, u32[]{:S(2)}) collective-permute-start(f32[64,128]{1,0:T(8,128)S(1)} %shard_map.83.own), channel_id=1, source_target_pairs={{0,128},{8,136},{128,0},{136,8},{1,129},{9,137},{129,1},{137,9},{2... | collective-permute-start | bytes 98312 | tf_op jit(solution)/shard_map/ppermute | solution.py:501
  57.2 4.1 %collective-permute-start.6 = (f32[64,128]{1,0:T(8,128)S(1)}, f32[64,128]{1,0:T(8,128)S(1)}, u32[]{:S(2)}, u32[]{:S(2)}) collective-permute-start(f32[64,128]{1,0:T(8,128)S(1)} %shard_map.83.own), channel_id=1, source_target_pairs={{0,8},{8,0},{128,136},{136,128},{1,9},{9,1},{129,137},{137,129},{2... | collective-permute-start | bytes 98312 | tf_op jit(solution)/shard_map/ppermute | solution.py:501
  62.1 14.1 %all-to-all-start.1 = ((bf16[32,56,128]{2,1,0:T(8,128)(2,1)}), bf16[32,56,128]{2,1,0:T(8,128)(2,1)S(1)}, u32[]{:S(2)}, u32[]{:S(2)}) async-start(bf16[32,56,128]{2,1,0:T(8,128)(2,1)} %get-tuple-element.54), calls=%async_computation.1 | async-start | bytes 917504 | tf_op jit(solution)/shard_map/all_to_all | solution.py:409
  76.2 5.2 %collective-permute-start.9 = (bf16[1792,128]{1,0:T(8,128)(2,1)S(1)}, bf16[1792,128]{1,0:T(8,128)(2,1)S(1)}, u32[]{:S(2)}, u32[]{:S(2)}) collective-permute-start(bf16[1792,128]{1,0:T(8,128)(2,1)S(1)} %bitcast.10), channel_id=1, source_target_pairs={{0,64},{64,0},{1,65},{65,1},{2,66},{66,2},{3,67},{67,3},{4,68},{68... | collective-permute-start | bytes 1376264 | tf_op jit(solution)/shard_map/ppermute | solution.py:405

commit v10 on v9

--- a/solution.py
+++ b/solution.py
@@ -253,8 +253,15 @@
             send[at : at + C // 2] = send_in[at : at + C // 2] + other
 
 
-def add_kernel(keep, received, chip):
-    chip[...] = (keep[...] + received[...]).astype(chip.dtype)
+def add_kernel(keep, received, chip, chip_v, sem):
+    started = []
+    step = COMM // 4
+    for i in range(4):
+        piece = pl.ds(i * step, step)
+        chip_v[piece] = keep[piece] + received[piece]
+        started += copies(sem.at[pl.ds(i, 1)], (chip_v.at[piece], chip.at[piece]))
+    for copy in started:
+        copy.wait()
 
 
 def part_kernel(parts, sums, packed):
@@ -262,12 +269,15 @@
     packed[PART:] = sums[...]
 
 
-def merge_kernel(own, one, two, three, parts, backward):
+def merge_kernel(own, one, three, two, parts, backward, parts_v, sem):
     total = (own[...] + one[...]) + (two[...] + three[...])
     part = total[:PART].astype(BF16)
-    for i in range(SIDE):
-        parts[i] = part
+    for i in range(SIDE // 4):
+        parts_v[i] = part
+    started = copies(sem, *((parts_v, parts.at[pl.ds(i * (SIDE // 4), SIDE // 4)]) for i in range(4)))
     backward[...] = own[PART:] + two[PART:]
+    for copy in started:
+        copy.wait()
 
 
 def place_kernel(flags, half_grad, grad, grad_v, sem, first):
@@ -476,7 +486,14 @@
         scalars=1,
         aliases=((1, 0), (2, 1)),
     )
-    chip = call(add_kernel, shape(COMM, C, dtype=WIRE), [], keep, swap(send, "core"))
+    chip = call(
+        add_kernel,
+        shape(COMM, C),
+        [pltpu.VMEM((COMM, C), F32), sems(4)],
+        keep,
+        swap(send, "core"),
+        out_far=(0,),
+    )
     parts = exchange(chip.reshape(SIDE, PART, C), ("y", "zn", "x"))
     scaled, sums = call(
         back_kernel,
@@ -498,9 +515,14 @@
     )
     sums = sums + swap(sums, "core")
     packed = call(part_kernel, shape(PART + 8, C), [], parts, sums)
-    others = [lax.ppermute(packed, ("zh", "zm"), [(i, i ^ flip) for i in range(4)]) for flip in (1, 2, 3)]
+    others = [lax.ppermute(packed, ("zh", "zm"), [(i, i ^ flip) for i in range(4)]) for flip in (1, 3, 2)]
     part, backward = call(
-        merge_kernel, (shape(SIDE, PART, C, dtype=BF16), shape(8, C)), [], packed, *others
+        merge_kernel,
+        (shape(SIDE, PART, C, dtype=BF16), shape(8, C)),
+        [pltpu.VMEM((SIDE // 4, PART, C), BF16), sems(4)],
+        packed,
+        *others,
+        out_far=(0,),
     )
     part, window = lax.optimization_barrier((part, window))
     block = shape(T, ROWS, W, dtype=BF16)
@@ -548,9 +570,6 @@
     return output.reshape(latents.shape), result.reshape(latents.shape), kernel_grad
 
 
-WIRE = F32
-
-
 def solution(mesh):
     fine = Mesh(mesh.devices.reshape(2, 2, 4, 2, 2, 4), ("zh", "core", "y", "zm", "zn", "x"))
     frames = P(("y", "zm", "zn", "x"), ("zh", "core"), None, None, None)

time: 83.4 us -> 83.4 us (level)
  no operation moved by 1% of the time
where the time goes in v10:
time: 83.4 us; the launch traced here: 83 us
  starting transfers between devices  36.5 us (44%)
  Pallas kernels  27.5 us (33%)
  waiting for transfers between devices  18 us (22%)
  between operations  0.95 us (1%)
    pallas_call x12, Pallas kernels, call(): pl.pallas_call(body, out_shape=shapes[0] if single else shapes, in_specs=...  27.5 us
    all_to_all x2, starting transfers between devices, exchange(): return lax.all_to_all(parts, axes, 0, 0)  15.7 us
    ppermute x6, starting transfers between devices, swap(): return lax.ppermute(value, axis, [(0, 1), (1, 0)])  12.1 us
    all_to_all x2, waiting for transfers between devices, exchange(): return lax.all_to_all(parts, axes, 0, 0)  8.8 us
    ppermute x3, starting transfers between devices, per_device(): lax.ppermute(packed, ('zh', 'zm'), [(i, i ^ flip) for i in range(4)])  5.74 us
    ppermute x6, waiting for transfers between devices, swap(): return lax.ppermute(value, axis, [(0, 1), (1, 0)])  3.94 us
    ppermute x1, starting transfers between devices, per_device(): before = lax.ppermute(to_far, slab, [(1, 2), (2, 1)])  2.95 us
    ppermute x1, waiting for transfers between devices, per_device(): before = lax.ppermute(to_far, slab, [(1, 2), (2, 1)])  2.82 us
  transfers between devices with their start and end apart: 12, of which 8 were waited for; matrix products, arithmetic and copies ran while one was open for 0% of the time, Pallas kernels for 26%

profile of v10, /device:TPU:1, one launch (start us, length us, event | category | flops | bytes accessed | tf_op | source)
XLA Modules:
  0.0 83.0 jit_solution(17289008352680143571)
XLA Ops:
  0.6 1.3 %shard_map.76.sums = f32[8,128]{1,0:T(8,128)S(1)} custom-call(bf16[4,512,128]{2,1,0:T(8,128)(2,1)} %bitcast.12), custom_call_target="tpu_custom_call" | custom-call | bytes 1048576 | tf_op jit(solution)/shard_map/pallas_call | solution.py:394
  2.0 7.8 %collective-permute-start = (f32[8,128]{1,0:T(8,128)S(1)}, f32[8,128]{1,0:T(8,128)S(1)}, u32[]{:S(2)}, u32[]{:S(2)}) collective-permute-start(f32[8,128]{1,0:T(8,128)S(1)} %shard_map.76.sums), channel_id=1, source_target_pairs={{0,128},{128,0},{1,129},{129,1},{2,130},{130,2},{3,131},{131,3},{4... | collective-permute-start | bytes 12296 | tf_op jit(solution)/shard_map/ppermute | solution.py:415
  9.8 0.1 pad_add_fusion.flags
  9.9 1.6 %shard_map.77 = (bf16[2,512,128]{2,1,0:T(8,128)(2,1)S(1)}, bf16[2,512,128]{2,1,0:T(8,128)(2,1)S(1)}) custom-call(s32[2]{0:T(128)S(1)} %pad_add_fusion.flags, f32[8,128]{1,0:T(8,128)S(1)} %shard_map.76.sums, bf16[4,512,128]{2,1,0:T(8,128)(2,1)} %bitcast.13, bf16[4,512,128]{2,1,0:T(8,128)(2,1)} %bitcast.18), custom_call_target="tpu_custom_call" | custom-call | bytes 1048576 | tf_op jit(solution)/shard_map/pallas_call | solution.py:394
  11.5 2.9 %collective-permute-start.3 = (bf16[2,512,128]{2,1,0:T(8,128)(2,1)S(1)}, bf16[2,512,128]{2,1,0:T(8,128)(2,1)S(1)}, u32[]{:S(2)}, u32[]{:S(2)}) collective-permute-start(bf16[2,512,128]{2,1,0:T(8,128)(2,1)S(1)} %get-tuple-element.44), channel_id=1, source_target_pairs={{64,128},{128,64},{65,129},{129,65},{66,130},{130,66},{67,131},{13... | collective-permute-start | bytes 786440 | tf_op jit(solution)/shard_map/ppermute | solution.py:451
  14.4 1.7 %shard_map.78 = (bf16[512,2048]{1,0:T(8,128)(2,1)S(1)}, f32[2,128,128]{2,1,0:T(8,128)S(1)}) custom-call(bf16[4,512,128]{2,1,0:T(8,128)(2,1)} %bitcast.14, bf16[4,512,128]{2,1,0:T(8,128)(2,1)} %bitcast.19, f32[1,128]{1,0:T(1,128)} %bitcast.22, f32[1,128]{1,0:T(1,128)} %bitcast.23), custom_call_target="tpu_custom_call" | custom-call | bytes 1048576 | tf_op jit(solution)/shard_map/pallas_call | solution.py:394
  16.2 0.0 collective-permute-done
  16.2 0.1 collective-permute-start.1
  16.3 0.5 collective-permute-start.2
  16.8 0.7 collective-permute-done.1
  17.4 3.2 %shard_map.79 = (bf16[1536,512]{1,0:T(8,128)(2,1)}, f32[1792,128]{1,0:T(8,128)S(1)}, f32[1792,128]{1,0:T(8,128)S(1)}, bf16[384,1024]{1,0:T(8,128)(2,1)S(1)}) custom-call(s32[2]{0:T(128)S(1)} %pad_add_fusion.flags, bf16[512,2048]{1,0:T(8,128)(2,1)S(1)} %get-tuple-element.35.adj, f32[16,128]{1,0:T(8,128)S(1)} %constant_dynamic-update-slice_fusion.totals, ...), custom_call_target="tpu_custom_call" | custom-call | flops 2000000000 | bytes 1048576 | tf_op jit(solution)/shard_map/pallas_call | solution.py:394
  20.6 2.8 %collective-permute-done.3.far = bf16[2,512,128]{2,1,0:T(8,128)(2,1)S(1)} collective-permute-done((bf16[2,512,128]{2,1,0:T(8,128)(2,1)S(1)}, bf16[2,512,128]{2,1,0:T(8,128)(2,1)S(1)}, u32[]{:S(2)}, u32[]{:S(2)}) %collective-permute-start.3) | collective-permute-done | bytes 262176 | tf_op jit(solution)/shard_map/ppermute | solution.py:451
  23.4 0.0 collective-permute-done.2.near
  23.4 1.4 %shard_map.80 = (f32[1792,128]{1,0:T(8,128)S(1)}, f32[1792,128]{1,0:T(8,128)S(1)}) custom-call(s32[2]{0:T(128)S(1)} %pad_add_fusion.flags, f32[1792,128]{1,0:T(8,128)S(1)} %get-tuple-element.41.keep_in, f32[1792,128]{1,0:T(8,128)S(1)} %get-tuple-element.42.send_in, ...), custom_call_target="tpu_custom_call", output_to_operand_aliasing={{0}: (1, {}), {1}: (2, {})} | custom-call | bytes 1048576 | tf_op jit(solution)/shard_map/pallas_call | solution.py:394
  24.9 0.1 collective-permute-start.4
  25.0 2.5 %collective-permute-done.4.received = f32[1792,128]{1,0:T(8,128)S(1)} collective-permute-done((f32[1792,128]{1,0:T(8,128)S(1)}, f32[1792,128]{1,0:T(8,128)S(1)}, u32[]{:S(2)}, u32[]{:S(2)}) %collective-permute-start.4) | collective-permute-done | bytes 917536 | tf_op jit(solution)/shard_map/ppermute | solution.py:415
  27.5 1.0 %shard_map.81 = f32[1792,128]{1,0:T(8,128)} custom-call(f32[1792,128]{1,0:T(8,128)S(1)} %get-tuple-element.49.keep, f32[1792,128]{1,0:T(8,128)S(1)} %collective-permute-done.4.received), custom_call_target="tpu_custom_call" | custom-call | bytes 1048576 | tf_op jit(solution)/shard_map/pallas_call | solution.py:394
  28.5 9.9 %all-to-all-start = ((f32[32,56,128]{2,1,0:T(8,128)}), f32[32,56,128]{2,1,0:T(8,128)S(1)}, u32[]{:S(2)}, u32[]{:S(2)}) async-start(f32[32,56,128]{2,1,0:T(8,128)} %bitcast.17), calls=%async_computation | async-start | bytes 1835008 | tf_op jit(solution)/shard_map/all_to_all | solution.py:419
  38.4 6.8 %shard_map.82 = (f32[4,512,128]{2,1,0:T(8,128)}, f32[8,128]{1,0:T(8,128)S(1)}) custom-call(s32[2]{0:T(128)S(1)} %pad_add_fusion.flags, bf16[4,512,128]{2,1,0:T(8,128)(2,1)} %bitcast.15, bf16[4,512,128]{2,1,0:T(8,128)(2,1)} %bitcast.20, bf16[2,512,128]{2,1,0:T(8,128)(2,1)S(1)} %collective-permute-done.2.near, ...), custom_call_target="tpu_custom_call" | custom-call | flops 4000000000 | bytes 1048576 | tf_op jit(solution)/shard_map/pallas_call | solution.py:394
  45.2 0.5 collective-permute-start.5
  45.7 0.8 collective-permute-done.5
  46.6 6.4 %all-to-all-done.parts = f32[32,56,128]{2,1,0:T(8,128)S(1)} async-done(((f32[32,56,128]{2,1,0:T(8,128)}), f32[32,56,128]{2,1,0:T(8,128)S(1)}, u32[]{:S(2)}, u32[]{:S(2)}) %all-to-all-start) | async-done | bytes 917536 | tf_op jit(solution)/shard_map/all_to_all | solution.py:419
  53.0 0.1 shard_map.83.own
  53.1 0.2 collective-permute-start.8
  53.3 3.8 %collective-permute-start.7 = (f32[64,128]{1,0:T(8,128)S(1)}, f32[64,128]{1,0:T(8,128)S(1)}, u32[]{:S(2)}, u32[]{:S(2)}) collective-permute-start(f32[64,128]{1,0:T(8,128)S(1)} %shard_map.83.own), channel_id=1, source_target_pairs={{0,136},{8,128},{128,8},{136,0},{1,137},{9,129},{129,9},{137,1},{2... | collective-permute-start | bytes 98312 | tf_op jit(solution)/shard_map/ppermute | solution.py:518
  57.1 1.7 %collective-permute-start.6 = (f32[64,128]{1,0:T(8,128)S(1)}, f32[64,128]{1,0:T(8,128)S(1)}, u32[]{:S(2)}, u32[]{:S(2)}) collective-permute-start(f32[64,128]{1,0:T(8,128)S(1)} %shard_map.83.own), channel_id=1, source_target_pairs={{0,8},{8,0},{128,136},{136,128},{1,9},{9,1},{129,137},{137,129},{2... | collective-permute-start | bytes 98312 | tf_op jit(solution)/shard_map/ppermute | solution.py:518
  58.8 1.0 %collective-permute-done.8.two = f32[64,128]{1,0:T(8,128)S(1)} collective-permute-done((f32[64,128]{1,0:T(8,128)S(1)}, f32[64,128]{1,0:T(8,128)S(1)}, u32[]{:S(2)}, u32[]{:S(2)}) %collective-permute-start.8) | collective-permute-done | bytes 32800 | tf_op jit(solution)/shard_map/ppermute | solution.py:518
  59.8 0.0 collective-permute-done.7.three
  59.8 1.4 %collective-permute-done.6.one = f32[64,128]{1,0:T(8,128)S(1)} collective-permute-done((f32[64,128]{1,0:T(8,128)S(1)}, f32[64,128]{1,0:T(8,128)S(1)}, u32[]{:S(2)}, u32[]{:S(2)}) %collective-permute-start.6) | collective-permute-done | bytes 32800 | tf_op jit(solution)/shard_map/ppermute | solution.py:518
  61.3 0.8 %shard_map.84 = (bf16[32,56,128]{2,1,0:T(8,128)(2,1)}, f32[8,128]{1,0:T(8,128)S(1)}) custom-call(f32[64,128]{1,0:T(8,128)S(1)} %shard_map.83.own, f32[64,128]{1,0:T(8,128)S(1)} %collective-permute-done.6.one, f32[64,128]{1,0:T(8,128)S(1)} %collective-permute-done.7.three, f32[64,128]{1,0:T(8,128)S(1)} %collective-permute-done.8.two), custom_call_target="tpu_custom_call" | custom-call | bytes 1048576 | tf_op jit(solution)/shard_map/pallas_call | solution.py:394
  62.1 5.8 %all-to-all-start.1 = ((bf16[32,56,128]{2,1,0:T(8,128)(2,1)}), bf16[32,56,128]{2,1,0:T(8,128)(2,1)S(1)}, u32[]{:S(2)}, u32[]{:S(2)}) async-start(bf16[32,56,128]{2,1,0:T(8,128)(2,1)} %get-tuple-element.54), calls=%async_computation.1 | async-start | bytes 917504 | tf_op jit(solution)/shard_map/all_to_all | solution.py:419
  67.9 6.5 %shard_map.85 = (bf16[4,512,128]{2,1,0:T(8,128)(2,1)}, bf16[4,512,128]{2,1,0:T(8,128)(2,1)}) custom-call(s32[2]{0:T(128)S(1)} %pad_add_fusion.flags, bf16[4,512,128]{2,1,0:T(8,128)(2,1)} %bitcast.16, bf16[4,512,128]{2,1,0:T(8,128)(2,1)} %bitcast.21, bf16[2,512,128]{2,1,0:T(8,128)(2,1)S(1)} %collective-permute-done.2.near, ...), custom_call_target="tpu_custom_call" | custom-call | flops 4000000000 | bytes 1048576 | tf_op jit(solution)/shard_map/pallas_call | solution.py:394
  74.4 2.4 %all-to-all-done.1 = bf16[32,56,128]{2,1,0:T(8,128)(2,1)S(1)} async-done(((bf16[32,56,128]{2,1,0:T(8,128)(2,1)}), bf16[32,56,128]{2,1,0:T(8,128)(2,1)S(1)}, u32[]{:S(2)}, u32[]{:S(2)}) %all-to-all-start.1) | async-done | bytes 458784 | tf_op jit(solution)/shard_map/all_to_all | solution.py:419
  76.8 3.1 %collective-permute-start.9 = (bf16[1792,128]{1,0:T(8,128)(2,1)S(1)}, bf16[1792,128]{1,0:T(8,128)(2,1)S(1)}, u32[]{:S(2)}, u32[]{:S(2)}) collective-permute-start(bf16[1792,128]{1,0:T(8,128)(2,1)S(1)} %bitcast.10), channel_id=1, source_target_pairs={{0,64},{64,0},{1,65},{65,1},{2,66},{66,2},{3,67},{67,3},{4,68},{68... | collective-permute-start | bytes 1376264 | tf_op jit(solution)/shard_map/ppermute | solution.py:415
  79.9 1.5 %shard_map.86.grad_in = f32[27,128,128]{2,1,0:T(8,128)} custom-call(s32[2]{0:T(128)S(1)} %pad_add_fusion.flags, bf16[1792,128]{1,0:T(8,128)(2,1)S(1)} %bitcast.11), custom_call_target="tpu_custom_call" | custom-call | flops 1000000000 | bytes 1048576 | tf_op jit(solution)/shard_map/pallas_call | solution.py:394
  81.4 0.0 collective-permute-done.9.half_grad
  81.4 1.5 %shard_map.87 = f32[27,128,128]{2,1,0:T(8,128)} custom-call(s32[2]{0:T(128)S(1)} %pad_add_fusion.flags, bf16[1792,128]{1,0:T(8,128)(2,1)S(1)} %collective-permute-done.9.half_grad, f32[27,128,128]{2,1,0:T(8,128)} %shard_map.86.grad_in), custom_call_target="tpu_custom_call", output_to_operand_aliasing={{}: (2, {})} | custom-call | bytes 1048576 | tf_op jit(solution)/shard_map/pallas_call | solution.py:394
  (4 shorter events, 0.0 us)
Async XLA Ops:
  2.0 14.2 %collective-permute-start = (f32[8,128]{1,0:T(8,128)S(1)}, f32[8,128]{1,0:T(8,128)S(1)}, u32[]{:S(2)}, u32[]{:S(2)}) collective-permute-start(f32[8,128]{1,0:T(8,128)S(1)} %shard_map.76.sums), channel_id=1, source_target_pairs={{0,128},{128,0},{1,129},{129,1},{2,130},{130,2},{3,131},{131,3},{4... | collective-permute-start | bytes 12296 | tf_op jit(solution)/shard_map/ppermute | solution.py:415
  11.5 12.0 %collective-permute-start.3 = (bf16[2,512,128]{2,1,0:T(8,128)(2,1)S(1)}, bf16[2,512,128]{2,1,0:T(8,128)(2,1)S(1)}, u32[]{:S(2)}, u32[]{:S(2)}) collective-permute-start(bf16[2,512,128]{2,1,0:T(8,128)(2,1)S(1)} %get-tuple-element.44), channel_id=1, source_target_pairs={{64,128},{128,64},{65,129},{129,65},{66,130},{130,66},{67,131},{13... | collective-permute-start | bytes 786440 | tf_op jit(solution)/shard_map/ppermute | solution.py:451
  16.2 1.3 %collective-permute-start.1 = (f32[8,128]{1,0:T(8,128)S(1)}, f32[8,128]{1,0:T(8,128)S(1)}, u32[]{:S(2)}, u32[]{:S(2)}) collective-permute-start(f32[8,128]{1,0:T(8,128)S(1)} %add.10), channel_id=1, source_target_pairs={{0,64},{64,0},{1,65},{65,1},{2,66},{66,2},{3,67},{67,3},{4,68},{68... | collective-permute-start | bytes 12296 | tf_op jit(solution)/shard_map/ppermute | solution.py:415
  16.3 7.2 %collective-permute-start.2 = (bf16[2,512,128]{2,1,0:T(8,128)(2,1)S(1)}, bf16[2,512,128]{2,1,0:T(8,128)(2,1)S(1)}, u32[]{:S(2)}, u32[]{:S(2)}) collective-permute-start(bf16[2,512,128]{2,1,0:T(8,128)(2,1)S(1)} %get-tuple-element.43), channel_id=1, source_target_pairs={{0,64},{64,0},{1,65},{65,1},{2,66},{66,2},{3,67},{67,3},{4,68},{68... | collective-permute-start | bytes 786440 | tf_op jit(solution)/shard_map/ppermute | solution.py:415
  24.9 2.6 %collective-permute-start.4 = (f32[1792,128]{1,0:T(8,128)S(1)}, f32[1792,128]{1,0:T(8,128)S(1)}, u32[]{:S(2)}, u32[]{:S(2)}) collective-permute-start(f32[1792,128]{1,0:T(8,128)S(1)} %get-tuple-element.50), channel_id=1, source_target_pairs={{0,64},{64,0},{1,65},{65,1},{2,66},{66,2},{3,67},{67,3},{4,68},{68... | collective-permute-start | bytes 2752520 | tf_op jit(solution)/shard_map/ppermute | solution.py:415
  28.5 24.6 %all-to-all-start = ((f32[32,56,128]{2,1,0:T(8,128)}), f32[32,56,128]{2,1,0:T(8,128)S(1)}, u32[]{:S(2)}, u32[]{:S(2)}) async-start(f32[32,56,128]{2,1,0:T(8,128)} %bitcast.17), calls=%async_computation | async-start | bytes 1835008 | tf_op jit(solution)/shard_map/all_to_all | solution.py:419
  45.2 1.3 %collective-permute-start.5 = (f32[8,128]{1,0:T(8,128)S(1)}, f32[8,128]{1,0:T(8,128)S(1)}, u32[]{:S(2)}, u32[]{:S(2)}) collective-permute-start(f32[8,128]{1,0:T(8,128)S(1)} %get-tuple-element.51), channel_id=1, source_target_pairs={{0,64},{64,0},{1,65},{65,1},{2,66},{66,2},{3,67},{67,3},{4,68},{68... | collective-permute-start | bytes 12296 | tf_op jit(solution)/shard_map/ppermute | solution.py:415
  53.1 6.8 %collective-permute-start.8 = (f32[64,128]{1,0:T(8,128)S(1)}, f32[64,128]{1,0:T(8,128)S(1)}, u32[]{:S(2)}, u32[]{:S(2)}) collective-permute-start(f32[64,128]{1,0:T(8,128)S(1)} %shard_map.83.own), channel_id=1, source_target_pairs={{0,128},{8,136},{128,0},{136,8},{1,129},{9,137},{129,1},{137,9},{2... | collective-permute-start | bytes 98312 | tf_op jit(solution)/shard_map/ppermute | solution.py:518
  53.3 6.6 %collective-permute-start.7 = (f32[64,128]{1,0:T(8,128)S(1)}, f32[64,128]{1,0:T(8,128)S(1)}, u32[]{:S(2)}, u32[]{:S(2)}) collective-permute-start(f32[64,128]{1,0:T(8,128)S(1)} %shard_map.83.own), channel_id=1, source_target_pairs={{0,136},{8,128},{128,8},{136,0},{1,137},{9,129},{129,9},{137,1},{2... | collective-permute-start | bytes 98312 | tf_op jit(solution)/shard_map/ppermute | solution.py:518
  57.1 4.2 %collective-permute-start.6 = (f32[64,128]{1,0:T(8,128)S(1)}, f32[64,128]{1,0:T(8,128)S(1)}, u32[]{:S(2)}, u32[]{:S(2)}) collective-permute-start(f32[64,128]{1,0:T(8,128)S(1)} %shard_map.83.own), channel_id=1, source_target_pairs={{0,8},{8,0},{128,136},{136,128},{1,9},{9,1},{129,137},{137,129},{2... | collective-permute-start | bytes 98312 | tf_op jit(solution)/shard_map/ppermute | solution.py:518
  62.1 14.7 %all-to-all-start.1 = ((bf16[32,56,128]{2,1,0:T(8,128)(2,1)}), bf16[32,56,128]{2,1,0:T(8,128)(2,1)S(1)}, u32[]{:S(2)}, u32[]{:S(2)}) async-start(bf16[32,56,128]{2,1,0:T(8,128)(2,1)} %get-tuple-element.54), calls=%async_computation.1 | async-start | bytes 917504 | tf_op jit(solution)/shard_map/all_to_all | solution.py:419
  76.8 4.6 %collective-permute-start.9 = (bf16[1792,128]{1,0:T(8,128)(2,1)S(1)}, bf16[1792,128]{1,0:T(8,128)(2,1)S(1)}, u32[]{:S(2)}, u32[]{:S(2)}) collective-permute-start(bf16[1792,128]{1,0:T(8,128)(2,1)S(1)} %bitcast.10), channel_id=1, source_target_pairs={{0,64},{64,0},{1,65},{65,1},{2,66},{66,2},{3,67},{67,3},{4,68},{68... | collective-permute-start | bytes 1376264 | tf_op jit(solution)/shard_map/ppermute | solution.py:415

commit v11 on v10

--- a/solution.py
+++ b/solution.py
@@ -71,8 +71,18 @@
     return started
 
 
-def start_kernel(lat, sums, lat_v, sem):
+def start_kernel(flags, lat, cot, sums, near, far, lat_v, sem, halo_sem):
     parts = copies(sem, *((lat.at[t], lat_v.at[t]) for t in range(T)))
+    tail, head = lat.at[T - HALO :], cot.at[:HALO]
+
+    @pl.when(flags[1] == 0)
+    def _():
+        copies(halo_sem, (tail, near), (head, far))
+
+    @pl.when(flags[1] != 0)
+    def _():
+        copies(halo_sem, (head, near), (tail, far))
+
     total = jnp.zeros((ROWS, W), F32)
     square = jnp.zeros((ROWS, W), F32)
     for t in range(T):
@@ -84,6 +94,8 @@
     square = jnp.sum(jnp.sum(square.reshape(GROUPS, -1, W), axis=1), axis=1, keepdims=True)
     row = row_of(total, 0) + row_of(square, GROUPS)
     sums[...] = jnp.broadcast_to(row, (8, W))
+    pltpu.make_async_copy(tail, near, halo_sem.at[0]).wait()
+    pltpu.make_async_copy(head, far, halo_sem.at[1]).wait()
 
 
 def put_adjoint(adj, f, mine):
@@ -93,21 +105,6 @@
             source = h - ki + 1
             block = mine[source].astype(BF16) if 0 <= source < H else zero
             adj[ki * C : (ki + 1) * C, (f * H + h) * W : (f * H + h + 1) * W] = block
-
-
-def halo_kernel(flags, sums, lat, cot, near, far, sem):
-    tail, head = lat.at[T - HALO :], cot.at[:HALO]
-
-    @pl.when(flags[1] == 0)
-    def _():
-        copies(sem, (tail, near), (head, far))
-
-    @pl.when(flags[1] != 0)
-    def _():
-        copies(sem, (head, near), (tail, far))
-
-    pltpu.make_async_copy(tail, near, sem.at[0]).wait()
-    pltpu.make_async_copy(head, far, sem.at[1]).wait()
 
 
 def prepare_kernel(lat, cot, gain, shift, adj, scales, lat_v, cot_v, gain_v, shift_v, tmp, sem):
@@ -433,8 +430,16 @@
     taps = pltpu.VMEM((3, ROWS, 3 * ROWS), BF16)
     kernel_scratch = pltpu.VMEM((27, C, C), BF16)
     scaled_scratch = pltpu.VMEM((T, ROWS, W), F32)
-    own = call(start_kernel, shape(8, W), [frames, sems(T)], lat, far=(0,))
-    to_near, to_far = call(halo_kernel, (halo, halo), [sems(2)], flags, own, lat, cot, far=(2, 3), scalars=1)
+    own, to_near, to_far = call(
+        start_kernel,
+        (shape(8, W), halo, halo),
+        [frames, sems(T), sems(2)],
+        flags,
+        lat,
+        cot,
+        far=(1, 2),
+        scalars=1,
+    )
     gain, to_far = lax.optimization_barrier((gain, to_far))
     adj, scales = call(
         prepare_kernel,

time: 83.4 us -> 82.5 us (0.989)
  Pallas kernels: 27.5 us -> 26.5 us
    pallas_call x12 -> x11, Pallas kernels: 27.5 us -> 26.5 us  [call(): pl.pallas_call(body, out_shape=shapes[0] if single else shapes, in_specs=...]
  transfers between devices with their start and end apart: 12 -> 12, of which waited for: 8 -> 8; matrix products, arithmetic and copies ran while one was open for 0% -> 0% of each run, Pallas kernels for 26% -> 24%
where the time goes in v11:
time: 82.5 us; the launch traced here: 82.1 us
  starting transfers between devices  36.7 us (44%)
  Pallas kernels  26.5 us (32%)
  waiting for transfers between devices  17.8 us (22%)
  between operations  0.95 us (1%)
    pallas_call x11, Pallas kernels, call(): pl.pallas_call(body, out_shape=shapes[0] if single else shapes, in_specs=...  26.5 us
    all_to_all x2, starting transfers between devices, exchange(): return lax.all_to_all(parts, axes, 0, 0)  15.3 us
    ppermute x6, starting transfers between devices, swap(): return lax.ppermute(value, axis, [(0, 1), (1, 0)])  12.7 us
    all_to_all x2, waiting for transfers between devices, exchange(): return lax.all_to_all(parts, axes, 0, 0)  8.72 us
    ppermute x3, starting transfers between devices, per_device(): lax.ppermute(packed, ('zh', 'zm'), [(i, i ^ flip) for i in range(4)])  5.74 us
    ppermute x6, waiting for transfers between devices, swap(): return lax.ppermute(value, axis, [(0, 1), (1, 0)])  3.94 us
    ppermute x1, starting transfers between devices, per_device(): before = lax.ppermute(to_far, slab, [(1, 2), (2, 1)])  3 us
    ppermute x1, waiting for transfers between devices, per_device(): before = lax.ppermute(to_far, slab, [(1, 2), (2, 1)])  2.82 us
  transfers between devices with their start and end apart: 12, of which 8 were waited for; matrix products, arithmetic and copies ran while one was open for 0% of the time, Pallas kernels for 24%

profile of v11, /device:TPU:1, one launch (start us, length us, event | category | flops | bytes accessed | tf_op | source)
XLA Modules:
  0.0 82.1 jit_solution(15194224621222625205)
XLA Ops:
  0.6 0.1 pad_add_fusion.flags
  0.7 2.0 %shard_map.76 = (f32[8,128]{1,0:T(8,128)S(1)}, bf16[2,512,128]{2,1,0:T(8,128)(2,1)S(1)}, bf16[2,512,128]{2,1,0:T(8,128)(2,1)S(1)}) custom-call(s32[2]{0:T(128)S(1)} %pad_add_fusion.flags, bf16[4,512,128]{2,1,0:T(8,128)(2,1)} %bitcast.13, bf16[4,512,128]{2,1,0:T(8,128)(2,1)} %bitcast.17), custom_call_target="tpu_custom_call" | custom-call | bytes 1048576 | tf_op jit(solution)/shard_map/pallas_call | solution.py:391
  2.7 7.8 %collective-permute-start = (f32[8,128]{1,0:T(8,128)S(1)}, f32[8,128]{1,0:T(8,128)S(1)}, u32[]{:S(2)}, u32[]{:S(2)}) collective-permute-start(f32[8,128]{1,0:T(8,128)S(1)} %get-tuple-element.38), channel_id=1, source_target_pairs={{0,128},{128,0},{1,129},{129,1},{2,130},{130,2},{3,131},{131,3},{4... | collective-permute-start | bytes 12296 | tf_op jit(solution)/shard_map/ppermute | solution.py:412
  10.5 3.0 %collective-permute-start.3 = (bf16[2,512,128]{2,1,0:T(8,128)(2,1)S(1)}, bf16[2,512,128]{2,1,0:T(8,128)(2,1)S(1)}, u32[]{:S(2)}, u32[]{:S(2)}) collective-permute-start(bf16[2,512,128]{2,1,0:T(8,128)(2,1)S(1)} %get-tuple-element.46), channel_id=1, source_target_pairs={{64,128},{128,64},{65,129},{129,65},{66,130},{130,66},{67,131},{13... | collective-permute-start | bytes 786440 | tf_op jit(solution)/shard_map/ppermute | solution.py:456
  13.5 1.7 %shard_map.77 = (bf16[512,2048]{1,0:T(8,128)(2,1)S(1)}, f32[2,128,128]{2,1,0:T(8,128)S(1)}) custom-call(bf16[4,512,128]{2,1,0:T(8,128)(2,1)} %bitcast.14, bf16[4,512,128]{2,1,0:T(8,128)(2,1)} %bitcast.18, f32[1,128]{1,0:T(1,128)} %bitcast.21, f32[1,128]{1,0:T(1,128)} %bitcast.22), custom_call_target="tpu_custom_call" | custom-call | bytes 1048576 | tf_op jit(solution)/shard_map/pallas_call | solution.py:391
  15.3 0.0 collective-permute-done
  15.3 0.1 collective-permute-start.1
  15.4 0.5 collective-permute-start.2
  15.9 0.7 collective-permute-done.1
  16.5 3.2 %shard_map.78 = (bf16[1536,512]{1,0:T(8,128)(2,1)}, f32[1792,128]{1,0:T(8,128)S(1)}, f32[1792,128]{1,0:T(8,128)S(1)}, bf16[384,1024]{1,0:T(8,128)(2,1)S(1)}) custom-call(s32[2]{0:T(128)S(1)} %pad_add_fusion.flags, bf16[512,2048]{1,0:T(8,128)(2,1)S(1)} %get-tuple-element.36.adj, f32[16,128]{1,0:T(8,128)S(1)} %constant_dynamic-update-slice_fusion.totals, ...), custom_call_target="tpu_custom_call" | custom-call | flops 2000000000 | bytes 1048576 | tf_op jit(solution)/shard_map/pallas_call | solution.py:391
  19.7 2.8 %collective-permute-done.3.far = bf16[2,512,128]{2,1,0:T(8,128)(2,1)S(1)} collective-permute-done((bf16[2,512,128]{2,1,0:T(8,128)(2,1)S(1)}, bf16[2,512,128]{2,1,0:T(8,128)(2,1)S(1)}, u32[]{:S(2)}, u32[]{:S(2)}) %collective-permute-start.3) | collective-permute-done | bytes 262176 | tf_op jit(solution)/shard_map/ppermute | solution.py:456
  22.5 0.0 collective-permute-done.2.near
  22.6 1.4 %shard_map.79 = (f32[1792,128]{1,0:T(8,128)S(1)}, f32[1792,128]{1,0:T(8,128)S(1)}) custom-call(s32[2]{0:T(128)S(1)} %pad_add_fusion.flags, f32[1792,128]{1,0:T(8,128)S(1)} %get-tuple-element.43.keep_in, f32[1792,128]{1,0:T(8,128)S(1)} %get-tuple-element.44.send_in, ...), custom_call_target="tpu_custom_call", output_to_operand_aliasing={{0}: (1, {}), {1}: (2, {})} | custom-call | bytes 1048576 | tf_op jit(solution)/shard_map/pallas_call | solution.py:391
  24.0 0.1 collective-permute-start.4
  24.1 2.5 %collective-permute-done.4.received = f32[1792,128]{1,0:T(8,128)S(1)} collective-permute-done((f32[1792,128]{1,0:T(8,128)S(1)}, f32[1792,128]{1,0:T(8,128)S(1)}, u32[]{:S(2)}, u32[]{:S(2)}) %collective-permute-start.4) | collective-permute-done | bytes 917536 | tf_op jit(solution)/shard_map/ppermute | solution.py:412
  26.6 1.0 %shard_map.80 = f32[1792,128]{1,0:T(8,128)} custom-call(f32[1792,128]{1,0:T(8,128)S(1)} %get-tuple-element.51.keep, f32[1792,128]{1,0:T(8,128)S(1)} %collective-permute-done.4.received), custom_call_target="tpu_custom_call" | custom-call | bytes 1048576 | tf_op jit(solution)/shard_map/pallas_call | solution.py:391
  27.6 9.9 %all-to-all-start = ((f32[32,56,128]{2,1,0:T(8,128)}), f32[32,56,128]{2,1,0:T(8,128)S(1)}, u32[]{:S(2)}, u32[]{:S(2)}) async-start(f32[32,56,128]{2,1,0:T(8,128)} %bitcast.12), calls=%async_computation | async-start | bytes 1835008 | tf_op jit(solution)/shard_map/all_to_all | solution.py:416
  37.4 6.8 %shard_map.81 = (f32[4,512,128]{2,1,0:T(8,128)}, f32[8,128]{1,0:T(8,128)S(1)}) custom-call(s32[2]{0:T(128)S(1)} %pad_add_fusion.flags, bf16[4,512,128]{2,1,0:T(8,128)(2,1)} %bitcast.15, bf16[4,512,128]{2,1,0:T(8,128)(2,1)} %bitcast.19, bf16[2,512,128]{2,1,0:T(8,128)(2,1)S(1)} %collective-permute-done.2.near, ...), custom_call_target="tpu_custom_call" | custom-call | flops 4000000000 | bytes 1048576 | tf_op jit(solution)/shard_map/pallas_call | solution.py:391
  44.3 0.5 collective-permute-start.5
  44.8 0.8 %collective-permute-done.5 = f32[8,128]{1,0:T(8,128)S(1)} collective-permute-done((f32[8,128]{1,0:T(8,128)S(1)}, f32[8,128]{1,0:T(8,128)S(1)}, u32[]{:S(2)}, u32[]{:S(2)}) %collective-permute-start.5) | collective-permute-done | bytes 4128 | tf_op jit(solution)/shard_map/ppermute | solution.py:412
  45.6 6.4 %all-to-all-done.parts = f32[32,56,128]{2,1,0:T(8,128)S(1)} async-done(((f32[32,56,128]{2,1,0:T(8,128)}), f32[32,56,128]{2,1,0:T(8,128)S(1)}, u32[]{:S(2)}, u32[]{:S(2)}) %all-to-all-start) | async-done | bytes 917536 | tf_op jit(solution)/shard_map/all_to_all | solution.py:416
  52.0 0.1 shard_map.82.own
  52.1 0.3 collective-permute-start.8
  52.4 3.8 %collective-permute-start.7 = (f32[64,128]{1,0:T(8,128)S(1)}, f32[64,128]{1,0:T(8,128)S(1)}, u32[]{:S(2)}, u32[]{:S(2)}) collective-permute-start(f32[64,128]{1,0:T(8,128)S(1)} %shard_map.82.own), channel_id=1, source_target_pairs={{0,136},{8,128},{128,8},{136,0},{1,137},{9,129},{129,9},{137,1},{2... | collective-permute-start | bytes 98312 | tf_op jit(solution)/shard_map/ppermute | solution.py:523
  56.2 1.6 %collective-permute-start.6 = (f32[64,128]{1,0:T(8,128)S(1)}, f32[64,128]{1,0:T(8,128)S(1)}, u32[]{:S(2)}, u32[]{:S(2)}) collective-permute-start(f32[64,128]{1,0:T(8,128)S(1)} %shard_map.82.own), channel_id=1, source_target_pairs={{0,8},{8,0},{128,136},{136,128},{1,9},{9,1},{129,137},{137,129},{2... | collective-permute-start | bytes 98312 | tf_op jit(solution)/shard_map/ppermute | solution.py:523
  57.9 1.1 %collective-permute-done.8.two = f32[64,128]{1,0:T(8,128)S(1)} collective-permute-done((f32[64,128]{1,0:T(8,128)S(1)}, f32[64,128]{1,0:T(8,128)S(1)}, u32[]{:S(2)}, u32[]{:S(2)}) %collective-permute-start.8) | collective-permute-done | bytes 32800 | tf_op jit(solution)/shard_map/ppermute | solution.py:523
  58.9 0.0 collective-permute-done.7.three
  58.9 1.3 %collective-permute-done.6.one = f32[64,128]{1,0:T(8,128)S(1)} collective-permute-done((f32[64,128]{1,0:T(8,128)S(1)}, f32[64,128]{1,0:T(8,128)S(1)}, u32[]{:S(2)}, u32[]{:S(2)}) %collective-permute-start.6) | collective-permute-done | bytes 32800 | tf_op jit(solution)/shard_map/ppermute | solution.py:523
  60.2 0.8 %shard_map.83 = (bf16[32,56,128]{2,1,0:T(8,128)(2,1)}, f32[8,128]{1,0:T(8,128)S(1)}) custom-call(f32[64,128]{1,0:T(8,128)S(1)} %shard_map.82.own, f32[64,128]{1,0:T(8,128)S(1)} %collective-permute-done.6.one, f32[64,128]{1,0:T(8,128)S(1)} %collective-permute-done.7.three, f32[64,128]{1,0:T(8,128)S(1)} %collective-permute-done.8.two), custom_call_target="tpu_custom_call" | custom-call | bytes 1048576 | tf_op jit(solution)/shard_map/pallas_call | solution.py:391
  61.1 5.4 %all-to-all-start.1 = ((bf16[32,56,128]{2,1,0:T(8,128)(2,1)}), bf16[32,56,128]{2,1,0:T(8,128)(2,1)S(1)}, u32[]{:S(2)}, u32[]{:S(2)}) async-start(bf16[32,56,128]{2,1,0:T(8,128)(2,1)} %get-tuple-element.56), calls=%async_computation.1 | async-start | bytes 917504 | tf_op jit(solution)/shard_map/all_to_all | solution.py:416
  66.5 6.5 %shard_map.84 = (bf16[4,512,128]{2,1,0:T(8,128)(2,1)}, bf16[4,512,128]{2,1,0:T(8,128)(2,1)}) custom-call(s32[2]{0:T(128)S(1)} %pad_add_fusion.flags, bf16[4,512,128]{2,1,0:T(8,128)(2,1)} %bitcast.16, bf16[4,512,128]{2,1,0:T(8,128)(2,1)} %bitcast.20, bf16[2,512,128]{2,1,0:T(8,128)(2,1)S(1)} %collective-permute-done.2.near, ...), custom_call_target="tpu_custom_call" | custom-call | flops 4000000000 | bytes 1048576 | tf_op jit(solution)/shard_map/pallas_call | solution.py:391
  73.0 2.3 %all-to-all-done.1 = bf16[32,56,128]{2,1,0:T(8,128)(2,1)S(1)} async-done(((bf16[32,56,128]{2,1,0:T(8,128)(2,1)}), bf16[32,56,128]{2,1,0:T(8,128)(2,1)S(1)}, u32[]{:S(2)}, u32[]{:S(2)}) %all-to-all-start.1) | async-done | bytes 458784 | tf_op jit(solution)/shard_map/all_to_all | solution.py:416
  75.3 3.7 %collective-permute-start.9 = (bf16[1792,128]{1,0:T(8,128)(2,1)S(1)}, bf16[1792,128]{1,0:T(8,128)(2,1)S(1)}, u32[]{:S(2)}, u32[]{:S(2)}) collective-permute-start(bf16[1792,128]{1,0:T(8,128)(2,1)S(1)} %bitcast.10), channel_id=1, source_target_pairs={{0,64},{64,0},{1,65},{65,1},{2,66},{66,2},{3,67},{67,3},{4,68},{68... | collective-permute-start | bytes 1376264 | tf_op jit(solution)/shard_map/ppermute | solution.py:412
  79.0 1.5 %shard_map.85.grad_in = f32[27,128,128]{2,1,0:T(8,128)} custom-call(s32[2]{0:T(128)S(1)} %pad_add_fusion.flags, bf16[1792,128]{1,0:T(8,128)(2,1)S(1)} %bitcast.11), custom_call_target="tpu_custom_call" | custom-call | flops 1000000000 | bytes 1048576 | tf_op jit(solution)/shard_map/pallas_call | solution.py:391
  80.5 0.0 collective-permute-done.9.half_grad
  80.5 1.5 %shard_map.86 = f32[27,128,128]{2,1,0:T(8,128)} custom-call(s32[2]{0:T(128)S(1)} %pad_add_fusion.flags, bf16[1792,128]{1,0:T(8,128)(2,1)S(1)} %collective-permute-done.9.half_grad, f32[27,128,128]{2,1,0:T(8,128)} %shard_map.85.grad_in), custom_call_target="tpu_custom_call", output_to_operand_aliasing={{}: (2, {})} | custom-call | bytes 1048576 | tf_op jit(solution)/shard_map/pallas_call | solution.py:391
  (4 shorter events, 0.0 us)
Async XLA Ops:
  2.7 12.6 %collective-permute-start = (f32[8,128]{1,0:T(8,128)S(1)}, f32[8,128]{1,0:T(8,128)S(1)}, u32[]{:S(2)}, u32[]{:S(2)}) collective-permute-start(f32[8,128]{1,0:T(8,128)S(1)} %get-tuple-element.38), channel_id=1, source_target_pairs={{0,128},{128,0},{1,129},{129,1},{2,130},{130,2},{3,131},{131,3},{4... | collective-permute-start | bytes 12296 | tf_op jit(solution)/shard_map/ppermute | solution.py:412
  10.5 12.0 %collective-permute-start.3 = (bf16[2,512,128]{2,1,0:T(8,128)(2,1)S(1)}, bf16[2,512,128]{2,1,0:T(8,128)(2,1)S(1)}, u32[]{:S(2)}, u32[]{:S(2)}) collective-permute-start(bf16[2,512,128]{2,1,0:T(8,128)(2,1)S(1)} %get-tuple-element.46), channel_id=1, source_target_pairs={{64,128},{128,64},{65,129},{129,65},{66,130},{130,66},{67,131},{13... | collective-permute-start | bytes 786440 | tf_op jit(solution)/shard_map/ppermute | solution.py:456
  15.3 1.3 %collective-permute-start.1 = (f32[8,128]{1,0:T(8,128)S(1)}, f32[8,128]{1,0:T(8,128)S(1)}, u32[]{:S(2)}, u32[]{:S(2)}) collective-permute-start(f32[8,128]{1,0:T(8,128)S(1)} %add.10), channel_id=1, source_target_pairs={{0,64},{64,0},{1,65},{65,1},{2,66},{66,2},{3,67},{67,3},{4,68},{68... | collective-permute-start | bytes 12296 | tf_op jit(solution)/shard_map/ppermute | solution.py:412
  15.4 7.2 %collective-permute-start.2 = (bf16[2,512,128]{2,1,0:T(8,128)(2,1)S(1)}, bf16[2,512,128]{2,1,0:T(8,128)(2,1)S(1)}, u32[]{:S(2)}, u32[]{:S(2)}) collective-permute-start(bf16[2,512,128]{2,1,0:T(8,128)(2,1)S(1)} %get-tuple-element.45), channel_id=1, source_target_pairs={{0,64},{64,0},{1,65},{65,1},{2,66},{66,2},{3,67},{67,3},{4,68},{68... | collective-permute-start | bytes 786440 | tf_op jit(solution)/shard_map/ppermute | solution.py:412
  24.0 2.6 %collective-permute-start.4 = (f32[1792,128]{1,0:T(8,128)S(1)}, f32[1792,128]{1,0:T(8,128)S(1)}, u32[]{:S(2)}, u32[]{:S(2)}) collective-permute-start(f32[1792,128]{1,0:T(8,128)S(1)} %get-tuple-element.52), channel_id=1, source_target_pairs={{0,64},{64,0},{1,65},{65,1},{2,66},{66,2},{3,67},{67,3},{4,68},{68... | collective-permute-start | bytes 2752520 | tf_op jit(solution)/shard_map/ppermute | solution.py:412
  27.6 24.5 %all-to-all-start = ((f32[32,56,128]{2,1,0:T(8,128)}), f32[32,56,128]{2,1,0:T(8,128)S(1)}, u32[]{:S(2)}, u32[]{:S(2)}) async-start(f32[32,56,128]{2,1,0:T(8,128)} %bitcast.12), calls=%async_computation | async-start | bytes 1835008 | tf_op jit(solution)/shard_map/all_to_all | solution.py:416
  44.3 1.3 %collective-permute-start.5 = (f32[8,128]{1,0:T(8,128)S(1)}, f32[8,128]{1,0:T(8,128)S(1)}, u32[]{:S(2)}, u32[]{:S(2)}) collective-permute-start(f32[8,128]{1,0:T(8,128)S(1)} %get-tuple-element.53), channel_id=1, source_target_pairs={{0,64},{64,0},{1,65},{65,1},{2,66},{66,2},{3,67},{67,3},{4,68},{68... | collective-permute-start | bytes 12296 | tf_op jit(solution)/shard_map/ppermute | solution.py:412
  52.1 6.8 %collective-permute-start.8 = (f32[64,128]{1,0:T(8,128)S(1)}, f32[64,128]{1,0:T(8,128)S(1)}, u32[]{:S(2)}, u32[]{:S(2)}) collective-permute-start(f32[64,128]{1,0:T(8,128)S(1)} %shard_map.82.own), channel_id=1, source_target_pairs={{0,128},{8,136},{128,0},{136,8},{1,129},{9,137},{129,1},{137,9},{2... | collective-permute-start | bytes 98312 | tf_op jit(solution)/shard_map/ppermute | solution.py:523
  52.4 6.5 %collective-permute-start.7 = (f32[64,128]{1,0:T(8,128)S(1)}, f32[64,128]{1,0:T(8,128)S(1)}, u32[]{:S(2)}, u32[]{:S(2)}) collective-permute-start(f32[64,128]{1,0:T(8,128)S(1)} %shard_map.82.own), channel_id=1, source_target_pairs={{0,136},{8,128},{128,8},{136,0},{1,137},{9,129},{129,9},{137,1},{2... | collective-permute-start | bytes 98312 | tf_op jit(solution)/shard_map/ppermute | solution.py:523
  56.2 4.0 %collective-permute-start.6 = (f32[64,128]{1,0:T(8,128)S(1)}, f32[64,128]{1,0:T(8,128)S(1)}, u32[]{:S(2)}, u32[]{:S(2)}) collective-permute-start(f32[64,128]{1,0:T(8,128)S(1)} %shard_map.82.own), channel_id=1, source_target_pairs={{0,8},{8,0},{128,136},{136,128},{1,9},{9,1},{129,137},{137,129},{2... | collective-permute-start | bytes 98312 | tf_op jit(solution)/shard_map/ppermute | solution.py:523
  61.1 14.3 %all-to-all-start.1 = ((bf16[32,56,128]{2,1,0:T(8,128)(2,1)}), bf16[32,56,128]{2,1,0:T(8,128)(2,1)S(1)}, u32[]{:S(2)}, u32[]{:S(2)}) async-start(bf16[32,56,128]{2,1,0:T(8,128)(2,1)} %get-tuple-element.56), calls=%async_computation.1 | async-start | bytes 917504 | tf_op jit(solution)/shard_map/all_to_all | solution.py:416
  75.3 5.2 %collective-permute-start.9 = (bf16[1792,128]{1,0:T(8,128)(2,1)S(1)}, bf16[1792,128]{1,0:T(8,128)(2,1)S(1)}, u32[]{:S(2)}, u32[]{:S(2)}) collective-permute-start(bf16[1792,128]{1,0:T(8,128)(2,1)S(1)} %bitcast.10), channel_id=1, source_target_pairs={{0,64},{64,0},{1,65},{65,1},{2,66},{66,2},{3,67},{67,3},{4,68},{68... | collective-permute-start | bytes 1376264 | tf_op jit(solution)/shard_map/ppermute | solution.py:412

commit v12 on v11

--- a/solution.py
+++ b/solution.py
@@ -71,17 +71,17 @@
     return started
 
 
-def start_kernel(flags, lat, cot, sums, near, far, lat_v, sem, halo_sem):
+def start_kernel(flags, lat, cot, sums, far, lat_v, sem, halo_sem):
     parts = copies(sem, *((lat.at[t], lat_v.at[t]) for t in range(T)))
     tail, head = lat.at[T - HALO :], cot.at[:HALO]
 
     @pl.when(flags[1] == 0)
     def _():
-        copies(halo_sem, (tail, near), (head, far))
+        copies(halo_sem, (head, far))
 
     @pl.when(flags[1] != 0)
     def _():
-        copies(halo_sem, (head, near), (tail, far))
+        copies(halo_sem, (tail, far))
 
     total = jnp.zeros((ROWS, W), F32)
     square = jnp.zeros((ROWS, W), F32)
@@ -94,8 +94,7 @@
     square = jnp.sum(jnp.sum(square.reshape(GROUPS, -1, W), axis=1), axis=1, keepdims=True)
     row = row_of(total, 0) + row_of(square, GROUPS)
     sums[...] = jnp.broadcast_to(row, (8, W))
-    pltpu.make_async_copy(tail, near, halo_sem.at[0]).wait()
-    pltpu.make_async_copy(head, far, halo_sem.at[1]).wait()
+    pltpu.make_async_copy(head, far, halo_sem.at[0]).wait()
 
 
 def put_adjoint(adj, f, mine):
@@ -107,7 +106,19 @@
             adj[ki * C : (ki + 1) * C, (f * H + h) * W : (f * H + h + 1) * W] = block
 
 
-def prepare_kernel(lat, cot, gain, shift, adj, scales, lat_v, cot_v, gain_v, shift_v, tmp, sem):
+def prepare_kernel(
+    flags, lat, cot, gain, shift, adj, scales, near, lat_v, cot_v, gain_v, shift_v, tmp, sem, halo_sem
+):
+    tail, head = lat.at[T - HALO :], cot.at[:HALO]
+
+    @pl.when(flags[1] == 0)
+    def _():
+        copies(halo_sem, (tail, near))
+
+    @pl.when(flags[1] != 0)
+    def _():
+        copies(halo_sem, (head, near))
+
     from_lat, from_cot, *small = copies(sem, (lat, lat_v), (cot, cot_v), (gain, gain_v), (shift, shift_v))
     from_lat.wait()
     for t in range(T):
@@ -120,6 +131,7 @@
         copy.wait()
     scales[0] = jnp.broadcast_to(channel_column(gain_v[...]), (C, W))
     scales[1] = jnp.broadcast_to(channel_column(shift_v[...]), (C, W))
+    pltpu.make_async_copy(tail, near, halo_sem.at[0]).wait()
 
 
 def clear(taps):
@@ -282,11 +294,11 @@
     core = flags[1] if first else 1 - flags[1]
     at = pl.multiple_of(core * half, half)
     started = []
-    for kt in range(3):
-        rows_of = half_grad[9 * kt * half : 9 * (kt + 1) * half].astype(F32)
-        grad_v[9 * kt : 9 * (kt + 1)] = rows_of.reshape(9, half, C)
-        taps = pl.ds(9 * kt, 9)
-        started += copies(sem.at[pl.ds(kt, 1)], (grad_v.at[taps], grad.at[taps, pl.ds(at, half)]))
+    for i in range(9):
+        rows_of = half_grad[3 * i * half : 3 * (i + 1) * half].astype(F32)
+        grad_v[3 * i : 3 * (i + 1)] = rows_of.reshape(3, half, C)
+        taps = pl.ds(3 * i, 3)
+        started += copies(sem.at[pl.ds(i, 1)], (grad_v.at[taps], grad.at[taps, pl.ds(at, half)]))
     for copy in started:
         copy.wait()
 
@@ -430,10 +442,10 @@
     taps = pltpu.VMEM((3, ROWS, 3 * ROWS), BF16)
     kernel_scratch = pltpu.VMEM((27, C, C), BF16)
     scaled_scratch = pltpu.VMEM((T, ROWS, W), F32)
-    own, to_near, to_far = call(
+    own, to_far = call(
         start_kernel,
-        (shape(8, W), halo, halo),
-        [frames, sems(T), sems(2)],
+        (shape(8, W), halo),
+        [frames, sems(T), sems(1)],
         flags,
         lat,
         cot,
@@ -441,15 +453,17 @@
         scalars=1,
     )
     gain, to_far = lax.optimization_barrier((gain, to_far))
-    adj, scales = call(
+    adj, scales, to_near = call(
         prepare_kernel,
-        (shape(4 * C, T * PLANE, dtype=BF16), shape(2, C, W)),
-        [frames, frames, row, row, tmp, sems(4)],
+        (shape(4 * C, T * PLANE, dtype=BF16), shape(2, C, W), halo),
+        [frames, frames, row, row, tmp, sems(4), sems(1)],
+        flags,
         lat,
         cot,
         gain,
         shift,
-        far=(0, 1, 2, 3),
+        far=(1, 2, 3, 4),
+        scalars=1,
         flops=0,
     )
     slab = ("zh", "core")
@@ -556,7 +570,7 @@
         (exchange(part, ("y", "zn", "x")).reshape(COMM, C), output, result)
     )
     other = swap(mine, "core")
-    half_scratch = [pltpu.VMEM((27, C // 2, C), F32), sems(3)]
+    half_scratch = [pltpu.VMEM((27, C // 2, C), F32), sems(9)]
     kernel_grad = call(
         place_first, shape(27, C, C), half_scratch, flags, mine, out_far=(0,), scalars=1, flops=10**9
     )

time: 82.5 us -> 82.4 us (level)
  transfers between devices with their start and end apart: 12 -> 12, of which waited for: 8 -> 8; matrix products, arithmetic and copies ran while one was open for 0% -> 0% of each run, Pallas kernels for 24% -> 25%
where the time goes in v12:
time: 82.4 us; the launch traced here: 82 us
  starting transfers between devices  36.5 us (44%)
  Pallas kernels  27.1 us (33%)
  waiting for transfers between devices  17.5 us (21%)
  between operations  0.95 us (1%)
    pallas_call x11, Pallas kernels, call(): pl.pallas_call(body, out_shape=shapes[0] if single else shapes, in_specs=...  27.1 us
    all_to_all x2, starting transfers between devices, exchange(): return lax.all_to_all(parts, axes, 0, 0)  15.7 us
    ppermute x6, starting transfers between devices, swap(): return lax.ppermute(value, axis, [(0, 1), (1, 0)])  12.1 us
    all_to_all x2, waiting for transfers between devices, exchange(): return lax.all_to_all(parts, axes, 0, 0)  8.81 us
    ppermute x3, starting transfers between devices, per_device(): lax.ppermute(packed, ('zh', 'zm'), [(i, i ^ flip) for i in range(4)])  5.74 us
    ppermute x6, waiting for transfers between devices, swap(): return lax.ppermute(value, axis, [(0, 1), (1, 0)])  3.94 us
    ppermute x1, starting transfers between devices, per_device(): before = lax.ppermute(to_far, slab, [(1, 2), (2, 1)])  2.94 us
    ppermute x3, waiting for transfers between devices, per_device(): lax.ppermute(packed, ('zh', 'zm'), [(i, i ^ flip) for i in range(4)])  2.45 us
  transfers between devices with their start and end apart: 12, of which 8 were waited for; matrix products, arithmetic and copies ran while one was open for 0% of the time, Pallas kernels for 25%

profile of v12, /device:TPU:1, one launch (start us, length us, event | category | flops | bytes accessed | tf_op | source)
XLA Modules:
  0.0 82.0 jit_solution(9552859556823991593)
XLA Ops:
  0.6 0.1 pad_add_fusion.flags
  0.7 1.9 %shard_map.76 = (f32[8,128]{1,0:T(8,128)S(1)}, bf16[2,512,128]{2,1,0:T(8,128)(2,1)S(1)}) custom-call(s32[2]{0:T(128)S(1)} %pad_add_fusion.flags, bf16[4,512,128]{2,1,0:T(8,128)(2,1)} %bitcast.13, bf16[4,512,128]{2,1,0:T(8,128)(2,1)} %bitcast.17), custom_call_target="tpu_custom_call" | custom-call | bytes 1048576 | tf_op jit(solution)/shard_map/pallas_call | solution.py:403
  2.6 7.8 %collective-permute-start = (f32[8,128]{1,0:T(8,128)S(1)}, f32[8,128]{1,0:T(8,128)S(1)}, u32[]{:S(2)}, u32[]{:S(2)}) collective-permute-start(f32[8,128]{1,0:T(8,128)S(1)} %get-tuple-element.38), channel_id=1, source_target_pairs={{0,128},{128,0},{1,129},{129,1},{2,130},{130,2},{3,131},{131,3},{4... | collective-permute-start | bytes 12296 | tf_op jit(solution)/shard_map/ppermute | solution.py:424
  10.4 2.9 %collective-permute-start.3 = (bf16[2,512,128]{2,1,0:T(8,128)(2,1)S(1)}, bf16[2,512,128]{2,1,0:T(8,128)(2,1)S(1)}, u32[]{:S(2)}, u32[]{:S(2)}) collective-permute-start(bf16[2,512,128]{2,1,0:T(8,128)(2,1)S(1)} %get-tuple-element.46), channel_id=1, source_target_pairs={{64,128},{128,64},{65,129},{129,65},{66,130},{130,66},{67,131},{13... | collective-permute-start | bytes 786440 | tf_op jit(solution)/shard_map/ppermute | solution.py:470
  13.4 2.3 %shard_map.77 = (bf16[512,2048]{1,0:T(8,128)(2,1)S(1)}, f32[2,128,128]{2,1,0:T(8,128)S(1)}, bf16[2,512,128]{2,1,0:T(8,128)(2,1)S(1)}) custom-call(s32[2]{0:T(128)S(1)} %pad_add_fusion.flags, bf16[4,512,128]{2,1,0:T(8,128)(2,1)} %bitcast.14, bf16[4,512,128]{2,1,0:T(8,128)(2,1)} %bitcast.18, f32[1,128]{1,0:T(1,128)} %bitcast.21, f32[1,128]{1,0:T(1,128)} %bitcast.22), custom_call_target="tpu_custom_call" | custom-call | bytes 1048576 | tf_op jit(solution)/shard_map/pallas_call | solution.py:403
  15.6 0.0 collective-permute-done
  15.7 0.1 collective-permute-start.1
  15.8 0.5 collective-permute-start.2
  16.3 0.7 collective-permute-done.1
  16.9 3.2 %shard_map.78 = (bf16[1536,512]{1,0:T(8,128)(2,1)}, f32[1792,128]{1,0:T(8,128)S(1)}, f32[1792,128]{1,0:T(8,128)S(1)}, bf16[384,1024]{1,0:T(8,128)(2,1)S(1)}) custom-call(s32[2]{0:T(128)S(1)} %pad_add_fusion.flags, bf16[512,2048]{1,0:T(8,128)(2,1)S(1)} %get-tuple-element.36.adj, f32[16,128]{1,0:T(8,128)S(1)} %constant_dynamic-update-slice_fusion.totals, ...), custom_call_target="tpu_custom_call" | custom-call | flops 2000000000 | bytes 1048576 | tf_op jit(solution)/shard_map/pallas_call | solution.py:403
  20.1 2.3 %collective-permute-done.3.far = bf16[2,512,128]{2,1,0:T(8,128)(2,1)S(1)} collective-permute-done((bf16[2,512,128]{2,1,0:T(8,128)(2,1)S(1)}, bf16[2,512,128]{2,1,0:T(8,128)(2,1)S(1)}, u32[]{:S(2)}, u32[]{:S(2)}) %collective-permute-start.3) | collective-permute-done | bytes 262176 | tf_op jit(solution)/shard_map/ppermute | solution.py:470
  22.4 0.0 collective-permute-done.2.near
  22.4 1.4 %shard_map.79 = (f32[1792,128]{1,0:T(8,128)S(1)}, f32[1792,128]{1,0:T(8,128)S(1)}) custom-call(s32[2]{0:T(128)S(1)} %pad_add_fusion.flags, f32[1792,128]{1,0:T(8,128)S(1)} %get-tuple-element.43.keep_in, f32[1792,128]{1,0:T(8,128)S(1)} %get-tuple-element.44.send_in, ...), custom_call_target="tpu_custom_call", output_to_operand_aliasing={{0}: (1, {}), {1}: (2, {})} | custom-call | bytes 1048576 | tf_op jit(solution)/shard_map/pallas_call | solution.py:403
  23.8 0.1 collective-permute-start.4
  23.9 2.5 %collective-permute-done.4.received = f32[1792,128]{1,0:T(8,128)S(1)} collective-permute-done((f32[1792,128]{1,0:T(8,128)S(1)}, f32[1792,128]{1,0:T(8,128)S(1)}, u32[]{:S(2)}, u32[]{:S(2)}) %collective-permute-start.4) | collective-permute-done | bytes 917536 | tf_op jit(solution)/shard_map/ppermute | solution.py:424
  26.4 1.0 %shard_map.80 = f32[1792,128]{1,0:T(8,128)} custom-call(f32[1792,128]{1,0:T(8,128)S(1)} %get-tuple-element.51.keep, f32[1792,128]{1,0:T(8,128)S(1)} %collective-permute-done.4.received), custom_call_target="tpu_custom_call" | custom-call | bytes 1048576 | tf_op jit(solution)/shard_map/pallas_call | solution.py:403
  27.4 9.9 %all-to-all-start = ((f32[32,56,128]{2,1,0:T(8,128)}), f32[32,56,128]{2,1,0:T(8,128)S(1)}, u32[]{:S(2)}, u32[]{:S(2)}) async-start(f32[32,56,128]{2,1,0:T(8,128)} %bitcast.12), calls=%async_computation | async-start | bytes 1835008 | tf_op jit(solution)/shard_map/all_to_all | solution.py:428
  37.3 6.8 %shard_map.81 = (f32[4,512,128]{2,1,0:T(8,128)}, f32[8,128]{1,0:T(8,128)S(1)}) custom-call(s32[2]{0:T(128)S(1)} %pad_add_fusion.flags, bf16[4,512,128]{2,1,0:T(8,128)(2,1)} %bitcast.15, bf16[4,512,128]{2,1,0:T(8,128)(2,1)} %bitcast.19, bf16[2,512,128]{2,1,0:T(8,128)(2,1)S(1)} %collective-permute-done.2.near, ...), custom_call_target="tpu_custom_call" | custom-call | flops 4000000000 | bytes 1048576 | tf_op jit(solution)/shard_map/pallas_call | solution.py:403
  44.2 0.5 collective-permute-start.5
  44.7 0.8 %collective-permute-done.5 = f32[8,128]{1,0:T(8,128)S(1)} collective-permute-done((f32[8,128]{1,0:T(8,128)S(1)}, f32[8,128]{1,0:T(8,128)S(1)}, u32[]{:S(2)}, u32[]{:S(2)}) %collective-permute-start.5) | collective-permute-done | bytes 4128 | tf_op jit(solution)/shard_map/ppermute | solution.py:424
  45.5 6.4 %all-to-all-done.parts = f32[32,56,128]{2,1,0:T(8,128)S(1)} async-done(((f32[32,56,128]{2,1,0:T(8,128)}), f32[32,56,128]{2,1,0:T(8,128)S(1)}, u32[]{:S(2)}, u32[]{:S(2)}) %all-to-all-start) | async-done | bytes 917536 | tf_op jit(solution)/shard_map/all_to_all | solution.py:428
  52.0 0.1 shard_map.82.own
  52.0 0.2 collective-permute-start.8
  52.2 3.8 %collective-permute-start.7 = (f32[64,128]{1,0:T(8,128)S(1)}, f32[64,128]{1,0:T(8,128)S(1)}, u32[]{:S(2)}, u32[]{:S(2)}) collective-permute-start(f32[64,128]{1,0:T(8,128)S(1)} %shard_map.82.own), channel_id=1, source_target_pairs={{0,136},{8,128},{128,8},{136,0},{1,137},{9,129},{129,9},{137,1},{2... | collective-permute-start | bytes 98312 | tf_op jit(solution)/shard_map/ppermute | solution.py:537
  56.1 1.7 %collective-permute-start.6 = (f32[64,128]{1,0:T(8,128)S(1)}, f32[64,128]{1,0:T(8,128)S(1)}, u32[]{:S(2)}, u32[]{:S(2)}) collective-permute-start(f32[64,128]{1,0:T(8,128)S(1)} %shard_map.82.own), channel_id=1, source_target_pairs={{0,8},{8,0},{128,136},{136,128},{1,9},{9,1},{129,137},{137,129},{2... | collective-permute-start | bytes 98312 | tf_op jit(solution)/shard_map/ppermute | solution.py:537
  57.8 1.0 %collective-permute-done.8.two = f32[64,128]{1,0:T(8,128)S(1)} collective-permute-done((f32[64,128]{1,0:T(8,128)S(1)}, f32[64,128]{1,0:T(8,128)S(1)}, u32[]{:S(2)}, u32[]{:S(2)}) %collective-permute-start.8) | collective-permute-done | bytes 32800 | tf_op jit(solution)/shard_map/ppermute | solution.py:537
  58.8 0.0 collective-permute-done.7.three
  58.8 1.4 %collective-permute-done.6.one = f32[64,128]{1,0:T(8,128)S(1)} collective-permute-done((f32[64,128]{1,0:T(8,128)S(1)}, f32[64,128]{1,0:T(8,128)S(1)}, u32[]{:S(2)}, u32[]{:S(2)}) %collective-permute-start.6) | collective-permute-done | bytes 32800 | tf_op jit(solution)/shard_map/ppermute | solution.py:537
  60.2 0.8 %shard_map.83 = (bf16[32,56,128]{2,1,0:T(8,128)(2,1)}, f32[8,128]{1,0:T(8,128)S(1)}) custom-call(f32[64,128]{1,0:T(8,128)S(1)} %shard_map.82.own, f32[64,128]{1,0:T(8,128)S(1)} %collective-permute-done.6.one, f32[64,128]{1,0:T(8,128)S(1)} %collective-permute-done.7.three, f32[64,128]{1,0:T(8,128)S(1)} %collective-permute-done.8.two), custom_call_target="tpu_custom_call" | custom-call | bytes 1048576 | tf_op jit(solution)/shard_map/pallas_call | solution.py:403
  61.1 5.8 %all-to-all-start.1 = ((bf16[32,56,128]{2,1,0:T(8,128)(2,1)}), bf16[32,56,128]{2,1,0:T(8,128)(2,1)S(1)}, u32[]{:S(2)}, u32[]{:S(2)}) async-start(bf16[32,56,128]{2,1,0:T(8,128)(2,1)} %get-tuple-element.56), calls=%async_computation.1 | async-start | bytes 917504 | tf_op jit(solution)/shard_map/all_to_all | solution.py:428
  66.8 6.5 %shard_map.84 = (bf16[4,512,128]{2,1,0:T(8,128)(2,1)}, bf16[4,512,128]{2,1,0:T(8,128)(2,1)}) custom-call(s32[2]{0:T(128)S(1)} %pad_add_fusion.flags, bf16[4,512,128]{2,1,0:T(8,128)(2,1)} %bitcast.16, bf16[4,512,128]{2,1,0:T(8,128)(2,1)} %bitcast.20, bf16[2,512,128]{2,1,0:T(8,128)(2,1)S(1)} %collective-permute-done.2.near, ...), custom_call_target="tpu_custom_call" | custom-call | flops 4000000000 | bytes 1048576 | tf_op jit(solution)/shard_map/pallas_call | solution.py:403
  73.4 2.4 %all-to-all-done.1 = bf16[32,56,128]{2,1,0:T(8,128)(2,1)S(1)} async-done(((bf16[32,56,128]{2,1,0:T(8,128)(2,1)}), bf16[32,56,128]{2,1,0:T(8,128)(2,1)S(1)}, u32[]{:S(2)}, u32[]{:S(2)}) %all-to-all-start.1) | async-done | bytes 458784 | tf_op jit(solution)/shard_map/all_to_all | solution.py:428
  75.7 3.1 %collective-permute-start.9 = (bf16[1792,128]{1,0:T(8,128)(2,1)S(1)}, bf16[1792,128]{1,0:T(8,128)(2,1)S(1)}, u32[]{:S(2)}, u32[]{:S(2)}) collective-permute-start(bf16[1792,128]{1,0:T(8,128)(2,1)S(1)} %bitcast.10), channel_id=1, source_target_pairs={{0,64},{64,0},{1,65},{65,1},{2,66},{66,2},{3,67},{67,3},{4,68},{68... | collective-permute-start | bytes 1376264 | tf_op jit(solution)/shard_map/ppermute | solution.py:424
  78.8 1.5 %shard_map.85.grad_in = f32[27,128,128]{2,1,0:T(8,128)} custom-call(s32[2]{0:T(128)S(1)} %pad_add_fusion.flags, bf16[1792,128]{1,0:T(8,128)(2,1)S(1)} %bitcast.11), custom_call_target="tpu_custom_call" | custom-call | flops 1000000000 | bytes 1048576 | tf_op jit(solution)/shard_map/pallas_call | solution.py:403
  80.3 0.0 collective-permute-done.9.half_grad
  80.4 1.5 %shard_map.86 = f32[27,128,128]{2,1,0:T(8,128)} custom-call(s32[2]{0:T(128)S(1)} %pad_add_fusion.flags, bf16[1792,128]{1,0:T(8,128)(2,1)S(1)} %collective-permute-done.9.half_grad, f32[27,128,128]{2,1,0:T(8,128)} %shard_map.85.grad_in), custom_call_target="tpu_custom_call", output_to_operand_aliasing={{}: (2, {})} | custom-call | bytes 1048576 | tf_op jit(solution)/shard_map/pallas_call | solution.py:403
  (4 shorter events, 0.0 us)
Async XLA Ops:
  2.6 13.1 %collective-permute-start = (f32[8,128]{1,0:T(8,128)S(1)}, f32[8,128]{1,0:T(8,128)S(1)}, u32[]{:S(2)}, u32[]{:S(2)}) collective-permute-start(f32[8,128]{1,0:T(8,128)S(1)} %get-tuple-element.38), channel_id=1, source_target_pairs={{0,128},{128,0},{1,129},{129,1},{2,130},{130,2},{3,131},{131,3},{4... | collective-permute-start | bytes 12296 | tf_op jit(solution)/shard_map/ppermute | solution.py:424
  10.4 12.0 %collective-permute-start.3 = (bf16[2,512,128]{2,1,0:T(8,128)(2,1)S(1)}, bf16[2,512,128]{2,1,0:T(8,128)(2,1)S(1)}, u32[]{:S(2)}, u32[]{:S(2)}) collective-permute-start(bf16[2,512,128]{2,1,0:T(8,128)(2,1)S(1)} %get-tuple-element.46), channel_id=1, source_target_pairs={{64,128},{128,64},{65,129},{129,65},{66,130},{130,66},{67,131},{13... | collective-permute-start | bytes 786440 | tf_op jit(solution)/shard_map/ppermute | solution.py:470
  15.7 1.3 %collective-permute-start.1 = (f32[8,128]{1,0:T(8,128)S(1)}, f32[8,128]{1,0:T(8,128)S(1)}, u32[]{:S(2)}, u32[]{:S(2)}) collective-permute-start(f32[8,128]{1,0:T(8,128)S(1)} %add.10), channel_id=1, source_target_pairs={{0,64},{64,0},{1,65},{65,1},{2,66},{66,2},{3,67},{67,3},{4,68},{68... | collective-permute-start | bytes 12296 | tf_op jit(solution)/shard_map/ppermute | solution.py:424
  15.8 6.6 %collective-permute-start.2 = (bf16[2,512,128]{2,1,0:T(8,128)(2,1)S(1)}, bf16[2,512,128]{2,1,0:T(8,128)(2,1)S(1)}, u32[]{:S(2)}, u32[]{:S(2)}) collective-permute-start(bf16[2,512,128]{2,1,0:T(8,128)(2,1)S(1)} %get-tuple-element.45), channel_id=1, source_target_pairs={{0,64},{64,0},{1,65},{65,1},{2,66},{66,2},{3,67},{67,3},{4,68},{68... | collective-permute-start | bytes 786440 | tf_op jit(solution)/shard_map/ppermute | solution.py:424
  23.8 2.6 %collective-permute-start.4 = (f32[1792,128]{1,0:T(8,128)S(1)}, f32[1792,128]{1,0:T(8,128)S(1)}, u32[]{:S(2)}, u32[]{:S(2)}) collective-permute-start(f32[1792,128]{1,0:T(8,128)S(1)} %get-tuple-element.52), channel_id=1, source_target_pairs={{0,64},{64,0},{1,65},{65,1},{2,66},{66,2},{3,67},{67,3},{4,68},{68... | collective-permute-start | bytes 2752520 | tf_op jit(solution)/shard_map/ppermute | solution.py:424
  27.4 24.6 %all-to-all-start = ((f32[32,56,128]{2,1,0:T(8,128)}), f32[32,56,128]{2,1,0:T(8,128)S(1)}, u32[]{:S(2)}, u32[]{:S(2)}) async-start(f32[32,56,128]{2,1,0:T(8,128)} %bitcast.12), calls=%async_computation | async-start | bytes 1835008 | tf_op jit(solution)/shard_map/all_to_all | solution.py:428
  44.2 1.3 %collective-permute-start.5 = (f32[8,128]{1,0:T(8,128)S(1)}, f32[8,128]{1,0:T(8,128)S(1)}, u32[]{:S(2)}, u32[]{:S(2)}) collective-permute-start(f32[8,128]{1,0:T(8,128)S(1)} %get-tuple-element.53), channel_id=1, source_target_pairs={{0,64},{64,0},{1,65},{65,1},{2,66},{66,2},{3,67},{67,3},{4,68},{68... | collective-permute-start | bytes 12296 | tf_op jit(solution)/shard_map/ppermute | solution.py:424
  52.0 6.8 %collective-permute-start.8 = (f32[64,128]{1,0:T(8,128)S(1)}, f32[64,128]{1,0:T(8,128)S(1)}, u32[]{:S(2)}, u32[]{:S(2)}) collective-permute-start(f32[64,128]{1,0:T(8,128)S(1)} %shard_map.82.own), channel_id=1, source_target_pairs={{0,128},{8,136},{128,0},{136,8},{1,129},{9,137},{129,1},{137,9},{2... | collective-permute-start | bytes 98312 | tf_op jit(solution)/shard_map/ppermute | solution.py:537
  52.2 6.6 %collective-permute-start.7 = (f32[64,128]{1,0:T(8,128)S(1)}, f32[64,128]{1,0:T(8,128)S(1)}, u32[]{:S(2)}, u32[]{:S(2)}) collective-permute-start(f32[64,128]{1,0:T(8,128)S(1)} %shard_map.82.own), channel_id=1, source_target_pairs={{0,136},{8,128},{128,8},{136,0},{1,137},{9,129},{129,9},{137,1},{2... | collective-permute-start | bytes 98312 | tf_op jit(solution)/shard_map/ppermute | solution.py:537
  56.1 4.2 %collective-permute-start.6 = (f32[64,128]{1,0:T(8,128)S(1)}, f32[64,128]{1,0:T(8,128)S(1)}, u32[]{:S(2)}, u32[]{:S(2)}) collective-permute-start(f32[64,128]{1,0:T(8,128)S(1)} %shard_map.82.own), channel_id=1, source_target_pairs={{0,8},{8,0},{128,136},{136,128},{1,9},{9,1},{129,137},{137,129},{2... | collective-permute-start | bytes 98312 | tf_op jit(solution)/shard_map/ppermute | solution.py:537
  61.1 14.7 %all-to-all-start.1 = ((bf16[32,56,128]{2,1,0:T(8,128)(2,1)}), bf16[32,56,128]{2,1,0:T(8,128)(2,1)S(1)}, u32[]{:S(2)}, u32[]{:S(2)}) async-start(bf16[32,56,128]{2,1,0:T(8,128)(2,1)} %get-tuple-element.56), calls=%async_computation.1 | async-start | bytes 917504 | tf_op jit(solution)/shard_map/all_to_all | solution.py:428
  75.7 4.6 %collective-permute-start.9 = (bf16[1792,128]{1,0:T(8,128)(2,1)S(1)}, bf16[1792,128]{1,0:T(8,128)(2,1)S(1)}, u32[]{:S(2)}, u32[]{:S(2)}) collective-permute-start(bf16[1792,128]{1,0:T(8,128)(2,1)S(1)} %bitcast.10), channel_id=1, source_target_pairs={{0,64},{64,0},{1,65},{65,1},{2,66},{66,2},{3,67},{67,3},{4,68},{68... | collective-permute-start | bytes 1376264 | tf_op jit(solution)/shard_map/ppermute | solution.py:424
